TPU v7x, 32 devices: a whole 2x2x4 slice. The times are simulated.
32 devices in a mesh: atm: 8 (over y, x, core), ocn: 4 (over z).
Axes of the slice: x: 2, y: 2, z: 4, core: 2. Of those that a mesh axis runs over, the one named last changes fastest.
Arguments:
- atm_state: float32 [6912, 3, 512], P('atm', None, 'ocn'), may hold values from -6 to 6
- diffusivity: float32 [6912, 3, 512], P('atm', None, 'ocn'), may hold values from 0.1 to 0.24
- ocean_state: float32 [8192, 3, 128], P(('atm', 'ocn')), may hold values from -6 to 6
- land_mask: int32 [8192, 128], P(('atm', 'ocn')), may hold values 0 or 1
- intersection_area: float32 [16384, 128], P(('atm', 'ocn')), may hold values from 0.2 to 1
- intersection_seg: int32 [16384], P(('atm', 'ocn')), may hold values from 0 to 255
- intersection_dest: int32 [16384, 1], P(('atm', 'ocn')), may hold values from 0 to 31; in each aligned block of 512 rows (0 to 511, 512 to 1023, ...) at most 32 rows name the same one
- intersection_row: int32 [16384], P(('atm', 'ocn')), may hold values from 0 to 863
Outputs:
- atm_next: float32 [6912, 3, 512], P('atm', None, 'ocn')
- ocean_flux: float32 [8192, 3, 128], P(('atm', 'ocn'))
Inputs may be any that keep to these rules, and one draw needn't show every extreme that they name: intersection_seg indexes the segments owned by the same device as the intersection row. `intersection_dest`: among the 512 intersection rows of one device, no device is named by more than 32 rows, and some device is named by exactly 32.
All inputs are finite; a program needn't handle non-finite values. No bound on the sum of `land_mask` on one device may be relied on, other than what follows from the above.
Results may differ from a plain program's by a relative error of at most 0.00002.
Values sent between devices are 32-bit elements; how exact they have to be, the bound alone decides.
No kernel may reach another device: no remote copies, remote signals or barrier semaphores. Data moves between devices by JAX's collectives and lax.ppermute only.
A program may use at most 64 MiB of HBM per device.

v0:
```python
import jax
import jax.numpy as jnp
from jax import lax
from jax.sharding import PartitionSpec as P

ITERS = 3


def with_halo(block, sides, width):
    for axis, dim in sides:
        count = lax.axis_size(axis)
        forward = [(i, i + 1) for i in range(count - 1)]
        backward = [(target, source) for source, target in forward]
        low = lax.ppermute(
            lax.slice_in_dim(block, block.shape[dim] - width, None, axis=dim), axis, forward
        )
        high = lax.ppermute(lax.slice_in_dim(block, 0, width, axis=dim), axis, backward)
        block = jnp.concatenate([low, block, high], axis=dim)
    return block


def beside_all(padded):
    return padded[2:, :, 1:-1] + padded[:-2, :, 1:-1] + padded[1:-1, :, 2:] + padded[1:-1, :, :-2]


def fluxes(ocean_part, air_part):
    wind_east = air_part[:, 1] - ocean_part[:, 1]
    wind_north = air_part[:, 2] - ocean_part[:, 2]
    wind_speed = jnp.sqrt(wind_east * wind_east + wind_north * wind_north + 0.5)
    temp_gap = ocean_part[:, 0] - air_part[:, 0]
    factor = 1.0 + 0.5 * jnp.tanh(temp_gap / wind_speed)
    return jnp.stack(
        [
            0.8 * factor * wind_speed * temp_gap,
            0.6 * factor * wind_speed * wind_east,
            0.6 * factor * wind_speed * wind_north,
        ],
        axis=1,
    )


def per_device(
    atm_state,
    diffusivity,
    ocean_state,
    land_mask,
    intersection_area,
    intersection_seg,
    intersection_dest,
    intersection_row,
):
    atm_count = lax.axis_size("atm")
    ocn_count = lax.axis_size("ocn")
    devices = atm_count * ocn_count
    row_count, chan_count, seg_width = atm_state.shape
    ov_rows = intersection_seg.shape[0]
    capacity = max(2, 2 * ov_rows // devices)
    padded = with_halo(atm_state, (("atm", 0), ("ocn", 2)), 1)
    smoothed = 0.5 * atm_state + 0.125 * beside_all(padded)
    target = intersection_dest[:, 0]
    matches = (target[:, None] == jnp.arange(devices, dtype=jnp.int32)[None, :]).astype(jnp.int32)
    position = jnp.sum((jnp.cumsum(matches, axis=0) - matches) * matches, axis=1)
    slot_index = target * capacity + position
    seg_rows = jnp.take(ocean_state, intersection_seg, axis=0)
    weight = intersection_area * jnp.take(land_mask, intersection_seg, axis=0).astype(jnp.float32)
    payload = jnp.concatenate([seg_rows, weight[:, None, :]], axis=1)
    outgoing = (
        jnp.zeros((devices * capacity, chan_count + 1, seg_width), jnp.float32)
        .at[slot_index]
        .set(payload)
    )
    out_labels = jnp.zeros((devices * capacity,), jnp.int32).at[slot_index].set(intersection_row)
    incoming = lax.all_to_all(outgoing, ("atm", "ocn"), split_axis=0, concat_axis=0, tiled=True)
    in_labels = lax.all_to_all(out_labels, ("atm", "ocn"), split_axis=0, concat_axis=0, tiled=True)
    air_rows = jnp.take(smoothed, in_labels, axis=0)
    weighted = incoming[:, chan_count : chan_count + 1, :] * fluxes(
        incoming[:, :chan_count, :], air_rows
    )
    air_sum = jax.ops.segment_sum(weighted, in_labels, num_segments=row_count)
    returned = lax.all_to_all(weighted, ("atm", "ocn"), split_axis=0, concat_axis=0, tiled=True)
    own_rows = jnp.take(returned, slot_index, axis=0)
    ocean_flux = jax.ops.segment_sum(own_rows, intersection_seg, num_segments=ocean_state.shape[0])
    direction_sign = jnp.array([1.0, -1.0, -1.0], dtype=jnp.float32)[None, :, None]
    current = atm_state + direction_sign * air_sum
    for iteration in range(ITERS):
        bordered = with_halo(current, (("atm", 0), ("ocn", 2)), 1)
        current = current + diffusivity * (beside_all(bordered) - 4.0 * current)
    return (current, ocean_flux)


def solution(mesh):
    placed = (
        P("atm", None, "ocn"),
        P("atm", None, "ocn"),
        P(("atm", "ocn"), None, None),
        P(("atm", "ocn"), None),
        P(("atm", "ocn"), None),
        P(("atm", "ocn")),
        P(("atm", "ocn"), None),
        P(("atm", "ocn")),
    )
    return jax.shard_map(
        per_device,
        mesh=mesh,
        in_specs=placed,
        out_specs=(P("atm", None, "ocn"), P(("atm", "ocn"), None, None)),
        check_vma=False,
    )
```

profile of v0, /device:TPU:1, one launch (start us, length us, event | category | flops | bytes accessed | tf_op | source)
XLA Modules:
  0.0 367.7 jit_solution(16777153145507847011)
XLA Ops:
  8.2 7.1 %all-to-all-start = ((s32[32,32,1]{1,2,0:T(1,128)}), s32[32,32,1]{1,2,0:T(1,128)S(1)}, u32[]{:S(2)}, u32[]{:S(2)}) async-start(s32[32,32,1]{1,2,0:T(1,128)} %bitcast.5), calls=%async_computation | async-start | bytes 32768 | tf_op jit(solution)/shard_map/all_to_all | solution.py:74
  22.7 47.5 %scatter_fusion = f32[1024,4,128]{2,1,0:T(4,128)} fusion(f32[1024,4,128]{2,1,0:T(4,128)} %broadcast_in_dim.70, s32[512]{0:T(512)S(1)} %bitcast.46, f32[512,4,128]{2,1,0:T(4,128)S(1)} %copy.138), kind=kCustom, calls=%fused_computation.5 | custom fusion | bytes 3147776 | tf_op jit(solution)/shard_map/scatter | solution.py:70
  70.2 5.9 %all-to-all-start.1 = ((f32[1024,4,128]{2,1,0:T(4,128)}), f32[1024,4,128]{2,1,0:T(4,128)}, u32[]{:S(2)}, u32[]{:S(2)}) async-start(f32[1024,4,128]{2,1,0:T(4,128)} %scatter_fusion), calls=%async_computation.1 | async-start | bytes 4194304 | tf_op jit(solution)/shard_map/all_to_all | solution.py:73
  79.3 3.3 collective-permute-start.1
  83.0 7.5 %collective-permute-done = f32[1,3,128]{2,1,0:T(4,128)S(1)} collective-permute-done((f32[1,3,128]{2,1,0:T(4,128)S(1)}, f32[1,3,128]{2,1,0:T(4,128)S(1)}, u32[]{:S(2)}, u32[]{:S(2)}) %collective-permute-start) | collective-permute-done | bytes 1568 | tf_op jit(solution)/shard_map/ppermute | solution.py:17
  92.3 4.2 %collective-permute-start.3 = (f32[866,3,1]{0,2,1:T(1,128)S(1)}, f32[866,3,1]{0,2,1:T(1,128)S(1)}, u32[]{:S(2)}, u32[]{:S(2)}) collective-permute-start(f32[866,3,1]{0,2,1:T(1,128)S(1)} %get-tuple-element.37), channel_id=1, source_target_pairs={{0,1},{1,2},{2,3},{4,5},{5,6},{6,7},{8,9},{9,10},{10,11},{12,13},{... | collective-permute-start | bytes 31184 | tf_op jit(solution)/shard_map/ppermute | solution.py:14
  100.9 9.8 %collective-permute-done.3 = f32[866,3,1]{0,2,1:T(1,128)S(1)} collective-permute-done((f32[866,3,1]{0,2,1:T(1,128)S(1)}, f32[866,3,1]{0,2,1:T(1,128)S(1)}, u32[]{:S(2)}, u32[]{:S(2)}) %collective-permute-start.3) | collective-permute-done | bytes 10424 | tf_op jit(solution)/shard_map/ppermute | solution.py:14
  115.7 3.8 %fusion.19 = f32[864,3,128]{2,1,0:T(4,128)S(1)} fusion(f32[864,3,128]{2,1,0:T(4,128)} %copy.177, f32[864,3,128]{2,1,0:T(4,128)} %copy.176, f32[864,3,128]{2,1,0:T(4,128)S(1)} %copy-done.9, f32[1,3,128]{2,1,0:T(4,128)} %copy-done.15, f32[1,3,128]{2,1,0:T(4,128)S(1)} %collective-permute-done), kind=kLoop, calls=%fused_computation.58 | loop fusion | flops 2654208 | bytes 5311488 | tf_op jit(solution)/shard_map/add | solution.py:59
  119.5 8.0 %gather_fusion.2 = f32[1024,3,128]{2,1,0:T(4,128)} fusion(f32[864,3,128]{2,1,0:T(4,128)S(1)} %fusion.19, s32[1024]{0:T(1024)S(1)} %broadcast_clamp_fusion), kind=kCustom, calls=%fused_computation.2 | custom fusion | bytes 3149824 | tf_op jit(solution)/shard_map/jit(_take)/gather | solution.py:75
  129.3 5.9 %fusion.28 = (f32[1024,1,128]{2,1,0:T(1,128)S(1)}, f32[1024,1,128]{2,1,0:T(1,128)S(1)}, f32[1024,1,128]{2,1,0:T(1,128)S(1)}, f32[1024,1,128]{2,1,0:T(1,128)S(1)}) fusion(f32[1024,4,128]{2,1,0:T(4,128)} %all-to-all-done.1), kind=kLoop, calls=%fused_computation.106 | loop fusion | bytes 4194304 | tf_op jit(solution)/shard_map/slice | solution.py:76
  138.8 66.4 %scatter_fusion.1 = f32[864,3,128]{2,1,0:T(4,128)S(1)} fusion(f32[864,3,128]{2,1,0:T(4,128)S(1)} %broadcast_in_dim.67, s32[1024]{0:T(1024)S(1)} %reshape.120, f32[1024,3,128]{2,1,0:T(4,128)} %copy.153), kind=kCustom, calls=%fused_computation.6 | custom fusion | flops 393216 | bytes 4722688 | tf_op jit(solution)/shard_map/scatter-add | solution.py:79
  207.7 6.3 %collective-permute-start.5 = (f32[1,3,128]{2,1,0:T(4,128)S(1)}, f32[1,3,128]{2,1,0:T(4,128)S(1)}, u32[]{:S(2)}, u32[]{:S(2)}) collective-permute-start(f32[1,3,128]{2,1,0:T(4,128)S(1)} %get-tuple-element.32), channel_id=1, source_target_pairs={{0,4},{4,8},{8,12},{12,16},{16,20},{20,24},{24,28},{1,5},{5,9},{9,... | collective-permute-start | bytes 4616 | tf_op jit(solution)/shard_map/ppermute | solution.py:14
  219.3 3.0 fusion.31
  227.2 16.4 %collective-permute-start.7 = (f32[866,3,1]{0,2,1:T(1,128)S(1)}, f32[866,3,1]{0,2,1:T(1,128)S(1)}, u32[]{:S(2)}, u32[]{:S(2)}) collective-permute-start(f32[866,3,1]{0,2,1:T(1,128)S(1)} %copy.157), channel_id=1, source_target_pairs={{0,1},{1,2},{2,3},{4,5},{5,6},{6,7},{8,9},{9,10},{10,11},{12,13},{... | collective-permute-start | bytes 31184 | tf_op jit(solution)/shard_map/ppermute | solution.py:14
  243.6 4.1 %all-to-all-start.2 = ((f32[1024,3,128]{2,1,0:T(4,128)}), f32[1024,3,128]{2,1,0:T(4,128)}, u32[]{:S(2)}, u32[]{:S(2)}) async-start(f32[1024,3,128]{2,1,0:T(4,128)} %copy.153), calls=%async_computation.2 | async-start | bytes 4194304 | tf_op jit(solution)/shard_map/all_to_all | solution.py:80
  251.0 9.7 %fusion = f32[864,3,128]{2,1,0:T(4,128)S(1)} fusion(f32[864,3,128]{2,1,0:T(4,128)S(1)} %multiply_add_fusion, f32[864,3,128]{2,0,1:T(8,128)S(1)} %copy-done.5, f32[866,3,1]{2,1,0:T(4,128)} %copy.158, f32[1,3,128]{2,1,0:T(4,128)S(1)} %collective-permute-done.4, f32[1,3,128]{2,1,0:T(4,128)S(1)} %collective-permute-done.5, f32[866,3,1]{2,1,0:T(4,128)} %copy.156), kind=kLoop, calls=%fused_computation.14 | loop fusion | flops 4976640 | bytes 4005168 | tf_op jit(solution)/shard_map/add | solution.py:87
  260.6 3.5 collective-permute-start.9
  266.1 3.4 collective-permute-done.8
  276.4 4.1 %collective-permute-start.11 = (f32[866,3,1]{0,2,1:T(1,128)}, f32[866,3,1]{0,2,1:T(1,128)S(1)}, u32[]{:S(2)}, u32[]{:S(2)}) collective-permute-start(f32[866,3,1]{0,2,1:T(1,128)} %copy.162), channel_id=1, source_target_pairs={{0,1},{1,2},{2,3},{4,5},{5,6},{6,7},{8,9},{9,10},{10,11},{12,13},{... | collective-permute-start | bytes 31184 | tf_op jit(solution)/shard_map/ppermute | solution.py:14
  284.5 9.9 %fusion.1 = f32[864,3,128]{2,1,0:T(4,128)S(1)} fusion(f32[864,3,128]{2,1,0:T(4,128)S(1)} %copy-done.4, f32[864,3,128]{2,0,1:T(8,128)} %param.10, f32[866,3,1]{2,1,0:T(4,128)} %copy.163, f32[1,3,128]{2,1,0:T(4,128)S(1)} %copy-done.14, f32[1,3,128]{2,1,0:T(4,128)S(1)} %collective-permute-done.9, f32[866,3,1]{2,1,0:T(4,128)} %copy.161), kind=kLoop, calls=%fused_computation.15 | loop fusion | flops 4976640 | bytes 4005168 | tf_op jit(solution)/shard_map/add | solution.py:87
  309.1 18.5 %collective-permute-start.15 = (f32[866,3,1]{0,2,1:T(1,128)}, f32[866,3,1]{0,2,1:T(1,128)S(1)}, u32[]{:S(2)}, u32[]{:S(2)}) collective-permute-start(f32[866,3,1]{0,2,1:T(1,128)} %copy.167), channel_id=1, source_target_pairs={{0,1},{1,2},{2,3},{4,5},{5,6},{6,7},{8,9},{9,10},{10,11},{12,13},{... | collective-permute-start | bytes 31184 | tf_op jit(solution)/shard_map/ppermute | solution.py:14
  335.5 9.7 %fusion.2 = f32[864,3,128]{2,1,0:T(4,128)S(1)} fusion(f32[864,3,128]{2,1,0:T(4,128)S(1)} %fusion.1, f32[864,3,128]{2,0,1:T(8,128)S(1)} %copy-done.6, f32[866,3,1]{2,1,0:T(4,128)} %copy.168, f32[1,3,128]{2,1,0:T(4,128)S(1)} %collective-permute-done.12, f32[1,3,128]{2,1,0:T(4,128)S(1)} %collective-permute-done.13, f32[866,3,1]{2,1,0:T(4,128)} %copy.166), kind=kLoop, calls=%fused_computation.16 | loop fusion | flops 4976640 | bytes 4005168 | tf_op jit(solution)/shard_map/add | solution.py:87
  346.3 3.1 gather_fusion.3
  350.2 16.7 %scatter_fusion.2 = f32[256,3,128]{2,1,0:T(4,128)S(1)} fusion(f32[256,3,128]{2,1,0:T(4,128)S(1)} %broadcast_in_dim.80, s32[512]{0:T(512)S(1)} %copy-done.12, f32[512,3,128]{2,1,0:T(4,128)S(1)} %copy.172), kind=kCustom, calls=%fused_computation.7 | custom fusion | flops 196608 | bytes 2361344 | tf_op jit(solution)/shard_map/scatter-add | solution.py:82
  (131 shorter events, 88.8 us)
Async XLA Ops:
  0.6 17.1 %copy-start = (f32[256,3,128]{2,0,1:T(8,128)S(1)}, f32[256,3,128]{2,0,1:T(8,128)}, u32[]{:S(2)}) copy-start(f32[256,3,128]{2,0,1:T(8,128)} %param.11) | copy-start | bytes 1179652
  0.6 16.1 %copy-start.2 = (s32[256,128]{1,0:T(8,128)S(1)}, s32[256,128]{1,0:T(8,128)}, u32[]{:S(2)}) copy-start(s32[256,128]{1,0:T(8,128)} %param.12) | copy-start | bytes 393220
  8.2 62.0 %all-to-all-start = ((s32[32,32,1]{1,2,0:T(1,128)}), s32[32,32,1]{1,2,0:T(1,128)S(1)}, u32[]{:S(2)}, u32[]{:S(2)}) async-start(s32[32,32,1]{1,2,0:T(1,128)} %bitcast.5), calls=%async_computation | async-start | bytes 32768 | tf_op jit(solution)/shard_map/all_to_all | solution.py:74
  70.2 59.2 %all-to-all-start.1 = ((f32[1024,4,128]{2,1,0:T(4,128)}), f32[1024,4,128]{2,1,0:T(4,128)}, u32[]{:S(2)}, u32[]{:S(2)}) async-start(f32[1024,4,128]{2,1,0:T(4,128)} %scatter_fusion), calls=%async_computation.1 | async-start | bytes 4194304 | tf_op jit(solution)/shard_map/all_to_all | solution.py:73
  77.0 13.5 %collective-permute-start = (f32[1,3,128]{2,1,0:T(4,128)S(1)}, f32[1,3,128]{2,1,0:T(4,128)S(1)}, u32[]{:S(2)}, u32[]{:S(2)}) collective-permute-start(f32[1,3,128]{2,1,0:T(4,128)S(1)} %get-tuple-element.39), channel_id=1, source_target_pairs={{4,0},{8,4},{12,8},{16,12},{20,16},{24,20},{28,24},{5,1},{9,5},{13... | collective-permute-start | bytes 4616 | tf_op jit(solution)/shard_map/ppermute | solution.py:17
  79.3 11.4 %collective-permute-start.1 = (f32[1,3,128]{2,1,0:T(4,128)S(1)}, f32[1,3,128]{2,1,0:T(4,128)S(1)}, u32[]{:S(2)}, u32[]{:S(2)}) collective-permute-start(f32[1,3,128]{2,1,0:T(4,128)S(1)} %get-tuple-element.38), channel_id=1, source_target_pairs={{0,4},{4,8},{8,12},{12,16},{16,20},{20,24},{24,28},{1,5},{5,9},{9,... | collective-permute-start | bytes 4616 | tf_op jit(solution)/shard_map/ppermute | solution.py:14
  91.0 9.9 %collective-permute-start.2 = (f32[866,3,1]{0,2,1:T(1,128)S(1)}, f32[866,3,1]{0,2,1:T(1,128)S(1)}, u32[]{:S(2)}, u32[]{:S(2)}) collective-permute-start(f32[866,3,1]{0,2,1:T(1,128)S(1)} %get-tuple-element.36), channel_id=1, source_target_pairs={{1,0},{2,1},{3,2},{5,4},{6,5},{7,6},{9,8},{10,9},{11,10},{13,12},{... | collective-permute-start | bytes 31184 | tf_op jit(solution)/shard_map/ppermute | solution.py:17
  92.3 18.4 %collective-permute-start.3 = (f32[866,3,1]{0,2,1:T(1,128)S(1)}, f32[866,3,1]{0,2,1:T(1,128)S(1)}, u32[]{:S(2)}, u32[]{:S(2)}) collective-permute-start(f32[866,3,1]{0,2,1:T(1,128)S(1)} %get-tuple-element.37), channel_id=1, source_target_pairs={{0,1},{1,2},{2,3},{4,5},{5,6},{6,7},{8,9},{9,10},{10,11},{12,13},{... | collective-permute-start | bytes 31184 | tf_op jit(solution)/shard_map/ppermute | solution.py:14
  138.8 66.5 %copy-start.18 = (f32[3]{0:T(128)S(1)}, f32[3]{0:T(128)}, u32[]{:S(2)}) copy-start(f32[3]{0:T(128)} %constant.86.clone) | copy-start | bytes 40
  207.7 8.3 %collective-permute-start.5 = (f32[1,3,128]{2,1,0:T(4,128)S(1)}, f32[1,3,128]{2,1,0:T(4,128)S(1)}, u32[]{:S(2)}, u32[]{:S(2)}) collective-permute-start(f32[1,3,128]{2,1,0:T(4,128)S(1)} %get-tuple-element.32), channel_id=1, source_target_pairs={{0,4},{4,8},{8,12},{12,16},{16,20},{20,24},{24,28},{1,5},{5,9},{9,... | collective-permute-start | bytes 4616 | tf_op jit(solution)/shard_map/ppermute | solution.py:14
  214.1 4.9 %collective-permute-start.4 = (f32[1,3,128]{2,1,0:T(4,128)S(1)}, f32[1,3,128]{2,1,0:T(4,128)S(1)}, u32[]{:S(2)}, u32[]{:S(2)}) collective-permute-start(f32[1,3,128]{2,1,0:T(4,128)S(1)} %get-tuple-element.33), channel_id=1, source_target_pairs={{4,0},{8,4},{12,8},{16,12},{20,16},{24,20},{28,24},{5,1},{9,5},{13... | collective-permute-start | bytes 4616 | tf_op jit(solution)/shard_map/ppermute | solution.py:17
  224.1 23.5 %collective-permute-start.6 = (f32[866,3,1]{0,2,1:T(1,128)S(1)}, f32[866,3,1]{0,2,1:T(1,128)S(1)}, u32[]{:S(2)}, u32[]{:S(2)}) collective-permute-start(f32[866,3,1]{0,2,1:T(1,128)S(1)} %copy.155), channel_id=1, source_target_pairs={{1,0},{2,1},{3,2},{5,4},{6,5},{7,6},{9,8},{10,9},{11,10},{13,12},{... | collective-permute-start | bytes 31184 | tf_op jit(solution)/shard_map/ppermute | solution.py:17
  227.2 22.1 %collective-permute-start.7 = (f32[866,3,1]{0,2,1:T(1,128)S(1)}, f32[866,3,1]{0,2,1:T(1,128)S(1)}, u32[]{:S(2)}, u32[]{:S(2)}) collective-permute-start(f32[866,3,1]{0,2,1:T(1,128)S(1)} %copy.157), channel_id=1, source_target_pairs={{0,1},{1,2},{2,3},{4,5},{5,6},{6,7},{8,9},{9,10},{10,11},{12,13},{... | collective-permute-start | bytes 31184 | tf_op jit(solution)/shard_map/ppermute | solution.py:14
  243.6 102.7 %all-to-all-start.2 = ((f32[1024,3,128]{2,1,0:T(4,128)}), f32[1024,3,128]{2,1,0:T(4,128)}, u32[]{:S(2)}, u32[]{:S(2)}) async-start(f32[1024,3,128]{2,1,0:T(4,128)} %copy.153), calls=%async_computation.2 | async-start | bytes 4194304 | tf_op jit(solution)/shard_map/all_to_all | solution.py:80
  260.6 9.9 %copy-start.3 = (f32[864,3,128]{2,1,0:T(4,128)}, f32[864,3,128]{2,1,0:T(4,128)S(1)}, u32[]{:S(2)}) copy-start(f32[864,3,128]{2,1,0:T(4,128)S(1)} %fusion) | copy-start | bytes 3981316
  260.6 5.5 %collective-permute-start.9 = (f32[1,3,128]{2,1,0:T(4,128)S(1)}, f32[1,3,128]{2,1,0:T(4,128)S(1)}, u32[]{:S(2)}, u32[]{:S(2)}) collective-permute-start(f32[1,3,128]{2,1,0:T(4,128)S(1)} %get-tuple-element.30), channel_id=1, source_target_pairs={{0,4},{4,8},{8,12},{12,16},{16,20},{20,24},{24,28},{1,5},{5,9},{9,... | collective-permute-start | bytes 4616 | tf_op jit(solution)/shard_map/ppermute | solution.py:14
  264.2 5.3 %collective-permute-start.8 = (f32[1,3,128]{2,1,0:T(4,128)S(1)}, f32[1,3,128]{2,1,0:T(4,128)S(1)}, u32[]{:S(2)}, u32[]{:S(2)}) collective-permute-start(f32[1,3,128]{2,1,0:T(4,128)S(1)} %get-tuple-element.31), channel_id=1, source_target_pairs={{4,0},{8,4},{12,8},{16,12},{20,16},{24,20},{28,24},{5,1},{9,5},{13... | collective-permute-start | bytes 4616 | tf_op jit(solution)/shard_map/ppermute | solution.py:17
  273.4 7.1 %collective-permute-start.10 = (f32[866,3,1]{0,2,1:T(1,128)}, f32[866,3,1]{0,2,1:T(1,128)}, u32[]{:S(2)}, u32[]{:S(2)}) collective-permute-start(f32[866,3,1]{0,2,1:T(1,128)} %copy.160), channel_id=1, source_target_pairs={{1,0},{2,1},{3,2},{5,4},{6,5},{7,6},{9,8},{10,9},{11,10},{13,12},{... | collective-permute-start | bytes 31184 | tf_op jit(solution)/shard_map/ppermute | solution.py:17
  276.4 6.4 %collective-permute-start.11 = (f32[866,3,1]{0,2,1:T(1,128)}, f32[866,3,1]{0,2,1:T(1,128)S(1)}, u32[]{:S(2)}, u32[]{:S(2)}) collective-permute-start(f32[866,3,1]{0,2,1:T(1,128)} %copy.162), channel_id=1, source_target_pairs={{0,1},{1,2},{2,3},{4,5},{5,6},{6,7},{8,9},{9,10},{10,11},{12,13},{... | collective-permute-start | bytes 31184 | tf_op jit(solution)/shard_map/ppermute | solution.py:14
  294.3 5.0 %collective-permute-start.13 = (f32[1,3,128]{2,1,0:T(4,128)S(1)}, f32[1,3,128]{2,1,0:T(4,128)S(1)}, u32[]{:S(2)}, u32[]{:S(2)}) collective-permute-start(f32[1,3,128]{2,1,0:T(4,128)S(1)} %get-tuple-element.28), channel_id=1, source_target_pairs={{0,4},{4,8},{8,12},{12,16},{16,20},{20,24},{24,28},{1,5},{5,9},{9,... | collective-permute-start | bytes 4616 | tf_op jit(solution)/shard_map/ppermute | solution.py:14
  297.4 4.9 %collective-permute-start.12 = (f32[1,3,128]{2,1,0:T(4,128)S(1)}, f32[1,3,128]{2,1,0:T(4,128)S(1)}, u32[]{:S(2)}, u32[]{:S(2)}) collective-permute-start(f32[1,3,128]{2,1,0:T(4,128)S(1)} %get-tuple-element.29), channel_id=1, source_target_pairs={{4,0},{8,4},{12,8},{16,12},{20,16},{24,20},{28,24},{5,1},{9,5},{13... | collective-permute-start | bytes 4616 | tf_op jit(solution)/shard_map/ppermute | solution.py:17
  309.1 24.7 %collective-permute-start.15 = (f32[866,3,1]{0,2,1:T(1,128)}, f32[866,3,1]{0,2,1:T(1,128)S(1)}, u32[]{:S(2)}, u32[]{:S(2)}) collective-permute-start(f32[866,3,1]{0,2,1:T(1,128)} %copy.167), channel_id=1, source_target_pairs={{0,1},{1,2},{2,3},{4,5},{5,6},{6,7},{8,9},{9,10},{10,11},{12,13},{... | collective-permute-start | bytes 31184 | tf_op jit(solution)/shard_map/ppermute | solution.py:14
  327.6 4.6 %collective-permute-start.14 = (f32[866,3,1]{0,2,1:T(1,128)}, f32[866,3,1]{0,2,1:T(1,128)S(1)}, u32[]{:S(2)}, u32[]{:S(2)}) collective-permute-start(f32[866,3,1]{0,2,1:T(1,128)} %copy.165), channel_id=1, source_target_pairs={{1,0},{2,1},{3,2},{5,4},{6,5},{7,6},{9,8},{10,9},{11,10},{13,12},{... | collective-permute-start | bytes 31184 | tf_op jit(solution)/shard_map/ppermute | solution.py:17
  350.1 17.6 %copy-start.1 = (f32[256,3,128]{2,0,1:T(8,128)S(1)}, f32[256,3,128]{2,0,1:T(8,128)}, u32[]{:S(2)}) copy-start(f32[256,3,128]{2,0,1:T(8,128)} %param.11) | copy-start | bytes 1179652
  (14 other events, 58.2 us)
where the time goes:
time: 375 us; the launch traced here: 368 us
  other arithmetic  131 us (35%)
  local copies, waits for them, and re-layouts  113 us (30%)
  starting transfers between devices  89.9 us (24%)
  waiting for transfers between devices  32.2 us (9%)
    scatter-add x1, other arithmetic, per_device(): air_sum = jax.ops.segment_sum(weighted, in_labels, num_segments=row_count)  66.4 us
    ppermute x8, starting transfers between devices, with_halo(): lax.ppermute(lax.slice_in_dim(block, block.shape[dim] - width, None, axis...  59.4 us
    scatter x1, local copies, waits for them, and re-layouts, per_device(): outgoing = jnp.zeros((devices * capacity, chan_count + 1, seg_width), jnp...  47.5 us
    add x3, other arithmetic, per_device(): current = current + diffusivity * (beside_all(bordered) - 4.0 * current)  29.2 us
    ppermute x8, waiting for transfers between devices, with_halo(): lax.ppermute(lax.slice_in_dim(block, 0, width, axis=dim), axis, backward)  22.3 us
    scatter-add x1, other arithmetic, per_device(): jax.ops.segment_sum(own_rows, intersection_seg, num_segments=ocean_state....  16.7 us
    ppermute x8, starting transfers between devices, with_halo(): lax.ppermute(lax.slice_in_dim(block, 0, width, axis=dim), axis, backward)  13.4 us
    slice x6, local copies, waits for them, and re-layouts, with_halo(): lax.slice_in_dim(block, 0, width, axis=dim)  12.4 us
  transfers between devices with their start and end apart: 19, of which 7 were waited for; matrix products, arithmetic and copies ran while one was open for 36% of the time, Pallas kernels for 0%

commit v1 on v0

v1 whole, which is shorter than its diff:
```python
import functools

import jax
import jax.numpy as jnp
from jax import lax
from jax.experimental import pallas as pl
from jax.experimental.pallas import tpu as pltpu
from jax.sharding import PartitionSpec as P

ITERS = 3
EDGE = 8
FLAT = 32
STRIP = 6 * ITERS
BOTH = ("atm", "ocn")
F32 = jnp.float32
BF16 = jnp.bfloat16


def split3(x):
    high = x.astype(BF16)
    rest = x - high.astype(F32)
    middle = rest.astype(BF16)
    low = (rest - middle.astype(F32)).astype(BF16)
    return high, middle, low


def dot(a, b, contract=(1, 0)):
    dims = (((contract[0],), (contract[1],)), ((), ()))
    return lax.dot_general(a, b, dims, preferred_element_type=F32)


def exact_dots(select, values, contract=(1, 0)):
    parts = [split3(x) for x in values]
    stacked = jnp.concatenate([p[level] for level in (2, 1, 0) for p in parts], axis=1)
    width, count = values[0].shape[1], len(values)
    result = dot(select, stacked, contract)

    def piece(level, index):
        at = (level * count + index) * width
        return result[:, at : at + width]

    return [(piece(0, i) + piece(1, i)) + piece(2, i) for i in range(count)]


def iota(shape, dim):
    return lax.broadcasted_iota(jnp.int32, shape, dim)


def one_hot(condition):
    return condition.astype(F32).astype(BF16)


class Late:
    def __init__(self, source, target, sem):
        self.target, self.copy = target, pltpu.make_async_copy(source, target, sem)
        self.copy.start()

    def get(self):
        if self.copy is not None:
            self.copy.wait()
            self.copy = None
        return self.target


def call(kernel, out_shape, operands, *, late=(), outs=None, flops=0, scratch=(), limit=16):
    total = sum(x.size * x.dtype.itemsize for x in operands)
    extra = {} if outs is None else {"out_specs": outs}
    given = [
        pltpu.with_memory_space_constraint(x, pltpu.HBM) if i in late else x
        for i, x in enumerate(operands)
    ]
    results = len(jax.tree.leaves(out_shape))

    def body(*refs):
        ends = len(operands), len(operands) + results, len(operands) + results + len(late)
        inputs, held = list(refs[: ends[0]]), refs[ends[1] : ends[2]]
        rest = refs[ends[2] :]
        if late:
            sems, rest = rest[0], rest[1:]
            for at, i in enumerate(late):
                inputs[i] = Late(inputs[i], held[at], sems.at[at])
        kernel(*inputs, *refs[ends[0] : ends[1]], *rest)

    held = [pltpu.VMEM(operands[i].shape, operands[i].dtype) for i in late]
    held += [pltpu.SemaphoreType.DMA((len(late),))] if late else []
    return pl.pallas_call(
        body,
        out_shape=out_shape,
        in_specs=[
            pl.BlockSpec(memory_space=pltpu.HBM if i in late else pltpu.VMEM)
            for i in range(len(operands))
        ],
        scratch_shapes=held + list(scratch),
        compiler_params=pltpu.CompilerParams(vmem_limit_bytes=limit << 20),
        cost_estimate=pl.CostEstimate(flops=flops, bytes_accessed=2 * total, transcendentals=0),
        **extra,
    )(*given)


def positions(target, devices):
    count = target.shape[1]
    earlier = one_hot(iota((count, count), 0) < iota((count, count), 1))
    match = iota((devices, count), 0) == target
    before = dot(one_hot(match), earlier)
    return jnp.sum(jnp.where(match, before, 0.0), axis=0, keepdims=True).astype(jnp.int32)


def pack_kernel(devices, cap, dest, seg, row, ocean, mask, area, out, staged, out_sems):
    target = dest.get()[...]
    slots = devices * cap
    count = target.shape[1]
    chans, segs, width = ocean.target.shape
    stores = []

    def send(index, size, values):
        piece = pl.ds(index * cap, size)
        staged[:, piece, :] = values.reshape(devices, size, width)
        store = pltpu.make_async_copy(
            staged.at[:, piece, :], out.at[:, piece, :], out_sems.at[index]
        )
        store.start()
        stores.append(store)

    position = positions(target, devices)
    slot = target * cap + position
    place = one_hot(iota((slots, count), 0) == slot)
    member = one_hot(iota((segs, count), 0) == seg.get()[...])
    of_seg = dot(place, member, (1, 1)).astype(BF16)
    values = ocean.get()
    for chan, sent in enumerate(exact_dots(of_seg, [values[chan] for chan in range(chans)])):
        send(chan, cap, sent)
    sea = dot(of_seg, mask.get()[...].astype(F32).astype(BF16))
    (reach,) = exact_dots(place, [area.get()[...]])
    send(chans, cap, reach * sea)
    line = iota((devices * EDGE, count), 0)
    tall = line == target * EDGE + (position & (EDGE - 1))
    flat = line == target * EDGE
    lane = iota((width, count), 0)
    tall_lane = lane == lax.shift_right_logical(position, EDGE.bit_length() - 1)
    flat_lane = lane == position + FLAT
    value = row.get()[...]
    coarse, fine = lax.shift_right_logical(value, 5).astype(F32), (value & 31).astype(F32)
    lanes = jnp.concatenate(
        [
            jnp.concatenate([jnp.where(at, v, 0.0) for at in (tall_lane, flat_lane)], axis=1)
            for v in (coarse, fine)
        ],
        axis=0,
    ).astype(BF16)
    labels = dot(jnp.concatenate([one_hot(tall), one_hot(flat)], axis=1), lanes, (1, 1))
    send(chans + 1, EDGE, labels[:, :width] * 32.0 + labels[:, width:])
    for store in stores:
        store.wait()


def edge_lane(takes, width, high):
    def lane(line):
        at, first = jnp.full(line.shape, -1, jnp.int32), 0
        for index, take in enumerate(takes):
            inside = (line >= first) & (line < first + take)
            start = index * width + (width - take if high else 0)
            at = jnp.where(inside, start + line - first, at)
            first += take
        return at

    return lane


def strip_lane(first, chans, width):
    def lane(line):
        at, place = jnp.full(line.shape, -1, jnp.int32), line % STRIP
        start = (first + line // STRIP) * width
        low = (place >= ITERS) & (place < 3 * ITERS)
        high = (place >= 3 * ITERS) & (place < 5 * ITERS)
        at = jnp.where(low, start + place - ITERS, at)
        at = jnp.where(high, start + width + place - 5 * ITERS, at)
        return jnp.where(line < chans * STRIP, at, -1)

    return lane


def fill_strip(own, left, right, first, chans, take):
    pieces = []
    gap = [jnp.zeros((ITERS - take, own.shape[1]), F32)] if take < ITERS else []
    for chan in range(chans):
        beside = slice(first + chan * take, first + (chan + 1) * take)
        inner = slice(chan * STRIP + ITERS, (chan + 1) * STRIP - ITERS)
        pieces += gap + [left[beside, :], own[inner, :], right[beside, :]] + gap
    pieces.append(jnp.zeros((own.shape[0] - chans * STRIP, own.shape[1]), F32))
    return jnp.concatenate(pieces, axis=0)


def edge_columns(pieces, outputs):
    width = pieces[0][0].shape[1]
    length = outputs[0][0].shape[1]
    tail = length - sum(piece.shape[0] for piece in pieces[0])
    whole = jnp.concatenate(
        [jnp.concatenate([*piece, jnp.zeros((tail, width), F32)], axis=0) for piece in pieces],
        axis=1,
    )
    rows = []
    for ref, lane in outputs:
        shape = (ref.shape[0], whole.shape[1])
        rows.append(iota(shape, 1) == lane(iota(shape, 0)))
    select = one_hot(jnp.concatenate([row.astype(jnp.int32) for row in rows], axis=0) > 0)
    top, middle, bottom = split3(whole)
    edges = dot(select, bottom, (1, 1)) + dot(select, middle, (1, 1))
    edges = edges + dot(select, top, (1, 1))
    first = 0
    for ref, _ in outputs:
        ref[...] = edges[first : first + ref.shape[0]]
        first += ref.shape[0]


def first_columns_kernel(before, after, atm, diff, low, high, own):
    chans, _, width = atm.target.shape
    bodies = [ref.get()[chan] for ref in (atm, diff) for chan in range(chans)]
    takes = [1] * chans + [ITERS - 1] * chans
    pieces = [(before[i], body, after[i]) for i, body in enumerate(bodies)]
    edge_columns(
        pieces,
        [
            (low, edge_lane(takes, width, False)),
            (high, edge_lane(takes, width, True)),
            (own, strip_lane(chans, chans, width)),
        ],
    )


def columns_kernel(before, body, after, low, high, own):
    chans, _, width = body.shape
    pieces = [(before[i], body[i], after[i]) for i in range(chans)]
    edge_columns(
        pieces,
        [
            (low, edge_lane([ITERS] * chans, width, False)),
            (high, edge_lane([ITERS] * chans, width, True)),
            (own, strip_lane(0, chans, width)),
        ],
    )


def beside_rows(x):
    rows = x.shape[0]
    return pltpu.roll(x, rows - 1, 0) + pltpu.roll(x, 1, 0)


def beside_columns(x):
    width = x.shape[1]
    return pltpu.roll(x, width - 1, 1), pltpu.roll(x, 1, 1)


def beside_body(body, side=None):
    rows, width = body.shape
    lane = iota(body.shape, 1)
    east, west = beside_columns(body)
    east = jnp.where(lane == width - 1, 0.0 if side is None else side, east)
    west = jnp.where(lane == 0, 0.0 if side is None else side, west)
    return beside_rows(body) + east + west


def smooth_kernel(cap, before, after, atm, dest, seg, smooth, seg_select, staged, held, sems):
    chans, rows, width = staged.shape
    segs, slots = held.shape
    target = dest.get()[...]
    slot = target * cap + positions(target, slots // cap)
    place = one_hot(iota((slots, target.shape[1]), 0) == slot)
    member = one_hot(iota((segs, target.shape[1]), 0) == seg.get()[...])
    held[...] = dot(member, place, (1, 1)).astype(BF16)
    stores = [pltpu.make_async_copy(held, seg_select, sems.at[0])]
    stores[0].start()
    state = atm.get()
    for chan in range(chans):
        body = jnp.concatenate([before[chan], state[chan], after[chan]], axis=0)
        staged[chan] = (0.5 * body + 0.125 * beside_body(body))[EDGE : EDGE + rows]
    stores.append(pltpu.make_async_copy(staged, smooth, sems.at[1]))
    stores[1].start()
    for store in stores:
        store.wait()


def nearest_columns(left, right, width, chans):
    edges = jnp.concatenate([left[:EDGE, :], right[:EDGE, :]], axis=0)
    shape = (6 * EDGE, chans * width)
    which, lane = iota(shape, 0), iota(shape, 1)
    line = which % (2 * EDGE)
    at = jnp.where(line < EDGE, line * width, (line - EDGE) * width + width - 1)
    select = one_hot((lane == at) & (line % EDGE < chans))
    return dot(jnp.concatenate(split3(edges), axis=0), select, (0, 0))


def flux_kernel(cap, incoming, left, right, smooth, out, label_rows, staged, sems):
    devices, _, width = incoming.shape
    chans, rows, _ = smooth.target.shape
    side = 0.125 * nearest_columns(left, right, width, chans)[EDGE : EDGE + rows]
    label_rows[...] = incoming[:, (chans + 1) * cap, :]
    whole = smooth.get()
    smoothed = jnp.concatenate([whole[chan] for chan in range(chans)], axis=1) + side
    table = jnp.concatenate(split3(smoothed)[::-1], axis=1)
    groups = sems.shape[0]
    each = devices // groups
    stores = []
    for group in range(groups):
        owners = slice(group * each, (group + 1) * each)

        def part(index):
            piece = incoming[owners, index * cap : (index + 1) * cap, :]
            return piece.reshape(each * cap, width)

        labels = incoming[owners, (chans + 1) * cap :, :]
        labels = jnp.concatenate(
            [labels[i, :, j : j + 1] for i in range(each) for j in range(cap // EDGE)], axis=0
        ).astype(jnp.int32)
        select = one_hot(iota((each * cap, rows), 1) == labels)
        found = dot(select, table)
        pieces = [found[:, i * width : (i + 1) * width] for i in range(3 * chans)]
        air = [
            (pieces[i] + pieces[chans + i]) + pieces[2 * chans + i] for i in range(chans)
        ]
        wind_east = air[1] - part(1)
        wind_north = air[2] - part(2)
        wind_speed = jnp.sqrt(wind_east * wind_east + wind_north * wind_north + 0.5)
        temp_gap = part(0) - air[0]
        factor = 1.0 + 0.5 * jnp.tanh(temp_gap / wind_speed)
        common = part(3) * factor * wind_speed
        for index, value in enumerate((0.8 * temp_gap, 0.6 * wind_east, 0.6 * wind_north)):
            staged[owners, index * cap : (index + 1) * cap, :] = (common * value).reshape(
                each, cap, width
            )
        store = pltpu.make_async_copy(
            staged.at[pl.ds(group * each, each)],
            out.at[pl.ds(group * each, each)],
            sems.at[group],
        )
        store.start()
        stores.append(store)
    for store in stores:
        store.wait()


def forced_kernel(cap, label_rows, weighted, atm, forced, top, bottom):
    devices, _, width = weighted.target.shape
    chans, rows, _ = forced.shape
    slots = devices * cap
    log = cap.bit_length() - 1
    labels = label_rows[...].astype(jnp.int32)
    spread = one_hot(iota((width, slots), 0) == (iota((width, slots), 1) & (cap - 1)) + FLAT)
    coarse = dot(lax.shift_right_logical(labels, 5).astype(F32).astype(BF16), spread)
    fine = dot((labels & 31).astype(F32).astype(BF16), spread)
    owner = lax.shift_right_logical(iota((devices, slots), 1), log)
    label = jnp.where(owner == iota((devices, slots), 0), coarse * 32.0 + fine, 0.0)
    label = jnp.sum(label, axis=0, keepdims=True).astype(jnp.int32)
    select = one_hot(iota((rows, slots), 0) == label)
    sent, state = weighted.get(), atm.get()
    values = [
        sent[:, chan * cap : (chan + 1) * cap, :].reshape(slots, width) for chan in range(chans)
    ]
    for chan, air_sum in enumerate(exact_dots(select, values)):
        result = state[chan] + air_sum if chan == 0 else state[chan] - air_sum
        forced[chan] = result
        top[chan] = result[:EDGE]
        bottom[chan] = result[-EDGE:]


def diffuse_kernel(
    forced, before, after, diff_own, diff_left, diff_right, diff_before, diff_after, diff,
    out, diff_strip,
):
    chans, rows, width = forced.shape
    diff_strip[...] = fill_strip(diff_own, diff_left, diff_right, chans, chans, ITERS - 1)
    for chan in range(chans):
        body = jnp.concatenate([before[chan], forced[chan], after[chan]], axis=0)
        body_diff = [diff_before[chans + chan], diff.get()[chan], diff_after[chans + chan]]
        body_diff = jnp.concatenate(body_diff, axis=0)
        for _ in range(ITERS):
            body = body + body_diff * (beside_body(body) - 4.0 * body)
        out[chan] = body[EDGE : EDGE + rows]


def sides_kernel(inner, own, left, right, diff_strip, out):
    chans, rows, width = inner.shape
    state = fill_strip(own, left, right, 0, chans, ITERS)
    spread = diff_strip[...]
    for _ in range(ITERS):
        east, west = beside_columns(state)
        state = state + spread * ((beside_rows(state) + east + west) - 4.0 * state)
    lines = state.shape[0]
    shape = (3 * lines, chans * width)
    which, lane = iota(shape, 0) % lines, iota(shape, 1)
    place, start = which % STRIP, which // STRIP * width
    low = (place >= ITERS) & (place < 2 * ITERS) & (lane == start + place - ITERS)
    high = place >= 4 * ITERS
    high = high & (place < 5 * ITERS) & (lane == start + width + place - 5 * ITERS)
    select = one_hot((which < chans * STRIP) & (low | high))
    edges = dot(jnp.concatenate(split3(state), axis=0), select, (0, 0))
    lane = iota((rows, width), 1)
    outer = (lane < ITERS) | (lane >= width - ITERS)
    for chan in range(chans):
        edge = edges[EDGE : EDGE + rows, chan * width : (chan + 1) * width]
        out[chan] = jnp.where(outer, edge, inner[chan])


def sum_kernel(cap, returned, seg_select, out):
    devices, _, width = returned.shape
    values = [
        returned[:, chan * cap : (chan + 1) * cap, :].reshape(devices * cap, width)
        for chan in range(out.shape[0])
    ]
    for chan, total in enumerate(exact_dots(seg_select.get()[...], values)):
        out[chan] = total


def shift(axis, low_edge, high_edge):
    count = lax.axis_size(axis)
    forward = [(i, i + 1) for i in range(count - 1)]
    backward = [(target, source) for source, target in forward]
    return lax.ppermute(high_edge, axis, forward), lax.ppermute(low_edge, axis, backward)


def per_device(atm, diff, ocean, mask, area, seg, dest, row):
    atm_count, ocn_count = lax.axis_size("atm"), lax.axis_size("ocn")
    devices = atm_count * ocn_count
    rows, chans, width = atm.shape
    count = seg.shape[0]
    segs = ocean.shape[0]
    cap = max(2, 2 * count // devices)
    slots = devices * cap
    atm = jnp.transpose(atm, (1, 0, 2))
    diff = jnp.transpose(diff, (1, 0, 2))
    ocean = jnp.transpose(ocean, (1, 0, 2))

    def shape(*dims, dtype=F32):
        return jax.ShapeDtypeStruct(dims, dtype)

    hbm, fast = pltpu.HBM, pl.BlockSpec(memory_space=pltpu.VMEM)
    slow = pl.BlockSpec(memory_space=hbm)
    dest, seg, row = dest.reshape(1, count), seg.reshape(1, count), row.reshape(1, count)
    packed = (devices, (chans + 1) * cap + EDGE, width)
    given = (dest, seg, row, ocean, mask, area)
    out = call(
        functools.partial(pack_kernel, devices, cap),
        hbm(packed, F32),
        given,
        late=tuple(range(len(given))),
        outs=slow,
        scratch=[pltpu.VMEM(packed, F32), pltpu.SemaphoreType.DMA((chans + 2,))],
        flops=2 * slots * count * (segs + 3 * width) + 6 * slots * segs * chans * width,
    )
    incoming = lax.all_to_all(out, BOTH, split_axis=0, concat_axis=0, tiled=True)

    long = -(-(rows + 2 * EDGE) // 128) * 128

    def lines(columns):
        return shape(-(-columns // EDGE) * EDGE, long)

    first = jnp.concatenate([atm[:, :EDGE], diff[:, :EDGE]], axis=0)
    final = jnp.concatenate([atm[:, -EDGE:], diff[:, -EDGE:]], axis=0)
    before, after = shift("atm", first, final)
    low, high, diff_own = call(
        first_columns_kernel,
        (lines(chans * ITERS), lines(chans * ITERS), lines(chans * STRIP)),
        (before, after, atm, diff),
        late=(2, 3),
        flops=6 * 2 * chans * long * width * 16,
    )
    left, right = shift("ocn", low, high)
    smooth, seg_select = call(
        functools.partial(smooth_kernel, cap),
        (hbm((chans, rows, width), F32), hbm((segs, slots), BF16)),
        (before, after, atm, dest, seg),
        late=(2, 3, 4),
        outs=(slow, slow),
        scratch=[
            pltpu.VMEM((chans, rows, width), F32),
            pltpu.VMEM((segs, slots), BF16),
            pltpu.SemaphoreType.DMA((2,)),
        ],
        flops=100 * rows * chans * width,
    )
    weighted, label_rows = call(
        functools.partial(flux_kernel, cap),
        (hbm((devices, chans * cap, width), F32), shape(devices, width)),
        (incoming, left, right, smooth),
        late=(3,),
        outs=(slow, fast),
        scratch=[
            pltpu.VMEM((devices, chans * cap, width), F32),
            pltpu.SemaphoreType.DMA((4,)),
        ],
        flops=100 * slots * width,
    )
    returned = lax.all_to_all(weighted, BOTH, split_axis=0, concat_axis=0, tiled=True)
    forced, top, bottom = call(
        functools.partial(forced_kernel, cap),
        (
            pltpu.VMEM((chans, rows, width), F32),
            shape(chans, EDGE, width),
            shape(chans, EDGE, width),
        ),
        (label_rows, weighted, atm),
        late=(1, 2),
        flops=6 * slots * rows * chans * width,
    )
    forced_before, forced_after = shift("atm", top, bottom)
    forced_low, forced_high, forced_own = call(
        columns_kernel,
        (lines(chans * ITERS), lines(chans * ITERS), lines(chans * STRIP)),
        (forced_before, forced, forced_after),
        flops=6 * chans * long * width * 16,
    )
    forced_left, forced_right = shift("ocn", forced_low, forced_high)
    inner, diff_strip = call(
        diffuse_kernel,
        (shape(chans, rows, width), lines(chans * STRIP)),
        (forced, forced_before, forced_after, diff_own, left, right, before, after, diff),
        late=(8,),
        flops=100 * chans * rows * width,
    )
    atm_next = call(
        sides_kernel,
        shape(chans, rows, width),
        (inner, forced_own, forced_left, forced_right, diff_strip),
        flops=100 * chans * rows * width,
    )
    ocean_flux = call(
        functools.partial(sum_kernel, cap),
        shape(chans, segs, width),
        (returned, seg_select),
        late=(1,),
        flops=6 * slots * segs * chans * width,
    )
    return jnp.transpose(atm_next, (1, 0, 2)), jnp.transpose(ocean_flux, (1, 0, 2))


def solution(mesh):
    placed = (
        P("atm", None, "ocn"),
        P("atm", None, "ocn"),
        P(BOTH, None, None),
        P(BOTH, None),
        P(BOTH, None),
        P(BOTH),
        P(BOTH, None),
        P(BOTH),
    )
    return jax.shard_map(
        per_device,
        mesh=mesh,
        in_specs=placed,
        out_specs=(P("atm", None, "ocn"), P(BOTH, None, None)),
        check_vma=False,
    )
```

time: 375 us -> 117 us (0.31); the launches traced: 368 us -> 115 us
  other arithmetic: 131 us -> 0.01 us
  local copies, waits for them, and re-layouts: 113 us -> 0.77 us
  starting transfers between devices: 89.9 us -> 29.8 us
  Pallas kernels: 0 us -> 31.7 us
  waiting for transfers between devices: 32.2 us -> 51.6 us
    scatter-add x2 -> x0, other arithmetic: 83.1 us -> none  [the longest x1 66.4 us: per_device(): air_sum = jax.ops.segment_sum(weighted, in_labels, num_segments=row_count)]
    ppermute x16 -> x8, starting transfers between devices: 72.8 us -> 18 us  [the longest x4 11.6 us: shift(): lax.ppermute(high_edge, axis, forward)]
    scatter x2 -> x0, local copies, waits for them, and re-layouts: 50.1 us -> none  [the longest x1 47.5 us: per_device(): outgoing = jnp.zeros((devices * capacity, chan_count + 1, seg_width), jnp...]
    add x5 -> x0, other arithmetic: 35.4 us -> none  [the longest x3 29.2 us: per_device(): current = current + diffusivity * (beside_all(bordered) - 4.0 * current)]
    pallas_call x0 -> x9, Pallas kernels: none -> 31.7 us  [call(): pl.pallas_call(body, out_shape=out_shape, in_specs=[pl.BlockSpec(memory_s...]
    slice x15 -> x1, local copies, waits for them, and re-layouts: 23.7 us -> 0.77 us  [per_device(): first = jnp.concatenate([atm[:, :EDGE], diff[:, :EDGE]], axis=0)]
    all_to_all x3 -> x2, waiting for transfers between devices: 0.01 us -> 21.4 us  [the longest x1 13 us: per_device(): lax.all_to_all(out, BOTH, split_axis=0, concat_axis=0, tiled=True)]
    gather x4 -> x0, local copies, waits for them, and re-layouts: 14.4 us -> none  [the longest x1 7.99 us: per_device(): air_rows = jnp.take(smoothed, in_labels, axis=0)]
  transfers between devices with their start and end apart: 19 -> 10, of which waited for: 7 -> 7; matrix products, arithmetic and copies ran while one was open for 36% -> 1% of each run, Pallas kernels for 0% -> 16%
where the time goes in v1:
time: 117 us; the launch traced here: 115 us
  waiting for transfers between devices  51.6 us (44%)
  Pallas kernels  31.7 us (27%)
  starting transfers between devices  29.8 us (25%)
    pallas_call x9, Pallas kernels, call(): pl.pallas_call(body, out_shape=out_shape, in_specs=[pl.BlockSpec(memory_s...  31.7 us
    ppermute x4, waiting for transfers between devices, shift(): lax.ppermute(high_edge, axis, forward)  23.2 us
    all_to_all x1, waiting for transfers between devices, per_device(): lax.all_to_all(out, BOTH, split_axis=0, concat_axis=0, tiled=True)  13 us
    ppermute x4, starting transfers between devices, shift(): lax.ppermute(high_edge, axis, forward)  11.6 us
    all_to_all x1, waiting for transfers between devices, per_device(): lax.all_to_all(weighted, BOTH, split_axis=0, concat_axis=0, tiled=True)  8.39 us
    all_to_all x1, starting transfers between devices, per_device(): lax.all_to_all(out, BOTH, split_axis=0, concat_axis=0, tiled=True)  7.1 us
    ppermute x4, waiting for transfers between devices, shift(): lax.ppermute(low_edge, axis, backward)  7.06 us
    ppermute x4, starting transfers between devices, shift(): lax.ppermute(low_edge, axis, backward)  6.43 us
  transfers between devices with their start and end apart: 10, of which 7 were waited for; matrix products, arithmetic and copies ran while one was open for 1% of the time, Pallas kernels for 16%

profile of v1, /device:TPU:1, one launch (start us, length us, event | category | flops | bytes accessed | tf_op | source)
XLA Modules:
  0.0 114.8 jit_solution(14438738756705926540)
XLA Ops:
  0.6 5.5 %shard_map.95 = f32[32,136,128]{2,1,0:T(8,128)} custom-call(s32[1,512]{1,0:T(1,128)} %bitcast.17, s32[1,512]{1,0:T(1,128)} %bitcast.19, s32[1,512]{1,0:T(1,128)} %bitcast.22, f32[3,256,128]{2,1,0:T(8,128)} %bitcast.21, s32[256,128]{1,0:T(8,128)} %refs_4_.1, f32[512,128]{1,0:T(8,128)} %refs_5_.1), custom_call_target="tpu_custom_call" | custom-call | flops 1275068416 | bytes 1585152 | tf_op jit(solution)/shard_map/pallas_call | solution.py:86
  6.2 7.1 %all-to-all-start = ((f32[32,136,128]{2,1,0:T(8,128)}), f32[32,136,128]{2,1,0:T(8,128)S(1)}, u32[]{:S(2)}, u32[]{:S(2)}) async-start(f32[32,136,128]{2,1,0:T(8,128)} %shard_map.95), calls=%async_computation | async-start | bytes 4456448 | tf_op jit(solution)/shard_map/all_to_all | solution.py:449
  14.1 3.5 %collective-permute-start = (f32[6,8,128]{2,1,0:T(8,128)S(1)}, f32[6,8,128]{2,1,0:T(8,128)S(1)}, u32[]{:S(2)}, u32[]{:S(2)}) collective-permute-start(f32[6,8,128]{2,1,0:T(8,128)S(1)} %pad_maximum_fusion), channel_id=1, source_target_pairs={{0,4},{4,8},{8,12},{12,16},{16,20},{20,24},{24,28},{1,5},{5,9},{9,... | collective-permute-start | bytes 73736 | tf_op jit(solution)/shard_map/ppermute | solution.py:417
  17.6 1.9 %collective-permute-start.1 = (f32[6,8,128]{2,1,0:T(8,128)S(1)}, f32[6,8,128]{2,1,0:T(8,128)S(1)}, u32[]{:S(2)}, u32[]{:S(2)}) collective-permute-start(f32[6,8,128]{2,1,0:T(8,128)S(1)} %pad_maximum_fusion.1), channel_id=1, source_target_pairs={{4,0},{8,4},{12,8},{16,12},{20,16},{24,20},{28,24},{5,1},{9,5},{13... | collective-permute-start | bytes 73736 | tf_op jit(solution)/shard_map/ppermute | solution.py:417
  19.5 6.1 %collective-permute-done.refs_0_.refs_6_ = f32[6,8,128]{2,1,0:T(8,128)S(1)} collective-permute-done((f32[6,8,128]{2,1,0:T(8,128)S(1)}, f32[6,8,128]{2,1,0:T(8,128)S(1)}, u32[]{:S(2)}, u32[]{:S(2)}) %collective-permute-start) | collective-permute-done | bytes 24608 | tf_op jit(solution)/shard_map/ppermute | solution.py:417
  25.6 3.7 %collective-permute-done.1.refs_1_.refs_7_ = f32[6,8,128]{2,1,0:T(8,128)S(1)} collective-permute-done((f32[6,8,128]{2,1,0:T(8,128)S(1)}, f32[6,8,128]{2,1,0:T(8,128)S(1)}, u32[]{:S(2)}, u32[]{:S(2)}) %collective-permute-start.1) | collective-permute-done | bytes 24608 | tf_op jit(solution)/shard_map/ppermute | solution.py:417
  29.3 3.1 %shard_map.96 = (f32[16,896]{1,0:T(8,128)S(1)}, f32[16,896]{1,0:T(8,128)S(1)}, f32[56,896]{1,0:T(8,128)S(1)}) custom-call(f32[6,8,128]{2,1,0:T(8,128)S(1)} %collective-permute-done.refs_0_.refs_6_, f32[6,8,128]{2,1,0:T(8,128)S(1)} %collective-permute-done.1.refs_1_.refs_7_, f32[3,864,128]{2,1,0:T(8,128)} %bitcast.9, f32[3,864,128]{2,1,0:T(8,128)} %bitcast.13), custom_call_target="tpu_custom_call" | custom-call | flops 66060288 | bytes 5406720 | tf_op jit(solution)/shard_map/pallas_call | solution.py:86
  32.4 1.3 %collective-permute-start.2 = (f32[16,896]{1,0:T(8,128)S(1)}, f32[16,896]{1,0:T(8,128)S(1)}, u32[]{:S(2)}, u32[]{:S(2)}) collective-permute-start(f32[16,896]{1,0:T(8,128)S(1)} %get-tuple-element.17), channel_id=1, source_target_pairs={{0,1},{1,2},{2,3},{4,5},{5,6},{6,7},{8,9},{9,10},{10,11},{12,13},{... | collective-permute-start | bytes 172040 | tf_op jit(solution)/shard_map/ppermute | solution.py:417
  33.7 1.3 %collective-permute-start.3 = (f32[16,896]{1,0:T(8,128)S(1)}, f32[16,896]{1,0:T(8,128)S(1)}, u32[]{:S(2)}, u32[]{:S(2)}) collective-permute-start(f32[16,896]{1,0:T(8,128)S(1)} %get-tuple-element.18), channel_id=1, source_target_pairs={{1,0},{2,1},{3,2},{5,4},{6,5},{7,6},{9,8},{10,9},{11,10},{13,12},{... | collective-permute-start | bytes 172040 | tf_op jit(solution)/shard_map/ppermute | solution.py:417
  35.0 3.9 %shard_map.97 = (f32[3,864,128]{2,1,0:T(8,128)}, bf16[256,1024]{1,0:T(8,128)(2,1)}) custom-call(f32[6,8,128]{2,1,0:T(8,128)S(1)} %collective-permute-done.refs_0_.refs_6_, f32[6,8,128]{2,1,0:T(8,128)S(1)} %collective-permute-done.1.refs_1_.refs_7_, f32[3,864,128]{2,1,0:T(8,128)} %bitcast.10, s32[1,512]{1,0:T(1,128)} %bitcast.18, s32[1,512]{1,0:T(1,128)} %bitcast.20), custom_call_target="tpu_custom_call" | custom-call | flops 33177600 | bytes 2760704 | tf_op jit(solution)/shard_map/pallas_call | solution.py:86
  38.9 12.4 %collective-permute-done.2.refs_1_.refs_4_ = f32[16,896]{1,0:T(8,128)S(1)} collective-permute-done((f32[16,896]{1,0:T(8,128)S(1)}, f32[16,896]{1,0:T(8,128)S(1)}, u32[]{:S(2)}, u32[]{:S(2)}) %collective-permute-start.2) | collective-permute-done | bytes 57376 | tf_op jit(solution)/shard_map/ppermute | solution.py:417
  51.3 13.0 %all-to-all-done.refs_0_ = f32[32,136,128]{2,1,0:T(8,128)S(1)} async-done(((f32[32,136,128]{2,1,0:T(8,128)}), f32[32,136,128]{2,1,0:T(8,128)S(1)}, u32[]{:S(2)}, u32[]{:S(2)}) %all-to-all-start) | async-done | bytes 2228256 | tf_op jit(solution)/shard_map/all_to_all | solution.py:449
  64.3 5.6 %shard_map.98 = (f32[32,96,128]{2,1,0:T(8,128)}, f32[32,128]{1,0:T(8,128)S(1)}) custom-call(f32[32,136,128]{2,1,0:T(8,128)S(1)} %all-to-all-done.refs_0_, f32[16,896]{1,0:T(8,128)S(1)} %collective-permute-done.2.refs_1_.refs_4_, f32[16,896]{1,0:T(8,128)S(1)} %collective-permute-done.3.refs_2_.refs_5_, f32[3,864,128]{2,1,0:T(8,128)} %get-tuple-element.19.refs_3_), custom_call_target="tpu_custom_call" | custom-call | flops 13107200 | bytes 7340032 | tf_op jit(solution)/shard_map/pallas_call | solution.py:86
  69.9 4.7 %all-to-all-start.1 = ((f32[32,96,128]{2,1,0:T(8,128)}), f32[32,96,128]{2,1,0:T(8,128)S(1)}, u32[]{:S(2)}, u32[]{:S(2)}) async-start(f32[32,96,128]{2,1,0:T(8,128)} %get-tuple-element.21.refs_1_), calls=%async_computation.1 | async-start | bytes 3145728 | tf_op jit(solution)/shard_map/all_to_all | solution.py:492
  74.6 4.3 %shard_map.99 = (f32[3,864,128]{2,1,0:T(8,128)S(1)}, f32[3,8,128]{2,1,0:T(8,128)S(1)}, f32[3,8,128]{2,1,0:T(8,128)S(1)}) custom-call(f32[32,128]{1,0:T(8,128)S(1)} %get-tuple-element.20.refs_0_, f32[32,96,128]{2,1,0:T(8,128)} %get-tuple-element.21.refs_1_, f32[3,864,128]{2,1,0:T(8,128)} %bitcast.11), custom_call_target="tpu_custom_call" | custom-call | flops 2038431744 | bytes 5832704 | tf_op jit(solution)/shard_map/pallas_call | solution.py:86
  78.9 3.5 %collective-permute-start.4 = (f32[3,8,128]{2,1,0:T(8,128)S(1)}, f32[3,8,128]{2,1,0:T(8,128)S(1)}, u32[]{:S(2)}, u32[]{:S(2)}) collective-permute-start(f32[3,8,128]{2,1,0:T(8,128)S(1)} %get-tuple-element.23), channel_id=1, source_target_pairs={{0,4},{4,8},{8,12},{12,16},{16,20},{20,24},{24,28},{1,5},{5,9},{9,... | collective-permute-start | bytes 36872 | tf_op jit(solution)/shard_map/ppermute | solution.py:417
  82.5 1.9 %collective-permute-start.5 = (f32[3,8,128]{2,1,0:T(8,128)S(1)}, f32[3,8,128]{2,1,0:T(8,128)S(1)}, u32[]{:S(2)}, u32[]{:S(2)}) collective-permute-start(f32[3,8,128]{2,1,0:T(8,128)S(1)} %get-tuple-element.24), channel_id=1, source_target_pairs={{4,0},{8,4},{12,8},{16,12},{20,16},{24,20},{28,24},{5,1},{9,5},{13... | collective-permute-start | bytes 36872 | tf_op jit(solution)/shard_map/ppermute | solution.py:417
  84.4 3.4 %collective-permute-done.5.refs_2_ = f32[3,8,128]{2,1,0:T(8,128)S(1)} collective-permute-done((f32[3,8,128]{2,1,0:T(8,128)S(1)}, f32[3,8,128]{2,1,0:T(8,128)S(1)}, u32[]{:S(2)}, u32[]{:S(2)}) %collective-permute-start.5) | collective-permute-done | bytes 12320 | tf_op jit(solution)/shard_map/ppermute | solution.py:417
  88.6 3.2 %collective-permute-start.6 = (f32[16,896]{1,0:T(8,128)S(1)}, f32[16,896]{1,0:T(8,128)S(1)}, u32[]{:S(2)}, u32[]{:S(2)}) collective-permute-start(f32[16,896]{1,0:T(8,128)S(1)} %get-tuple-element.28), channel_id=1, source_target_pairs={{0,1},{1,2},{2,3},{4,5},{5,6},{6,7},{8,9},{9,10},{10,11},{12,13},{... | collective-permute-start | bytes 172040 | tf_op jit(solution)/shard_map/ppermute | solution.py:417
  93.1 3.5 %shard_map.100 = (f32[3,864,128]{2,1,0:T(8,128)S(1)}, f32[56,896]{1,0:T(8,128)S(1)}) custom-call(f32[3,864,128]{2,1,0:T(8,128)S(1)} %get-tuple-element.22.refs_0_.refs_1_, f32[3,8,128]{2,1,0:T(8,128)S(1)} %collective-permute-done.4.refs_1_.refs_0_, f32[3,8,128]{2,1,0:T(8,128)S(1)} %collective-permute-done.5.refs_2_, ...), custom_call_target="tpu_custom_call" | custom-call | flops 33177600 | bytes 6086656 | tf_op jit(solution)/shard_map/pallas_call | solution.py:86
  96.6 4.7 %collective-permute-done.6.refs_2_ = f32[16,896]{1,0:T(8,128)S(1)} collective-permute-done((f32[16,896]{1,0:T(8,128)S(1)}, f32[16,896]{1,0:T(8,128)S(1)}, u32[]{:S(2)}, u32[]{:S(2)}) %collective-permute-start.6) | collective-permute-done | bytes 57376 | tf_op jit(solution)/shard_map/ppermute | solution.py:417
  101.3 2.2 %shard_map.102 = f32[3,864,128]{2,1,0:T(8,128)} custom-call(f32[3,864,128]{2,1,0:T(8,128)S(1)} %get-tuple-element.26.refs_0_, f32[56,896]{1,0:T(8,128)S(1)} %get-tuple-element.27.refs_1_, f32[16,896]{1,0:T(8,128)S(1)} %collective-permute-done.6.refs_2_, f32[16,896]{1,0:T(8,128)S(1)} %collective-permute-done.7.refs_3_, f32[56,896]{1,0:T(8,128)S(1)} %get-tuple-element.30.refs_4_), custom_call_target="tpu_custom_call" | custom-call | flops 33177600 | bytes 3686400 | tf_op jit(solution)/shard_map/pallas_call | solution.py:86
  103.6 8.4 %all-to-all-done.1.refs_0_ = f32[32,96,128]{2,1,0:T(8,128)S(1)} async-done(((f32[32,96,128]{2,1,0:T(8,128)}), f32[32,96,128]{2,1,0:T(8,128)S(1)}, u32[]{:S(2)}, u32[]{:S(2)}) %all-to-all-start.1) | async-done | bytes 1572896 | tf_op jit(solution)/shard_map/all_to_all | solution.py:492
  111.9 2.7 %shard_map.103 = f32[3,256,128]{2,1,0:T(8,128)} custom-call(f32[32,96,128]{2,1,0:T(8,128)S(1)} %all-to-all-done.1.refs_0_, bf16[256,1024]{1,0:T(8,128)(2,1)} %get-tuple-element.31.refs_1_), custom_call_target="tpu_custom_call" | custom-call | flops 603979776 | bytes 4194304 | tf_op jit(solution)/shard_map/pallas_call | solution.py:86
  (8 shorter events, 2.9 us)
Async XLA Ops:
  6.2 58.1 %all-to-all-start = ((f32[32,136,128]{2,1,0:T(8,128)}), f32[32,136,128]{2,1,0:T(8,128)S(1)}, u32[]{:S(2)}, u32[]{:S(2)}) async-start(f32[32,136,128]{2,1,0:T(8,128)} %shard_map.95), calls=%async_computation | async-start | bytes 4456448 | tf_op jit(solution)/shard_map/all_to_all | solution.py:449
  14.1 11.5 %collective-permute-start = (f32[6,8,128]{2,1,0:T(8,128)S(1)}, f32[6,8,128]{2,1,0:T(8,128)S(1)}, u32[]{:S(2)}, u32[]{:S(2)}) collective-permute-start(f32[6,8,128]{2,1,0:T(8,128)S(1)} %pad_maximum_fusion), channel_id=1, source_target_pairs={{0,4},{4,8},{8,12},{12,16},{16,20},{20,24},{24,28},{1,5},{5,9},{9,... | collective-permute-start | bytes 73736 | tf_op jit(solution)/shard_map/ppermute | solution.py:417
  17.6 11.7 %collective-permute-start.1 = (f32[6,8,128]{2,1,0:T(8,128)S(1)}, f32[6,8,128]{2,1,0:T(8,128)S(1)}, u32[]{:S(2)}, u32[]{:S(2)}) collective-permute-start(f32[6,8,128]{2,1,0:T(8,128)S(1)} %pad_maximum_fusion.1), channel_id=1, source_target_pairs={{4,0},{8,4},{12,8},{16,12},{20,16},{24,20},{28,24},{5,1},{9,5},{13... | collective-permute-start | bytes 73736 | tf_op jit(solution)/shard_map/ppermute | solution.py:417
  32.4 18.9 %collective-permute-start.2 = (f32[16,896]{1,0:T(8,128)S(1)}, f32[16,896]{1,0:T(8,128)S(1)}, u32[]{:S(2)}, u32[]{:S(2)}) collective-permute-start(f32[16,896]{1,0:T(8,128)S(1)} %get-tuple-element.17), channel_id=1, source_target_pairs={{0,1},{1,2},{2,3},{4,5},{5,6},{6,7},{8,9},{9,10},{10,11},{12,13},{... | collective-permute-start | bytes 172040 | tf_op jit(solution)/shard_map/ppermute | solution.py:417
  33.7 17.6 %collective-permute-start.3 = (f32[16,896]{1,0:T(8,128)S(1)}, f32[16,896]{1,0:T(8,128)S(1)}, u32[]{:S(2)}, u32[]{:S(2)}) collective-permute-start(f32[16,896]{1,0:T(8,128)S(1)} %get-tuple-element.18), channel_id=1, source_target_pairs={{1,0},{2,1},{3,2},{5,4},{6,5},{7,6},{9,8},{10,9},{11,10},{13,12},{... | collective-permute-start | bytes 172040 | tf_op jit(solution)/shard_map/ppermute | solution.py:417
  69.9 42.1 %all-to-all-start.1 = ((f32[32,96,128]{2,1,0:T(8,128)}), f32[32,96,128]{2,1,0:T(8,128)S(1)}, u32[]{:S(2)}, u32[]{:S(2)}) async-start(f32[32,96,128]{2,1,0:T(8,128)} %get-tuple-element.21.refs_1_), calls=%async_computation.1 | async-start | bytes 3145728 | tf_op jit(solution)/shard_map/all_to_all | solution.py:492
  78.9 5.5 %collective-permute-start.4 = (f32[3,8,128]{2,1,0:T(8,128)S(1)}, f32[3,8,128]{2,1,0:T(8,128)S(1)}, u32[]{:S(2)}, u32[]{:S(2)}) collective-permute-start(f32[3,8,128]{2,1,0:T(8,128)S(1)} %get-tuple-element.23), channel_id=1, source_target_pairs={{0,4},{4,8},{8,12},{12,16},{16,20},{20,24},{24,28},{1,5},{5,9},{9,... | collective-permute-start | bytes 36872 | tf_op jit(solution)/shard_map/ppermute | solution.py:417
  82.5 5.3 %collective-permute-start.5 = (f32[3,8,128]{2,1,0:T(8,128)S(1)}, f32[3,8,128]{2,1,0:T(8,128)S(1)}, u32[]{:S(2)}, u32[]{:S(2)}) collective-permute-start(f32[3,8,128]{2,1,0:T(8,128)S(1)} %get-tuple-element.24), channel_id=1, source_target_pairs={{4,0},{8,4},{12,8},{16,12},{20,16},{24,20},{28,24},{5,1},{9,5},{13... | collective-permute-start | bytes 36872 | tf_op jit(solution)/shard_map/ppermute | solution.py:417
  88.6 12.7 %collective-permute-start.6 = (f32[16,896]{1,0:T(8,128)S(1)}, f32[16,896]{1,0:T(8,128)S(1)}, u32[]{:S(2)}, u32[]{:S(2)}) collective-permute-start(f32[16,896]{1,0:T(8,128)S(1)} %get-tuple-element.28), channel_id=1, source_target_pairs={{0,1},{1,2},{2,3},{4,5},{5,6},{6,7},{8,9},{9,10},{10,11},{12,13},{... | collective-permute-start | bytes 172040 | tf_op jit(solution)/shard_map/ppermute | solution.py:417
  91.8 9.5 %collective-permute-start.7 = (f32[16,896]{1,0:T(8,128)S(1)}, f32[16,896]{1,0:T(8,128)S(1)}, u32[]{:S(2)}, u32[]{:S(2)}) collective-permute-start(f32[16,896]{1,0:T(8,128)S(1)} %get-tuple-element.29), channel_id=1, source_target_pairs={{1,0},{2,1},{3,2},{5,4},{6,5},{7,6},{9,8},{10,9},{11,10},{13,12},{... | collective-permute-start | bytes 172040 | tf_op jit(solution)/shard_map/ppermute | solution.py:417

commit v2 on v1

--- a/solution.py
+++ b/solution.py
@@ -11,6 +11,11 @@
 EDGE = 8
 FLAT = 32
 STRIP = 6 * ITERS
+COST_SEND = 1 << 10
+COST_OWN = 1 << 10
+COST_MIRROR = 15 << 20
+COST_FIRST = 1 << 10
+COST_SMOOTH = 100 << 20
 BOTH = ("atm", "ocn")
 F32 = jnp.float32
 BF16 = jnp.bfloat16
@@ -62,37 +67,47 @@
         return self.target
 
 
-def call(kernel, out_shape, operands, *, late=(), outs=None, flops=0, scratch=(), limit=16):
+def call(
+    kernel, out_shape, operands, *, late=(), plain=(), smem=(), after=(), outs=None, cost=None, scratch=(), aliases={},
+):
     total = sum(x.size * x.dtype.itemsize for x in operands)
     extra = {} if outs is None else {"out_specs": outs}
+    count = len(operands)
+    operands = [*operands, *after]
+    unread = range(count, len(operands))
+    slow = [*late, *plain, *aliases]
     given = [
-        pltpu.with_memory_space_constraint(x, pltpu.HBM) if i in late else x
+        pltpu.with_memory_space_constraint(x, pltpu.HBM) if i in slow else x
         for i, x in enumerate(operands)
     ]
     results = len(jax.tree.leaves(out_shape))
 
     def body(*refs):
-        ends = len(operands), len(operands) + results, len(operands) + results + len(late)
-        inputs, held = list(refs[: ends[0]]), refs[ends[1] : ends[2]]
-        rest = refs[ends[2] :]
+        first, second = len(operands), len(operands) + results
+        inputs, held = list(refs[:count]), refs[second : second + len(late)]
+        rest = refs[second + len(late) :]
         if late:
             sems, rest = rest[0], rest[1:]
             for at, i in enumerate(late):
                 inputs[i] = Late(inputs[i], held[at], sems.at[at])
-        kernel(*inputs, *refs[ends[0] : ends[1]], *rest)
+        kernel(*inputs, *refs[first:second], *rest)
 
     held = [pltpu.VMEM(operands[i].shape, operands[i].dtype) for i in late]
     held += [pltpu.SemaphoreType.DMA((len(late),))] if late else []
+
+    def space(i):
+        if i in unread:
+            return pl.ANY
+        return pltpu.HBM if i in slow else pltpu.SMEM if i in smem else pltpu.VMEM
+
     return pl.pallas_call(
         body,
         out_shape=out_shape,
-        in_specs=[
-            pl.BlockSpec(memory_space=pltpu.HBM if i in late else pltpu.VMEM)
-            for i in range(len(operands))
-        ],
+        in_specs=[pl.BlockSpec(memory_space=space(i)) for i in range(len(operands))],
         scratch_shapes=held + list(scratch),
-        compiler_params=pltpu.CompilerParams(vmem_limit_bytes=limit << 20),
-        cost_estimate=pl.CostEstimate(flops=flops, bytes_accessed=2 * total, transcendentals=0),
+        input_output_aliases=aliases,
+        compiler_params=pltpu.CompilerParams(vmem_limit_bytes=16 << 20),
+        cost_estimate=pl.CostEstimate(flops=(cost or 0) * 1000, bytes_accessed=cost or total, transcendentals=0),
         **extra,
     )(*given)
 
@@ -105,16 +120,18 @@
     return jnp.sum(jnp.where(match, before, 0.0), axis=0, keepdims=True).astype(jnp.int32)
 
 
-def pack_kernel(devices, cap, dest, seg, row, ocean, mask, area, out, staged, out_sems):
-    target = dest.get()[...]
-    slots = devices * cap
+def pack(sizes, half, target, seg, value, ocean, weight, out, staged, out_sems):
+    devices, ocn_count, cap = sizes
+    across = ocn_count // 2
+    owners = devices // 2
+    slots = owners * cap
     count = target.shape[1]
-    chans, segs, width = ocean.target.shape
+    chans, (segs, width) = len(ocean), ocean[0].shape
     stores = []
 
     def send(index, size, values):
         piece = pl.ds(index * cap, size)
-        staged[:, piece, :] = values.reshape(devices, size, width)
+        staged[:, piece, :] = values.reshape(owners, size, width)
         store = pltpu.make_async_copy(
             staged.at[:, piece, :], out.at[:, piece, :], out_sems.at[index]
         )
@@ -122,23 +139,23 @@
         stores.append(store)
 
     position = positions(target, devices)
-    slot = target * cap + position
+    beside = target % ocn_count
+    group = target // ocn_count * across + beside % across
+    group = jnp.where(beside // across == half, group, owners)
+    slot = group * cap + position
     place = one_hot(iota((slots, count), 0) == slot)
-    member = one_hot(iota((segs, count), 0) == seg.get()[...])
+    member = one_hot(iota((segs, count), 0) == seg)
     of_seg = dot(place, member, (1, 1)).astype(BF16)
-    values = ocean.get()
-    for chan, sent in enumerate(exact_dots(of_seg, [values[chan] for chan in range(chans)])):
+    for chan, sent in enumerate(exact_dots(of_seg, ocean)):
         send(chan, cap, sent)
-    sea = dot(of_seg, mask.get()[...].astype(F32).astype(BF16))
-    (reach,) = exact_dots(place, [area.get()[...]])
-    send(chans, cap, reach * sea)
-    line = iota((devices * EDGE, count), 0)
-    tall = line == target * EDGE + (position & (EDGE - 1))
-    flat = line == target * EDGE
+    (reach,) = exact_dots(place, [weight])
+    send(chans, cap, reach)
+    line = iota((owners * EDGE, count), 0)
+    tall = line == group * EDGE + (position & (EDGE - 1))
+    flat = line == group * EDGE
     lane = iota((width, count), 0)
     tall_lane = lane == lax.shift_right_logical(position, EDGE.bit_length() - 1)
     flat_lane = lane == position + FLAT
-    value = row.get()[...]
     coarse, fine = lax.shift_right_logical(value, 5).astype(F32), (value & 31).astype(F32)
     lanes = jnp.concatenate(
         [
@@ -149,8 +166,59 @@
     ).astype(BF16)
     labels = dot(jnp.concatenate([one_hot(tall), one_hot(flat)], axis=1), lanes, (1, 1))
     send(chans + 1, EDGE, labels[:, :width] * 32.0 + labels[:, width:])
+    return stores
+
+
+def send_kernel(ocean, seg, mask, area, dest, row, sent, kept, sems):
+    segs, width = mask.target.shape
+    count = area.target.shape[0]
+    lines = count // width
+    chans = ocean.target.shape[0]
+    values = ocean.get()
+    stores = [
+        pltpu.make_async_copy(
+            values.at[chan], sent.at[pl.ds(chan * segs, segs), :], sems.at[chan]
+        )
+        for chan in range(chans)
+    ]
+    for store in stores:
+        store.start()
+    found = seg.get()[...]
+    member = one_hot(iota((segs, count), 0) == found)
+    sea = dot(member, mask.get()[...].astype(F32).astype(BF16), (0, 0))
+    kept[:count, :] = area.get()[...] * sea
+    flat = [
+        index[:, line * width : (line + 1) * width].astype(F32)
+        for index in (dest.get()[...], found, row.get()[...])
+        for line in range(lines)
+    ]
+    rest = kept.shape[0] - count - len(flat)
+    kept[count:, :] = jnp.concatenate(flat + [jnp.zeros((rest, width), F32)], axis=0)
+    target = sent.at[pl.ds(chans * segs, kept.shape[0]), :]
+    stores.append(pltpu.make_async_copy(kept, target, sems.at[chans]))
+    stores[-1].start()
     for store in stores:
         store.wait()
+
+
+def pack_kernel(sizes, count, chans, half, sent, out, staged, out_sems):
+    given = sent.get() if isinstance(sent, Late) else sent
+    width = given.shape[1]
+    lines = count // width
+    rest = -(-3 * lines // 16) * 16
+    segs = (given.shape[0] - count - rest) // chans
+    first = chans * segs + count
+
+    def vector(index):
+        at = first + index * lines
+        pieces = [given[at + line : at + line + 1, :] for line in range(lines)]
+        return jnp.concatenate(pieces, axis=1).astype(jnp.int32)
+
+    ocean = [given[chan * segs : (chan + 1) * segs, :] for chan in range(chans)]
+    weight = given[chans * segs : first, :]
+    indices = [vector(index) for index in range(3)]
+    for copy in pack(sizes, half[0], *indices, ocean, weight, out, staged, out_sems):
+        copy.wait()
 
 
 def edge_lane(takes, width, high):
@@ -259,8 +327,8 @@
     return beside_rows(body) + east + west
 
 
-def smooth_kernel(cap, before, after, atm, dest, seg, smooth, seg_select, staged, held, sems):
-    chans, rows, width = staged.shape
+def smooth_kernel(cap, before, after, left, right, atm, dest, seg, table, seg_select, held, sems):
+    chans, rows, width = atm.target.shape
     segs, slots = held.shape
     target = dest.get()[...]
     slot = target * cap + positions(target, slots // cap)
@@ -269,12 +337,14 @@
     held[...] = dot(member, place, (1, 1)).astype(BF16)
     stores = [pltpu.make_async_copy(held, seg_select, sems.at[0])]
     stores[0].start()
+    sides = nearest_columns(left, right, width, chans)
     state = atm.get()
+    parts = []
     for chan in range(chans):
         body = jnp.concatenate([before[chan], state[chan], after[chan]], axis=0)
-        staged[chan] = (0.5 * body + 0.125 * beside_body(body))[EDGE : EDGE + rows]
-    stores.append(pltpu.make_async_copy(staged, smooth, sems.at[1]))
-    stores[1].start()
+        side = sides[: body.shape[0], chan * width : (chan + 1) * width]
+        parts.append(split3((0.5 * body + 0.125 * beside_body(body, side))[EDGE : EDGE + rows]))
+    table[...] = jnp.concatenate([p[level] for level in (2, 1, 0) for p in parts], axis=1)
     for store in stores:
         store.wait()
 
@@ -289,34 +359,33 @@
     return dot(jnp.concatenate(split3(edges), axis=0), select, (0, 0))
 
 
-def flux_kernel(cap, incoming, left, right, smooth, out, label_rows, staged, sems):
-    devices, _, width = incoming.shape
-    chans, rows, _ = smooth.target.shape
-    side = 0.125 * nearest_columns(left, right, width, chans)[EDGE : EDGE + rows]
+def flux_kernel(cap, ocn_count, mirrored, half, incoming, table, *rest):
+    out, label_rows, staged, sems = rest[-4:]
+    incoming = incoming if mirrored else incoming.get()
+    owners, _, width = incoming.shape
+    chans = staged.shape[1] // cap
+    rows = table.shape[0]
+    across = ocn_count // 2
+    base = (1 - half[0] if mirrored else half[0]) * across
+    groups = 2
+    each = owners // groups
+    stores = []
     label_rows[...] = incoming[:, (chans + 1) * cap, :]
-    whole = smooth.get()
-    smoothed = jnp.concatenate([whole[chan] for chan in range(chans)], axis=1) + side
-    table = jnp.concatenate(split3(smoothed)[::-1], axis=1)
-    groups = sems.shape[0]
-    each = devices // groups
-    stores = []
     for group in range(groups):
-        owners = slice(group * each, (group + 1) * each)
+        part_of = slice(group * each, (group + 1) * each)
 
         def part(index):
-            piece = incoming[owners, index * cap : (index + 1) * cap, :]
+            piece = incoming[part_of, index * cap : (index + 1) * cap, :]
             return piece.reshape(each * cap, width)
 
-        labels = incoming[owners, (chans + 1) * cap :, :]
+        labels = incoming[part_of, (chans + 1) * cap :, :]
         labels = jnp.concatenate(
             [labels[i, :, j : j + 1] for i in range(each) for j in range(cap // EDGE)], axis=0
         ).astype(jnp.int32)
         select = one_hot(iota((each * cap, rows), 1) == labels)
-        found = dot(select, table)
+        found = dot(select, table[...])
         pieces = [found[:, i * width : (i + 1) * width] for i in range(3 * chans)]
-        air = [
-            (pieces[i] + pieces[chans + i]) + pieces[2 * chans + i] for i in range(chans)
-        ]
+        air = [(pieces[i] + pieces[chans + i]) + pieces[2 * chans + i] for i in range(chans)]
         wind_east = air[1] - part(1)
         wind_north = air[2] - part(2)
         wind_speed = jnp.sqrt(wind_east * wind_east + wind_north * wind_north + 0.5)
@@ -324,26 +393,42 @@
         factor = 1.0 + 0.5 * jnp.tanh(temp_gap / wind_speed)
         common = part(3) * factor * wind_speed
         for index, value in enumerate((0.8 * temp_gap, 0.6 * wind_east, 0.6 * wind_north)):
-            staged[owners, index * cap : (index + 1) * cap, :] = (common * value).reshape(
+            staged[part_of, index * cap : (index + 1) * cap, :] = (common * value).reshape(
                 each, cap, width
             )
-        store = pltpu.make_async_copy(
-            staged.at[pl.ds(group * each, each)],
-            out.at[pl.ds(group * each, each)],
-            sems.at[group],
-        )
-        store.start()
-        stores.append(store)
+        for line in range(group * each // across, (group + 1) * each // across):
+            store = pltpu.make_async_copy(
+                staged.at[pl.ds(line * across, across)],
+                out.at[pl.ds(line * ocn_count + base, across)],
+                sems.at[line],
+            )
+            store.start()
+            stores.append(store)
     for store in stores:
         store.wait()
 
 
-def forced_kernel(cap, label_rows, weighted, atm, forced, top, bottom):
-    devices, _, width = weighted.target.shape
+def forced_kernel(
+    cap, ocn_count, half, own_labels, mirror_labels, weighted, atm, forced, top, bottom, held, sems
+):
+    owners, width = own_labels.shape
+    devices = 2 * owners
     chans, rows, _ = forced.shape
     slots = devices * cap
     log = cap.bit_length() - 1
-    labels = label_rows[...].astype(jnp.int32)
+    across = ocn_count // 2
+    loads = [
+        pltpu.make_async_copy(
+            weighted.at[pl.ds(line * ocn_count + base * across, across)],
+            held.at[pl.ds(side * owners + line * across, across)],
+            sems.at[side * (owners // across) + line],
+        )
+        for side, base in enumerate((half[0], 1 - half[0]))
+        for line in range(owners // across)
+    ]
+    for load in loads:
+        load.start()
+    labels = jnp.concatenate([own_labels[...], mirror_labels[...]], axis=0).astype(jnp.int32)
     spread = one_hot(iota((width, slots), 0) == (iota((width, slots), 1) & (cap - 1)) + FLAT)
     coarse = dot(lax.shift_right_logical(labels, 5).astype(F32).astype(BF16), spread)
     fine = dot((labels & 31).astype(F32).astype(BF16), spread)
@@ -351,9 +436,11 @@
     label = jnp.where(owner == iota((devices, slots), 0), coarse * 32.0 + fine, 0.0)
     label = jnp.sum(label, axis=0, keepdims=True).astype(jnp.int32)
     select = one_hot(iota((rows, slots), 0) == label)
-    sent, state = weighted.get(), atm.get()
+    state = atm.get()
+    for load in loads:
+        load.wait()
     values = [
-        sent[:, chan * cap : (chan + 1) * cap, :].reshape(slots, width) for chan in range(chans)
+        held[:, chan * cap : (chan + 1) * cap, :].reshape(slots, width) for chan in range(chans)
     ]
     for chan, air_sum in enumerate(exact_dots(select, values)):
         result = state[chan] + air_sum if chan == 0 else state[chan] - air_sum
@@ -364,21 +451,43 @@
 
 def diffuse_kernel(
     forced, before, after, diff_own, diff_left, diff_right, diff_before, diff_after, diff,
-    out, diff_strip,
+    out, diff_strip, staged, sems,
 ):
     chans, rows, width = forced.shape
     diff_strip[...] = fill_strip(diff_own, diff_left, diff_right, chans, chans, ITERS - 1)
+    stores = []
     for chan in range(chans):
         body = jnp.concatenate([before[chan], forced[chan], after[chan]], axis=0)
         body_diff = [diff_before[chans + chan], diff.get()[chan], diff_after[chans + chan]]
         body_diff = jnp.concatenate(body_diff, axis=0)
         for _ in range(ITERS):
             body = body + body_diff * (beside_body(body) - 4.0 * body)
-        out[chan] = body[EDGE : EDGE + rows]
-
-
-def sides_kernel(inner, own, left, right, diff_strip, out):
-    chans, rows, width = inner.shape
+        staged[chan] = body[EDGE : EDGE + rows]
+        stores.append(pltpu.make_async_copy(staged.at[chan], out.at[chan], sems.at[chan]))
+        stores[-1].start()
+    for store in stores:
+        store.wait()
+
+
+def finish_kernel(
+    cap, returned, own, left, right, diff_strip, seg_select, inner, ocean_flux, atm_next,
+    flux_staged, staged, sems,
+):
+    devices, _, width = returned.shape
+    chans, rows, _ = staged.shape
+    stores = []
+
+    def send(source, target):
+        stores.append(pltpu.make_async_copy(source, target, sems.at[len(stores)]))
+        stores[-1].start()
+
+    values = [
+        returned[:, chan * cap : (chan + 1) * cap, :].reshape(devices * cap, width)
+        for chan in range(chans)
+    ]
+    for chan, total in enumerate(exact_dots(seg_select.get()[...], values)):
+        flux_staged[chan] = total
+    send(flux_staged, ocean_flux)
     state = fill_strip(own, left, right, 0, chans, ITERS)
     spread = diff_strip[...]
     for _ in range(ITERS):
@@ -389,25 +498,19 @@
     which, lane = iota(shape, 0) % lines, iota(shape, 1)
     place, start = which % STRIP, which // STRIP * width
     low = (place >= ITERS) & (place < 2 * ITERS) & (lane == start + place - ITERS)
-    high = place >= 4 * ITERS
-    high = high & (place < 5 * ITERS) & (lane == start + width + place - 5 * ITERS)
+    high = (place >= 4 * ITERS) & (place < 5 * ITERS)
+    high = high & (lane == start + width + place - 5 * ITERS)
     select = one_hot((which < chans * STRIP) & (low | high))
     edges = dot(jnp.concatenate(split3(state), axis=0), select, (0, 0))
     lane = iota((rows, width), 1)
     outer = (lane < ITERS) | (lane >= width - ITERS)
+    middle = inner.get()
     for chan in range(chans):
         edge = edges[EDGE : EDGE + rows, chan * width : (chan + 1) * width]
-        out[chan] = jnp.where(outer, edge, inner[chan])
-
-
-def sum_kernel(cap, returned, seg_select, out):
-    devices, _, width = returned.shape
-    values = [
-        returned[:, chan * cap : (chan + 1) * cap, :].reshape(devices * cap, width)
-        for chan in range(out.shape[0])
-    ]
-    for chan, total in enumerate(exact_dots(seg_select.get()[...], values)):
-        out[chan] = total
+        staged[chan] = jnp.where(outer, edge, middle[chan])
+        send(staged.at[chan], atm_next.at[chan])
+    for store in stores:
+        store.wait()
 
 
 def shift(axis, low_edge, high_edge):
@@ -435,99 +538,146 @@
     hbm, fast = pltpu.HBM, pl.BlockSpec(memory_space=pltpu.VMEM)
     slow = pl.BlockSpec(memory_space=hbm)
     dest, seg, row = dest.reshape(1, count), seg.reshape(1, count), row.reshape(1, count)
-    packed = (devices, (chans + 1) * cap + EDGE, width)
-    given = (dest, seg, row, ocean, mask, area)
-    out = call(
-        functools.partial(pack_kernel, devices, cap),
-        hbm(packed, F32),
-        given,
-        late=tuple(range(len(given))),
+    across = ocn_count // 2
+    owners = devices // 2
+    half = (lax.axis_index("ocn") // across).astype(jnp.int32).reshape(1)
+    halves = [
+        [i * ocn_count + side * across + j for i in range(atm_count) for j in range(across)]
+        for side in range(2)
+    ]
+    mirror = [(j, (j + across) % ocn_count) for j in range(ocn_count)]
+    sizes = (devices, ocn_count, cap)
+    packed = (owners, (chans + 1) * cap + EDGE, width)
+    lines_sent = chans * segs + count + -(-3 * count // width // 16) * 16
+
+    def exchange(x):
+        return lax.all_to_all(
+            x, BOTH, split_axis=0, concat_axis=0, tiled=True, axis_index_groups=halves
+        )
+
+    sent = call(
+        send_kernel,
+        hbm((lines_sent, width), F32),
+        (ocean, seg, mask, area, dest, row),
+        late=(0, 1, 2, 3, 4, 5),
         outs=slow,
-        scratch=[pltpu.VMEM(packed, F32), pltpu.SemaphoreType.DMA((chans + 2,))],
-        flops=2 * slots * count * (segs + 3 * width) + 6 * slots * segs * chans * width,
-    )
-    incoming = lax.all_to_all(out, BOTH, split_axis=0, concat_axis=0, tiled=True)
-
-    long = -(-(rows + 2 * EDGE) // 128) * 128
-
-    def lines(columns):
-        return shape(-(-columns // EDGE) * EDGE, long)
+        scratch=[
+            pltpu.VMEM((lines_sent - chans * segs, width), F32),
+            pltpu.SemaphoreType.DMA((chans + 1,)),
+        ],
+        cost=COST_SEND,
+    )
+    received = lax.ppermute(sent, "ocn", mirror)
+
+    def packing(sent, late, cost, *ahead):
+        return call(
+            functools.partial(pack_kernel, sizes, count, chans),
+            hbm(packed, F32),
+            (half, sent),
+            smem=(0,),
+            late=late,
+            after=ahead,
+            outs=slow,
+            scratch=[pltpu.VMEM(packed, F32), pltpu.SemaphoreType.DMA((chans + 2,))],
+            cost=cost,
+        )
 
     first = jnp.concatenate([atm[:, :EDGE], diff[:, :EDGE]], axis=0)
     final = jnp.concatenate([atm[:, -EDGE:], diff[:, -EDGE:]], axis=0)
     before, after = shift("atm", first, final)
+    own_packed = packing(sent, (1,), COST_OWN)
+    own_incoming = exchange(own_packed)
+    long = -(-(rows + 2 * EDGE) // 128) * 128
+
+    def lines(columns):
+        return shape(-(-columns // EDGE) * EDGE, long)
+
     low, high, diff_own = call(
         first_columns_kernel,
         (lines(chans * ITERS), lines(chans * ITERS), lines(chans * STRIP)),
         (before, after, atm, diff),
         late=(2, 3),
-        flops=6 * 2 * chans * long * width * 16,
+        after=(own_packed,),
+        cost=COST_FIRST,
     )
     left, right = shift("ocn", low, high)
-    smooth, seg_select = call(
+    mirror_packed = packing(received, (), COST_MIRROR, diff_own)
+    mirror_incoming = exchange(mirror_packed)
+
+    table, seg_select = call(
         functools.partial(smooth_kernel, cap),
-        (hbm((chans, rows, width), F32), hbm((segs, slots), BF16)),
-        (before, after, atm, dest, seg),
-        late=(2, 3, 4),
-        outs=(slow, slow),
-        scratch=[
-            pltpu.VMEM((chans, rows, width), F32),
-            pltpu.VMEM((segs, slots), BF16),
-            pltpu.SemaphoreType.DMA((2,)),
-        ],
-        flops=100 * rows * chans * width,
-    )
-    weighted, label_rows = call(
-        functools.partial(flux_kernel, cap),
-        (hbm((devices, chans * cap, width), F32), shape(devices, width)),
-        (incoming, left, right, smooth),
-        late=(3,),
-        outs=(slow, fast),
-        scratch=[
-            pltpu.VMEM((devices, chans * cap, width), F32),
-            pltpu.SemaphoreType.DMA((4,)),
-        ],
-        flops=100 * slots * width,
-    )
+        (pltpu.VMEM((rows, 3 * chans * width), BF16), hbm((segs, slots), BF16)),
+        (before, after, left, right, atm, dest, seg),
+        late=(4, 5, 6),
+        after=(mirror_packed,),
+        outs=(fast, slow),
+        cost=COST_SMOOTH,
+        scratch=[pltpu.VMEM((segs, slots), BF16), pltpu.SemaphoreType.DMA((1,))],
+    )
+
+    def flux(incoming, mirrored, begun):
+        return call(
+            functools.partial(flux_kernel, cap, ocn_count, mirrored),
+            (
+                hbm((devices, chans * cap, width), F32),
+                shape(owners, width),
+            ),
+            (half, incoming, table, *begun),
+            smem=(0,),
+            late=() if mirrored else (1,),
+            outs=(slow, fast),
+            scratch=[
+                pltpu.VMEM((owners, chans * cap, width), F32),
+                pltpu.SemaphoreType.DMA((atm_count,)),
+            ],
+            aliases={3: 0} if begun else {},
+        )
+
+    begun, own_labels = flux(own_incoming, False, ())
+    weighted, mirror_labels = flux(mirror_incoming, True, (begun,))
     returned = lax.all_to_all(weighted, BOTH, split_axis=0, concat_axis=0, tiled=True)
     forced, top, bottom = call(
-        functools.partial(forced_kernel, cap),
+        functools.partial(forced_kernel, cap, ocn_count),
         (
             pltpu.VMEM((chans, rows, width), F32),
             shape(chans, EDGE, width),
             shape(chans, EDGE, width),
         ),
-        (label_rows, weighted, atm),
-        late=(1, 2),
-        flops=6 * slots * rows * chans * width,
+        (half, own_labels, mirror_labels, weighted, atm),
+        smem=(0,),
+        plain=(3,),
+        late=(4,),
+        scratch=[
+            pltpu.VMEM((devices, chans * cap, width), F32),
+            pltpu.SemaphoreType.DMA((2 * atm_count,)),
+        ],
     )
     forced_before, forced_after = shift("atm", top, bottom)
     forced_low, forced_high, forced_own = call(
         columns_kernel,
         (lines(chans * ITERS), lines(chans * ITERS), lines(chans * STRIP)),
         (forced_before, forced, forced_after),
-        flops=6 * chans * long * width * 16,
     )
     forced_left, forced_right = shift("ocn", forced_low, forced_high)
     inner, diff_strip = call(
         diffuse_kernel,
-        (shape(chans, rows, width), lines(chans * STRIP)),
+        (hbm((chans, rows, width), F32), lines(chans * STRIP)),
         (forced, forced_before, forced_after, diff_own, left, right, before, after, diff),
         late=(8,),
-        flops=100 * chans * rows * width,
-    )
-    atm_next = call(
-        sides_kernel,
-        shape(chans, rows, width),
-        (inner, forced_own, forced_left, forced_right, diff_strip),
-        flops=100 * chans * rows * width,
-    )
-    ocean_flux = call(
-        functools.partial(sum_kernel, cap),
-        shape(chans, segs, width),
-        (returned, seg_select),
-        late=(1,),
-        flops=6 * slots * segs * chans * width,
+        outs=(slow, fast),
+        scratch=[pltpu.VMEM((chans, rows, width), F32), pltpu.SemaphoreType.DMA((chans,))],
+    )
+    ocean_flux, atm_next = call(
+        functools.partial(finish_kernel, cap),
+        (hbm((chans, segs, width), F32), hbm((chans, rows, width), F32)),
+        (returned, forced_own, forced_left, forced_right, diff_strip, seg_select, inner),
+        late=(5, 6),
+        outs=(slow, slow),
+        scratch=[
+            pltpu.VMEM((chans, segs, width), F32),
+            pltpu.VMEM((chans, rows, width), F32),
+            pltpu.SemaphoreType.DMA((1 + chans,)),
+        ],
     )
     return jnp.transpose(atm_next, (1, 0, 2)), jnp.transpose(ocean_flux, (1, 0, 2))
 

time: 117 us -> 111 us (0.949); the launches traced: 115 us -> 110 us
  waiting for transfers between devices: 51.6 us -> 38 us
  starting transfers between devices: 29.8 us -> 35.1 us
  Pallas kernels: 31.7 us -> 33.8 us
  local copies, waits for them, and re-layouts: 0.77 us -> 2.02 us
    ppermute x4, waiting for transfers between devices: 23.2 us -> 7.43 us  [shift(): lax.ppermute(high_edge, axis, forward)]
    all_to_all x1 -> x2, starting transfers between devices: 7.1 us -> 10.8 us  [exchange(): lax.all_to_all(x, BOTH, split_axis=0, concat_axis=0, tiled=True, axis_ind...]
    ppermute x0 -> x1, starting transfers between devices: none -> 3.2 us  [per_device(): received = lax.ppermute(sent, 'ocn', mirror)]
    all_to_all x1, waiting for transfers between devices: 8.39 us -> 10.6 us  [per_device(): lax.all_to_all(weighted, BOTH, split_axis=0, concat_axis=0, tiled=True)]
    pallas_call x9 -> x11, Pallas kernels: 31.7 us -> 33.8 us  [call(): pl.pallas_call(body, out_shape=out_shape, in_specs=[pl.BlockSpec(memory_s...]
    ppermute x0 -> x1, waiting for transfers between devices: none -> 1.84 us  [per_device(): received = lax.ppermute(sent, 'ocn', mirror)]
    all_to_all x1, starting transfers between devices: 4.7 us -> 3.44 us  [per_device(): lax.all_to_all(weighted, BOTH, split_axis=0, concat_axis=0, tiled=True)]
    unnamed x0 -> x6, local copies, waits for them, and re-layouts: none -> 1.26 us
  transfers between devices with their start and end apart: 10 -> 12, of which waited for: 7 -> 8; matrix products, arithmetic and copies ran while one was open for 1% -> 1% of each run, Pallas kernels for 16% -> 23%
where the time goes in v2:
time: 111 us; the launch traced here: 110 us
  waiting for transfers between devices  38 us (34%)
  starting transfers between devices  35.1 us (32%)
  Pallas kernels  33.8 us (30%)
  local copies, waits for them, and re-layouts  2.02 us (2%)
    pallas_call x11, Pallas kernels, call(): pl.pallas_call(body, out_shape=out_shape, in_specs=[pl.BlockSpec(memory_s...  33.8 us
    all_to_all x2, waiting for transfers between devices, exchange(): lax.all_to_all(x, BOTH, split_axis=0, concat_axis=0, tiled=True, axis_ind...  12.1 us
    ppermute x4, starting transfers between devices, shift(): lax.ppermute(high_edge, axis, forward)  11.3 us
    all_to_all x2, starting transfers between devices, exchange(): lax.all_to_all(x, BOTH, split_axis=0, concat_axis=0, tiled=True, axis_ind...  10.8 us
    all_to_all x1, waiting for transfers between devices, per_device(): lax.all_to_all(weighted, BOTH, split_axis=0, concat_axis=0, tiled=True)  10.6 us
    ppermute x4, waiting for transfers between devices, shift(): lax.ppermute(high_edge, axis, forward)  7.43 us
    ppermute x4, starting transfers between devices, shift(): lax.ppermute(low_edge, axis, backward)  6.43 us
    ppermute x4, waiting for transfers between devices, shift(): lax.ppermute(low_edge, axis, backward)  6.04 us
  transfers between devices with their start and end apart: 12, of which 8 were waited for; matrix products, arithmetic and copies ran while one was open for 1% of the time, Pallas kernels for 23%

profile of v2, /device:TPU:1, one launch (start us, length us, event | category | flops | bytes accessed | tf_op | source)
XLA Modules:
  0.0 110.0 jit_solution(2372562074940521265)
XLA Ops:
  0.6 2.2 %shard_map.95.refs_1_ = f32[1296,128]{1,0:T(8,128)} custom-call(f32[3,256,128]{2,1,0:T(8,128)} %bitcast.16, s32[1,512]{1,0:T(1,128)} %bitcast.18, s32[256,128]{1,0:T(8,128)} %refs_2_.1, f32[512,128]{1,0:T(8,128)} %refs_3_.1, s32[1,512]{1,0:T(1,128)} %bitcast.20, s32[1,512]{1,0:T(1,128)} %bitcast.17), custom_call_target="tpu_custom_call" | custom-call | flops 1024000 | bytes 1024 | tf_op jit(solution)/shard_map/pallas_call | solution.py:103
  2.8 3.2 %collective-permute-start = (f32[1296,128]{1,0:T(8,128)}, f32[1296,128]{1,0:T(8,128)S(1)}, u32[]{:S(2)}, u32[]{:S(2)}) collective-permute-start(f32[1296,128]{1,0:T(8,128)} %shard_map.95.refs_1_), channel_id=1, source_target_pairs={{0,2},{1,3},{2,0},{3,1},{4,6},{5,7},{6,4},{7,5},{8,10},{9,11},{10,... | collective-permute-start | bytes 1990664 | tf_op jit(solution)/shard_map/ppermute | solution.py:570
  6.0 3.3 %shard_map.96.refs_4_ = f32[16,136,128]{2,1,0:T(8,128)} custom-call(s32[1]{0:T(128)} %bitcast.refs_0_, f32[1296,128]{1,0:T(8,128)} %shard_map.95.refs_1_), custom_call_target="tpu_custom_call" | custom-call | flops 1024000 | bytes 1024 | tf_op jit(solution)/shard_map/pallas_call | solution.py:103
  9.3 5.9 %all-to-all-start.1 = ((f32[16,136,128]{2,1,0:T(8,128)}), f32[16,136,128]{2,1,0:T(8,128)S(1)}, u32[]{:S(2)}, u32[]{:S(2)}) async-start(f32[16,136,128]{2,1,0:T(8,128)} %shard_map.96.refs_4_), calls=%async_computation.1 | async-start | bytes 2228224 | tf_op jit(solution)/shard_map/all_to_all | solution.py:554
  15.9 3.5 %collective-permute-start.1 = (f32[6,8,128]{2,1,0:T(8,128)S(1)}, f32[6,8,128]{2,1,0:T(8,128)S(1)}, u32[]{:S(2)}, u32[]{:S(2)}) collective-permute-start(f32[6,8,128]{2,1,0:T(8,128)S(1)} %pad_maximum_fusion), channel_id=1, source_target_pairs={{0,4},{4,8},{8,12},{12,16},{16,20},{20,24},{24,28},{1,5},{5,9},{9,... | collective-permute-start | bytes 73736 | tf_op jit(solution)/shard_map/ppermute | solution.py:520
  21.4 3.8 %collective-permute-done.1.refs_0_.refs_6_ = f32[6,8,128]{2,1,0:T(8,128)S(1)} collective-permute-done((f32[6,8,128]{2,1,0:T(8,128)S(1)}, f32[6,8,128]{2,1,0:T(8,128)S(1)}, u32[]{:S(2)}, u32[]{:S(2)}) %collective-permute-start.1) | collective-permute-done | bytes 24608 | tf_op jit(solution)/shard_map/ppermute | solution.py:520
  25.2 2.4 %collective-permute-done.2.refs_1_.refs_7_ = f32[6,8,128]{2,1,0:T(8,128)S(1)} collective-permute-done((f32[6,8,128]{2,1,0:T(8,128)S(1)}, f32[6,8,128]{2,1,0:T(8,128)S(1)}, u32[]{:S(2)}, u32[]{:S(2)}) %collective-permute-start.2) | collective-permute-done | bytes 24608 | tf_op jit(solution)/shard_map/ppermute | solution.py:520
  27.6 3.1 %shard_map.97 = (f32[16,896]{1,0:T(8,128)S(1)}, f32[16,896]{1,0:T(8,128)S(1)}, f32[56,896]{1,0:T(8,128)S(1)}) custom-call(f32[6,8,128]{2,1,0:T(8,128)S(1)} %collective-permute-done.1.refs_0_.refs_6_, f32[6,8,128]{2,1,0:T(8,128)S(1)} %collective-permute-done.2.refs_1_.refs_7_, f32[3,864,128]{2,1,0:T(8,128)} %bitcast.10, f32[3,864,128]{2,1,0:T(8,128)} %bitcast.14, ...), custom_call_target="tpu_custom_call" | custom-call | flops 1024000 | bytes 1024 | tf_op jit(solution)/shard_map/pallas_call | solution.py:103
  35.1 2.2 %shard_map.98.refs_7_ = f32[16,136,128]{2,1,0:T(8,128)} custom-call(s32[1]{0:T(128)} %bitcast.refs_0_, f32[1296,128]{1,0:T(8,128)S(1)} %collective-permute-done.refs_1_, f32[56,896]{1,0:T(8,128)S(1)} %get-tuple-element.21.refs_2_.refs_3_), custom_call_target="tpu_custom_call" | custom-call | flops 15728640000 | bytes 15728640 | tf_op jit(solution)/shard_map/pallas_call | solution.py:103
  37.3 5.3 %all-to-all-done.1.refs_1_ = f32[16,136,128]{2,1,0:T(8,128)S(1)} async-done(((f32[16,136,128]{2,1,0:T(8,128)}), f32[16,136,128]{2,1,0:T(8,128)S(1)}, u32[]{:S(2)}, u32[]{:S(2)}) %all-to-all-start.1) | async-done | bytes 1114144 | tf_op jit(solution)/shard_map/all_to_all | solution.py:554
  42.6 4.9 %all-to-all-start = ((f32[16,136,128]{2,1,0:T(8,128)}), f32[16,136,128]{2,1,0:T(8,128)S(1)}, u32[]{:S(2)}, u32[]{:S(2)}) async-start(f32[16,136,128]{2,1,0:T(8,128)} %shard_map.98.refs_7_), calls=%async_computation | async-start | bytes 2228224 | tf_op jit(solution)/shard_map/all_to_all | solution.py:554
  48.8 3.2 %shard_map.99 = (bf16[864,1152]{1,0:T(8,128)(2,1)S(1)}, bf16[256,1024]{1,0:T(8,128)(2,1)}) custom-call(f32[6,8,128]{2,1,0:T(8,128)S(1)} %collective-permute-done.1.refs_0_.refs_6_, f32[6,8,128]{2,1,0:T(8,128)S(1)} %collective-permute-done.2.refs_1_.refs_7_, f32[16,896]{1,0:T(8,128)S(1)} %collective-permute-done.3.refs_2_.refs_4_, ...), custom_call_target="tpu_custom_call" | custom-call | flops 104857600000 | bytes 104857600 | tf_op jit(solution)/shard_map/pallas_call | solution.py:103
  52.0 3.9 %shard_map.100 = (f32[32,96,128]{2,1,0:T(8,128)}, f32[16,128]{1,0:T(8,128)S(1)}) custom-call(s32[1]{0:T(128)} %bitcast.refs_0_, f32[16,136,128]{2,1,0:T(8,128)} %copy-done.2, bf16[864,1152]{1,0:T(8,128)(2,1)S(1)} %get-tuple-element.24.refs_2_), custom_call_target="tpu_custom_call" | custom-call | bytes 3104772 | tf_op jit(solution)/shard_map/pallas_call | solution.py:103
  55.9 6.8 %all-to-all-done.refs_1_ = f32[16,136,128]{2,1,0:T(8,128)S(1)} async-done(((f32[16,136,128]{2,1,0:T(8,128)}), f32[16,136,128]{2,1,0:T(8,128)S(1)}, u32[]{:S(2)}, u32[]{:S(2)}) %all-to-all-start) | async-done | bytes 1114144 | tf_op jit(solution)/shard_map/all_to_all | solution.py:554
  62.7 2.7 %shard_map.101 = (f32[32,96,128]{2,1,0:T(8,128)}, f32[16,128]{1,0:T(8,128)S(1)}) custom-call(s32[1]{0:T(128)} %bitcast.refs_0_, f32[16,136,128]{2,1,0:T(8,128)S(1)} %all-to-all-done.refs_1_, bf16[864,1152]{1,0:T(8,128)(2,1)S(1)} %get-tuple-element.24.refs_2_, f32[32,96,128]{2,1,0:T(8,128)} %get-tuple-element.25.refs_3_), custom_call_target="tpu_custom_call", output_to_operand_aliasing={{0}: (3, {})} | custom-call | bytes 4677636 | tf_op jit(solution)/shard_map/pallas_call | solution.py:103
  65.4 3.4 %all-to-all-start.2 = ((f32[32,96,128]{2,1,0:T(8,128)}), f32[32,96,128]{2,1,0:T(8,128)S(1)}, u32[]{:S(2)}, u32[]{:S(2)}) async-start(f32[32,96,128]{2,1,0:T(8,128)} %get-tuple-element.26.refs_3_), calls=%async_computation.2 | async-start | bytes 3145728 | tf_op jit(solution)/shard_map/all_to_all | solution.py:638
  68.8 4.6 %shard_map.102 = (f32[3,864,128]{2,1,0:T(8,128)S(1)}, f32[3,8,128]{2,1,0:T(8,128)S(1)}, f32[3,8,128]{2,1,0:T(8,128)S(1)}) custom-call(s32[1]{0:T(128)} %bitcast.refs_0_, f32[16,128]{1,0:T(8,128)S(1)} %get-tuple-element.27.refs_1_, f32[16,128]{1,0:T(8,128)S(1)} %get-tuple-element.28.refs_2_, f32[32,96,128]{2,1,0:T(8,128)} %get-tuple-element.26.refs_3_, ...), custom_call_target="tpu_custom_call" | custom-call | bytes 2916356 | tf_op jit(solution)/shard_map/pallas_call | solution.py:103
  73.4 3.5 %collective-permute-start.5 = (f32[3,8,128]{2,1,0:T(8,128)S(1)}, f32[3,8,128]{2,1,0:T(8,128)S(1)}, u32[]{:S(2)}, u32[]{:S(2)}) collective-permute-start(f32[3,8,128]{2,1,0:T(8,128)S(1)} %get-tuple-element.29), channel_id=1, source_target_pairs={{0,4},{4,8},{8,12},{12,16},{16,20},{20,24},{24,28},{1,5},{5,9},{9,... | collective-permute-start | bytes 36872 | tf_op jit(solution)/shard_map/ppermute | solution.py:520
  78.9 3.6 %collective-permute-done.6.refs_2_ = f32[3,8,128]{2,1,0:T(8,128)S(1)} collective-permute-done((f32[3,8,128]{2,1,0:T(8,128)S(1)}, f32[3,8,128]{2,1,0:T(8,128)S(1)}, u32[]{:S(2)}, u32[]{:S(2)}) %collective-permute-start.6) | collective-permute-done | bytes 12320 | tf_op jit(solution)/shard_map/ppermute | solution.py:520
  83.3 2.9 %collective-permute-start.7 = (f32[16,896]{1,0:T(8,128)S(1)}, f32[16,896]{1,0:T(8,128)S(1)}, u32[]{:S(2)}, u32[]{:S(2)}) collective-permute-start(f32[16,896]{1,0:T(8,128)S(1)} %get-tuple-element.33), channel_id=1, source_target_pairs={{0,1},{1,2},{2,3},{4,5},{5,6},{6,7},{8,9},{9,10},{10,11},{12,13},{... | collective-permute-start | bytes 172040 | tf_op jit(solution)/shard_map/ppermute | solution.py:520
  87.6 4.3 %shard_map.104 = (f32[3,864,128]{2,1,0:T(8,128)}, f32[56,896]{1,0:T(8,128)S(1)}) custom-call(f32[3,864,128]{2,1,0:T(8,128)S(1)} %get-tuple-element.30.refs_1_.refs_0_, f32[3,8,128]{2,1,0:T(8,128)S(1)} %collective-permute-done.5.refs_0_.refs_1_, f32[3,8,128]{2,1,0:T(8,128)S(1)} %collective-permute-done.6.refs_2_, ...), custom_call_target="tpu_custom_call" | custom-call | bytes 3043328 | tf_op jit(solution)/shard_map/pallas_call | solution.py:103
  91.9 3.7 %collective-permute-done.7.refs_2_ = f32[16,896]{1,0:T(8,128)S(1)} collective-permute-done((f32[16,896]{1,0:T(8,128)S(1)}, f32[16,896]{1,0:T(8,128)S(1)}, u32[]{:S(2)}, u32[]{:S(2)}) %collective-permute-start.7) | collective-permute-done | bytes 57376 | tf_op jit(solution)/shard_map/ppermute | solution.py:520
  95.6 10.6 %all-to-all-done.2.refs_0_ = f32[32,96,128]{2,1,0:T(8,128)S(1)} async-done(((f32[32,96,128]{2,1,0:T(8,128)}), f32[32,96,128]{2,1,0:T(8,128)S(1)}, u32[]{:S(2)}, u32[]{:S(2)}) %all-to-all-start.2) | async-done | bytes 1572896 | tf_op jit(solution)/shard_map/all_to_all | solution.py:638
  106.2 3.7 %shard_map.105 = (f32[3,256,128]{2,1,0:T(8,128)}, f32[3,864,128]{2,1,0:T(8,128)}) custom-call(f32[32,96,128]{2,1,0:T(8,128)S(1)} %all-to-all-done.2.refs_0_, f32[56,896]{1,0:T(8,128)S(1)} %get-tuple-element.32.refs_1_, f32[16,896]{1,0:T(8,128)S(1)} %collective-permute-done.7.refs_2_, f32[16,896]{1,0:T(8,128)S(1)} %collective-permute-done.8.refs_3_, ...), custom_call_target="tpu_custom_call" | custom-call | bytes 3940352 | tf_op jit(solution)/shard_map/pallas_call | solution.py:103
  (20 shorter events, 12.4 us)
Async XLA Ops:
  2.8 32.3 %collective-permute-start = (f32[1296,128]{1,0:T(8,128)}, f32[1296,128]{1,0:T(8,128)S(1)}, u32[]{:S(2)}, u32[]{:S(2)}) collective-permute-start(f32[1296,128]{1,0:T(8,128)} %shard_map.95.refs_1_), channel_id=1, source_target_pairs={{0,2},{1,3},{2,0},{3,1},{4,6},{5,7},{6,4},{7,5},{8,10},{9,11},{10,... | collective-permute-start | bytes 1990664 | tf_op jit(solution)/shard_map/ppermute | solution.py:570
  9.3 18.3 %copy-start = (f32[16,136,128]{2,1,0:T(8,128)S(1)}, f32[16,136,128]{2,1,0:T(8,128)}, u32[]{:S(2)}) copy-start(f32[16,136,128]{2,1,0:T(8,128)} %shard_map.96.refs_4_) | copy-start | bytes 3342340
  9.3 33.3 %all-to-all-start.1 = ((f32[16,136,128]{2,1,0:T(8,128)}), f32[16,136,128]{2,1,0:T(8,128)S(1)}, u32[]{:S(2)}, u32[]{:S(2)}) async-start(f32[16,136,128]{2,1,0:T(8,128)} %shard_map.96.refs_4_), calls=%async_computation.1 | async-start | bytes 2228224 | tf_op jit(solution)/shard_map/all_to_all | solution.py:554
  15.9 9.2 %collective-permute-start.1 = (f32[6,8,128]{2,1,0:T(8,128)S(1)}, f32[6,8,128]{2,1,0:T(8,128)S(1)}, u32[]{:S(2)}, u32[]{:S(2)}) collective-permute-start(f32[6,8,128]{2,1,0:T(8,128)S(1)} %pad_maximum_fusion), channel_id=1, source_target_pairs={{0,4},{4,8},{8,12},{12,16},{16,20},{20,24},{24,28},{1,5},{5,9},{9,... | collective-permute-start | bytes 73736 | tf_op jit(solution)/shard_map/ppermute | solution.py:520
  19.5 8.1 %collective-permute-start.2 = (f32[6,8,128]{2,1,0:T(8,128)S(1)}, f32[6,8,128]{2,1,0:T(8,128)S(1)}, u32[]{:S(2)}, u32[]{:S(2)}) collective-permute-start(f32[6,8,128]{2,1,0:T(8,128)S(1)} %pad_maximum_fusion.1), channel_id=1, source_target_pairs={{4,0},{8,4},{12,8},{16,12},{20,16},{24,20},{28,24},{5,1},{9,5},{13... | collective-permute-start | bytes 73736 | tf_op jit(solution)/shard_map/ppermute | solution.py:520
  30.7 16.9 %collective-permute-start.3 = (f32[16,896]{1,0:T(8,128)S(1)}, f32[16,896]{1,0:T(8,128)S(1)}, u32[]{:S(2)}, u32[]{:S(2)}) collective-permute-start(f32[16,896]{1,0:T(8,128)S(1)} %get-tuple-element.22), channel_id=1, source_target_pairs={{0,1},{1,2},{2,3},{4,5},{5,6},{6,7},{8,9},{9,10},{10,11},{12,13},{... | collective-permute-start | bytes 172040 | tf_op jit(solution)/shard_map/ppermute | solution.py:520
  32.0 15.6 %collective-permute-start.4 = (f32[16,896]{1,0:T(8,128)S(1)}, f32[16,896]{1,0:T(8,128)S(1)}, u32[]{:S(2)}, u32[]{:S(2)}) collective-permute-start(f32[16,896]{1,0:T(8,128)S(1)} %get-tuple-element.23), channel_id=1, source_target_pairs={{1,0},{2,1},{3,2},{5,4},{6,5},{7,6},{9,8},{10,9},{11,10},{13,12},{... | collective-permute-start | bytes 172040 | tf_op jit(solution)/shard_map/ppermute | solution.py:520
  42.6 4.9 %copy-start.2 = (f32[16,136,128]{2,1,0:T(8,128)}, f32[16,136,128]{2,1,0:T(8,128)S(1)}, u32[]{:S(2)}) copy-start(f32[16,136,128]{2,1,0:T(8,128)S(1)} %all-to-all-done.1.refs_1_) | copy-start | bytes 3342340
  42.6 20.1 %all-to-all-start = ((f32[16,136,128]{2,1,0:T(8,128)}), f32[16,136,128]{2,1,0:T(8,128)S(1)}, u32[]{:S(2)}, u32[]{:S(2)}) async-start(f32[16,136,128]{2,1,0:T(8,128)} %shard_map.98.refs_7_), calls=%async_computation | async-start | bytes 2228224 | tf_op jit(solution)/shard_map/all_to_all | solution.py:554
  47.6 1.3 %copy-start.1 = (f32[16,136,128]{2,1,0:T(8,128)S(1)}, f32[16,136,128]{2,1,0:T(8,128)}, u32[]{:S(2)}) copy-start(f32[16,136,128]{2,1,0:T(8,128)} %shard_map.98.refs_7_) | copy-start | bytes 3342340
  65.4 40.8 %all-to-all-start.2 = ((f32[32,96,128]{2,1,0:T(8,128)}), f32[32,96,128]{2,1,0:T(8,128)S(1)}, u32[]{:S(2)}, u32[]{:S(2)}) async-start(f32[32,96,128]{2,1,0:T(8,128)} %get-tuple-element.26.refs_3_), calls=%async_computation.2 | async-start | bytes 3145728 | tf_op jit(solution)/shard_map/all_to_all | solution.py:638
  73.4 5.5 %collective-permute-start.5 = (f32[3,8,128]{2,1,0:T(8,128)S(1)}, f32[3,8,128]{2,1,0:T(8,128)S(1)}, u32[]{:S(2)}, u32[]{:S(2)}) collective-permute-start(f32[3,8,128]{2,1,0:T(8,128)S(1)} %get-tuple-element.29), channel_id=1, source_target_pairs={{0,4},{4,8},{8,12},{12,16},{16,20},{20,24},{24,28},{1,5},{5,9},{9,... | collective-permute-start | bytes 36872 | tf_op jit(solution)/shard_map/ppermute | solution.py:520
  77.0 5.6 %collective-permute-start.6 = (f32[3,8,128]{2,1,0:T(8,128)S(1)}, f32[3,8,128]{2,1,0:T(8,128)S(1)}, u32[]{:S(2)}, u32[]{:S(2)}) collective-permute-start(f32[3,8,128]{2,1,0:T(8,128)S(1)} %get-tuple-element.31), channel_id=1, source_target_pairs={{4,0},{8,4},{12,8},{16,12},{20,16},{24,20},{28,24},{5,1},{9,5},{13... | collective-permute-start | bytes 36872 | tf_op jit(solution)/shard_map/ppermute | solution.py:520
  83.3 12.2 %collective-permute-start.7 = (f32[16,896]{1,0:T(8,128)S(1)}, f32[16,896]{1,0:T(8,128)S(1)}, u32[]{:S(2)}, u32[]{:S(2)}) collective-permute-start(f32[16,896]{1,0:T(8,128)S(1)} %get-tuple-element.33), channel_id=1, source_target_pairs={{0,1},{1,2},{2,3},{4,5},{5,6},{6,7},{8,9},{9,10},{10,11},{12,13},{... | collective-permute-start | bytes 172040 | tf_op jit(solution)/shard_map/ppermute | solution.py:520
  86.3 9.3 %collective-permute-start.8 = (f32[16,896]{1,0:T(8,128)S(1)}, f32[16,896]{1,0:T(8,128)S(1)}, u32[]{:S(2)}, u32[]{:S(2)}) collective-permute-start(f32[16,896]{1,0:T(8,128)S(1)} %get-tuple-element.34), channel_id=1, source_target_pairs={{1,0},{2,1},{3,2},{5,4},{6,5},{7,6},{9,8},{10,9},{11,10},{13,12},{... | collective-permute-start | bytes 172040 | tf_op jit(solution)/shard_map/ppermute | solution.py:520

commit v3 on v2

--- a/solution.py
+++ b/solution.py
@@ -13,7 +13,7 @@
 STRIP = 6 * ITERS
 COST_SEND = 1 << 10
 COST_OWN = 1 << 10
-COST_MIRROR = 15 << 20
+COST_MIRROR = 16 << 20
 COST_FIRST = 1 << 10
 COST_SMOOTH = 100 << 20
 BOTH = ("atm", "ocn")
@@ -169,53 +169,42 @@
     return stores
 
 
-def send_kernel(ocean, seg, mask, area, dest, row, sent, kept, sems):
+def send_kernel(seg, mask, area, dest, row, ocean, sent):
     segs, width = mask.target.shape
     count = area.target.shape[0]
     lines = count // width
     chans = ocean.target.shape[0]
-    values = ocean.get()
-    stores = [
-        pltpu.make_async_copy(
-            values.at[chan], sent.at[pl.ds(chan * segs, segs), :], sems.at[chan]
-        )
-        for chan in range(chans)
-    ]
-    for store in stores:
-        store.start()
+    first = chans * segs
     found = seg.get()[...]
     member = one_hot(iota((segs, count), 0) == found)
     sea = dot(member, mask.get()[...].astype(F32).astype(BF16), (0, 0))
-    kept[:count, :] = area.get()[...] * sea
+    sent[first : first + count, :] = area.get()[...] * sea
     flat = [
         index[:, line * width : (line + 1) * width].astype(F32)
         for index in (dest.get()[...], found, row.get()[...])
         for line in range(lines)
     ]
-    rest = kept.shape[0] - count - len(flat)
-    kept[count:, :] = jnp.concatenate(flat + [jnp.zeros((rest, width), F32)], axis=0)
-    target = sent.at[pl.ds(chans * segs, kept.shape[0]), :]
-    stores.append(pltpu.make_async_copy(kept, target, sems.at[chans]))
-    stores[-1].start()
-    for store in stores:
-        store.wait()
+    rest = sent.shape[0] - first - count - len(flat)
+    sent[first + count :, :] = jnp.concatenate(flat + [jnp.zeros((rest, width), F32)], axis=0)
+    values = ocean.get()
+    for chan in range(chans):
+        sent[chan * segs : (chan + 1) * segs, :] = values[chan]
 
 
 def pack_kernel(sizes, count, chans, half, sent, out, staged, out_sems):
-    given = sent.get() if isinstance(sent, Late) else sent
-    width = given.shape[1]
+    width = sent.shape[1]
     lines = count // width
     rest = -(-3 * lines // 16) * 16
-    segs = (given.shape[0] - count - rest) // chans
+    segs = (sent.shape[0] - count - rest) // chans
     first = chans * segs + count
 
     def vector(index):
         at = first + index * lines
-        pieces = [given[at + line : at + line + 1, :] for line in range(lines)]
+        pieces = [sent[at + line : at + line + 1, :] for line in range(lines)]
         return jnp.concatenate(pieces, axis=1).astype(jnp.int32)
 
-    ocean = [given[chan * segs : (chan + 1) * segs, :] for chan in range(chans)]
-    weight = given[chans * segs : first, :]
+    ocean = [sent[chan * segs : (chan + 1) * segs, :] for chan in range(chans)]
+    weight = sent[chans * segs : first, :]
     indices = [vector(index) for index in range(3)]
     for copy in pack(sizes, half[0], *indices, ocean, weight, out, staged, out_sems):
         copy.wait()
@@ -557,25 +546,19 @@
 
     sent = call(
         send_kernel,
-        hbm((lines_sent, width), F32),
-        (ocean, seg, mask, area, dest, row),
+        shape(lines_sent, width),
+        (seg, mask, area, dest, row, ocean),
         late=(0, 1, 2, 3, 4, 5),
-        outs=slow,
-        scratch=[
-            pltpu.VMEM((lines_sent - chans * segs, width), F32),
-            pltpu.SemaphoreType.DMA((chans + 1,)),
-        ],
         cost=COST_SEND,
     )
     received = lax.ppermute(sent, "ocn", mirror)
 
-    def packing(sent, late, cost, *ahead):
+    def packing(sent, cost, *ahead):
         return call(
             functools.partial(pack_kernel, sizes, count, chans),
             hbm(packed, F32),
             (half, sent),
             smem=(0,),
-            late=late,
             after=ahead,
             outs=slow,
             scratch=[pltpu.VMEM(packed, F32), pltpu.SemaphoreType.DMA((chans + 2,))],
@@ -585,7 +568,7 @@
     first = jnp.concatenate([atm[:, :EDGE], diff[:, :EDGE]], axis=0)
     final = jnp.concatenate([atm[:, -EDGE:], diff[:, -EDGE:]], axis=0)
     before, after = shift("atm", first, final)
-    own_packed = packing(sent, (1,), COST_OWN)
+    own_packed = packing(sent, COST_OWN)
     own_incoming = exchange(own_packed)
     long = -(-(rows + 2 * EDGE) // 128) * 128
 
@@ -601,7 +584,7 @@
         cost=COST_FIRST,
     )
     left, right = shift("ocn", low, high)
-    mirror_packed = packing(received, (), COST_MIRROR, diff_own)
+    mirror_packed = packing(received, COST_MIRROR, diff_own)
     mirror_incoming = exchange(mirror_packed)
 
     table, seg_select = call(

time: 111 us -> 109 us (0.982)
  Pallas kernels: 33.8 us -> 31.8 us
    pallas_call x11, Pallas kernels: 33.8 us -> 31.8 us  [call(): pl.pallas_call(body, out_shape=out_shape, in_specs=[pl.BlockSpec(memory_s...]
  transfers between devices with their start and end apart: 12 -> 12, of which waited for: 8 -> 8; matrix products, arithmetic and copies ran while one was open for 1% -> 1% of each run, Pallas kernels for 23% -> 22%
where the time goes in v3:
time: 109 us; the launch traced here: 108 us
  waiting for transfers between devices  38.2 us (35%)
  starting transfers between devices  35.1 us (32%)
  Pallas kernels  31.8 us (29%)
  local copies, waits for them, and re-layouts  2.02 us (2%)
    pallas_call x11, Pallas kernels, call(): pl.pallas_call(body, out_shape=out_shape, in_specs=[pl.BlockSpec(memory_s...  31.8 us
    ppermute x4, starting transfers between devices, shift(): lax.ppermute(high_edge, axis, forward)  11.3 us
    all_to_all x2, waiting for transfers between devices, exchange(): lax.all_to_all(x, BOTH, split_axis=0, concat_axis=0, tiled=True, axis_ind...  11.2 us
    all_to_all x2, starting transfers between devices, exchange(): lax.all_to_all(x, BOTH, split_axis=0, concat_axis=0, tiled=True, axis_ind...  10.8 us
    all_to_all x1, waiting for transfers between devices, per_device(): lax.all_to_all(weighted, BOTH, split_axis=0, concat_axis=0, tiled=True)  10.6 us
    ppermute x4, waiting for transfers between devices, shift(): lax.ppermute(high_edge, axis, forward)  7.63 us
    ppermute x4, waiting for transfers between devices, shift(): lax.ppermute(low_edge, axis, backward)  6.44 us
    ppermute x4, starting transfers between devices, shift(): lax.ppermute(low_edge, axis, backward)  6.43 us
  transfers between devices with their start and end apart: 12, of which 8 were waited for; matrix products, arithmetic and copies ran while one was open for 1% of the time, Pallas kernels for 22%

profile of v3, /device:TPU:1, one launch (start us, length us, event | category | flops | bytes accessed | tf_op | source)
XLA Modules:
  0.0 108.1 jit_solution(2813051704001734044)
XLA Ops:
  1.9 3.2 %collective-permute-start = (f32[1296,128]{1,0:T(8,128)S(1)}, f32[1296,128]{1,0:T(8,128)S(1)}, u32[]{:S(2)}, u32[]{:S(2)}) collective-permute-start(f32[1296,128]{1,0:T(8,128)S(1)} %shard_map.95.refs_1_), channel_id=1, source_target_pairs={{0,2},{1,3},{2,0},{3,1},{4,6},{5,7},{6,4},{7,5},{8,10},{9,11},{10,... | collective-permute-start | bytes 1990664 | tf_op jit(solution)/shard_map/ppermute | solution.py:554
  5.1 2.1 %shard_map.96.refs_4_ = f32[16,136,128]{2,1,0:T(8,128)} custom-call(s32[1]{0:T(128)} %bitcast.refs_0_, f32[1296,128]{1,0:T(8,128)S(1)} %shard_map.95.refs_1_), custom_call_target="tpu_custom_call" | custom-call | flops 1024000 | bytes 1024 | tf_op jit(solution)/shard_map/pallas_call | solution.py:103
  7.3 5.8 %all-to-all-start.1 = ((f32[16,136,128]{2,1,0:T(8,128)}), f32[16,136,128]{2,1,0:T(8,128)}, u32[]{:S(2)}, u32[]{:S(2)}) async-start(f32[16,136,128]{2,1,0:T(8,128)} %shard_map.96.refs_4_), calls=%async_computation.1 | async-start | bytes 2228224 | tf_op jit(solution)/shard_map/all_to_all | solution.py:543
  13.9 3.5 %collective-permute-start.1 = (f32[6,8,128]{2,1,0:T(8,128)S(1)}, f32[6,8,128]{2,1,0:T(8,128)S(1)}, u32[]{:S(2)}, u32[]{:S(2)}) collective-permute-start(f32[6,8,128]{2,1,0:T(8,128)S(1)} %pad_maximum_fusion), channel_id=1, source_target_pairs={{0,4},{4,8},{8,12},{12,16},{16,20},{20,24},{24,28},{1,5},{5,9},{9,... | collective-permute-start | bytes 73736 | tf_op jit(solution)/shard_map/ppermute | solution.py:509
  19.4 4.0 %collective-permute-done.1.refs_0_.refs_6_ = f32[6,8,128]{2,1,0:T(8,128)S(1)} collective-permute-done((f32[6,8,128]{2,1,0:T(8,128)S(1)}, f32[6,8,128]{2,1,0:T(8,128)S(1)}, u32[]{:S(2)}, u32[]{:S(2)}) %collective-permute-start.1) | collective-permute-done | bytes 24608 | tf_op jit(solution)/shard_map/ppermute | solution.py:509
  23.3 2.8 %collective-permute-done.2.refs_1_.refs_7_ = f32[6,8,128]{2,1,0:T(8,128)S(1)} collective-permute-done((f32[6,8,128]{2,1,0:T(8,128)S(1)}, f32[6,8,128]{2,1,0:T(8,128)S(1)}, u32[]{:S(2)}, u32[]{:S(2)}) %collective-permute-start.2) | collective-permute-done | bytes 24608 | tf_op jit(solution)/shard_map/ppermute | solution.py:509
  26.1 3.1 %shard_map.97 = (f32[16,896]{1,0:T(8,128)S(1)}, f32[16,896]{1,0:T(8,128)S(1)}, f32[56,896]{1,0:T(8,128)S(1)}) custom-call(f32[6,8,128]{2,1,0:T(8,128)S(1)} %collective-permute-done.1.refs_0_.refs_6_, f32[6,8,128]{2,1,0:T(8,128)S(1)} %collective-permute-done.2.refs_1_.refs_7_, f32[3,864,128]{2,1,0:T(8,128)} %bitcast.10, f32[3,864,128]{2,1,0:T(8,128)} %bitcast.14, ...), custom_call_target="tpu_custom_call" | custom-call | flops 1024000 | bytes 1024 | tf_op jit(solution)/shard_map/pallas_call | solution.py:103
  31.9 2.3 %collective-permute-done.refs_1_ = f32[1296,128]{1,0:T(8,128)S(1)} collective-permute-done((f32[1296,128]{1,0:T(8,128)S(1)}, f32[1296,128]{1,0:T(8,128)S(1)}, u32[]{:S(2)}, u32[]{:S(2)}) %collective-permute-start) | collective-permute-done | bytes 663584 | tf_op jit(solution)/shard_map/ppermute | solution.py:554
  34.1 2.2 %shard_map.98.refs_7_ = f32[16,136,128]{2,1,0:T(8,128)} custom-call(s32[1]{0:T(128)} %bitcast.refs_0_, f32[1296,128]{1,0:T(8,128)S(1)} %collective-permute-done.refs_1_, f32[56,896]{1,0:T(8,128)S(1)} %get-tuple-element.21.refs_2_.refs_3_), custom_call_target="tpu_custom_call" | custom-call | flops 16777216000 | bytes 16777216 | tf_op jit(solution)/shard_map/pallas_call | solution.py:103
  36.3 4.4 %all-to-all-done.1.refs_1_ = f32[16,136,128]{2,1,0:T(8,128)} async-done(((f32[16,136,128]{2,1,0:T(8,128)}), f32[16,136,128]{2,1,0:T(8,128)}, u32[]{:S(2)}, u32[]{:S(2)}) %all-to-all-start.1) | async-done | bytes 1114144 | tf_op jit(solution)/shard_map/all_to_all | solution.py:543
  40.7 4.9 %all-to-all-start = ((f32[16,136,128]{2,1,0:T(8,128)}), f32[16,136,128]{2,1,0:T(8,128)S(1)}, u32[]{:S(2)}, u32[]{:S(2)}) async-start(f32[16,136,128]{2,1,0:T(8,128)} %shard_map.98.refs_7_), calls=%async_computation | async-start | bytes 2228224 | tf_op jit(solution)/shard_map/all_to_all | solution.py:543
  46.9 3.2 %shard_map.99 = (bf16[864,1152]{1,0:T(8,128)(2,1)S(1)}, bf16[256,1024]{1,0:T(8,128)(2,1)}) custom-call(f32[6,8,128]{2,1,0:T(8,128)S(1)} %collective-permute-done.1.refs_0_.refs_6_, f32[6,8,128]{2,1,0:T(8,128)S(1)} %collective-permute-done.2.refs_1_.refs_7_, f32[16,896]{1,0:T(8,128)S(1)} %collective-permute-done.3.refs_2_.refs_4_, ...), custom_call_target="tpu_custom_call" | custom-call | flops 104857600000 | bytes 104857600 | tf_op jit(solution)/shard_map/pallas_call | solution.py:103
  50.1 3.9 %shard_map.100 = (f32[32,96,128]{2,1,0:T(8,128)}, f32[16,128]{1,0:T(8,128)S(1)}) custom-call(s32[1]{0:T(128)} %bitcast.refs_0_, f32[16,136,128]{2,1,0:T(8,128)} %all-to-all-done.1.refs_1_, bf16[864,1152]{1,0:T(8,128)(2,1)S(1)} %get-tuple-element.24.refs_2_), custom_call_target="tpu_custom_call" | custom-call | bytes 3104772 | tf_op jit(solution)/shard_map/pallas_call | solution.py:103
  54.0 6.8 %all-to-all-done.refs_1_ = f32[16,136,128]{2,1,0:T(8,128)S(1)} async-done(((f32[16,136,128]{2,1,0:T(8,128)}), f32[16,136,128]{2,1,0:T(8,128)S(1)}, u32[]{:S(2)}, u32[]{:S(2)}) %all-to-all-start) | async-done | bytes 1114144 | tf_op jit(solution)/shard_map/all_to_all | solution.py:543
  60.8 2.6 %shard_map.101 = (f32[32,96,128]{2,1,0:T(8,128)}, f32[16,128]{1,0:T(8,128)S(1)}) custom-call(s32[1]{0:T(128)} %bitcast.refs_0_, f32[16,136,128]{2,1,0:T(8,128)S(1)} %all-to-all-done.refs_1_, bf16[864,1152]{1,0:T(8,128)(2,1)S(1)} %get-tuple-element.24.refs_2_, f32[32,96,128]{2,1,0:T(8,128)} %get-tuple-element.25.refs_3_), custom_call_target="tpu_custom_call", output_to_operand_aliasing={{0}: (3, {})} | custom-call | bytes 4677636 | tf_op jit(solution)/shard_map/pallas_call | solution.py:103
  63.5 3.5 %all-to-all-start.2 = ((f32[32,96,128]{2,1,0:T(8,128)}), f32[32,96,128]{2,1,0:T(8,128)S(1)}, u32[]{:S(2)}, u32[]{:S(2)}) async-start(f32[32,96,128]{2,1,0:T(8,128)} %get-tuple-element.26.refs_3_), calls=%async_computation.2 | async-start | bytes 3145728 | tf_op jit(solution)/shard_map/all_to_all | solution.py:621
  66.9 4.6 %shard_map.102 = (f32[3,864,128]{2,1,0:T(8,128)S(1)}, f32[3,8,128]{2,1,0:T(8,128)S(1)}, f32[3,8,128]{2,1,0:T(8,128)S(1)}) custom-call(s32[1]{0:T(128)} %bitcast.refs_0_, f32[16,128]{1,0:T(8,128)S(1)} %get-tuple-element.27.refs_1_, f32[16,128]{1,0:T(8,128)S(1)} %get-tuple-element.28.refs_2_, f32[32,96,128]{2,1,0:T(8,128)} %get-tuple-element.26.refs_3_, ...), custom_call_target="tpu_custom_call" | custom-call | bytes 2916356 | tf_op jit(solution)/shard_map/pallas_call | solution.py:103
  71.5 3.5 %collective-permute-start.5 = (f32[3,8,128]{2,1,0:T(8,128)S(1)}, f32[3,8,128]{2,1,0:T(8,128)S(1)}, u32[]{:S(2)}, u32[]{:S(2)}) collective-permute-start(f32[3,8,128]{2,1,0:T(8,128)S(1)} %get-tuple-element.29), channel_id=1, source_target_pairs={{0,4},{4,8},{8,12},{12,16},{16,20},{20,24},{24,28},{1,5},{5,9},{9,... | collective-permute-start | bytes 36872 | tf_op jit(solution)/shard_map/ppermute | solution.py:509
  77.0 3.6 %collective-permute-done.6.refs_2_ = f32[3,8,128]{2,1,0:T(8,128)S(1)} collective-permute-done((f32[3,8,128]{2,1,0:T(8,128)S(1)}, f32[3,8,128]{2,1,0:T(8,128)S(1)}, u32[]{:S(2)}, u32[]{:S(2)}) %collective-permute-start.6) | collective-permute-done | bytes 12320 | tf_op jit(solution)/shard_map/ppermute | solution.py:509
  81.5 2.9 %collective-permute-start.7 = (f32[16,896]{1,0:T(8,128)S(1)}, f32[16,896]{1,0:T(8,128)S(1)}, u32[]{:S(2)}, u32[]{:S(2)}) collective-permute-start(f32[16,896]{1,0:T(8,128)S(1)} %get-tuple-element.33), channel_id=1, source_target_pairs={{0,1},{1,2},{2,3},{4,5},{5,6},{6,7},{8,9},{9,10},{10,11},{12,13},{... | collective-permute-start | bytes 172040 | tf_op jit(solution)/shard_map/ppermute | solution.py:509
  85.7 4.3 %shard_map.104 = (f32[3,864,128]{2,1,0:T(8,128)}, f32[56,896]{1,0:T(8,128)S(1)}) custom-call(f32[3,864,128]{2,1,0:T(8,128)S(1)} %get-tuple-element.30.refs_1_.refs_0_, f32[3,8,128]{2,1,0:T(8,128)S(1)} %collective-permute-done.5.refs_0_.refs_1_, f32[3,8,128]{2,1,0:T(8,128)S(1)} %collective-permute-done.6.refs_2_, ...), custom_call_target="tpu_custom_call" | custom-call | bytes 3043328 | tf_op jit(solution)/shard_map/pallas_call | solution.py:103
  90.0 3.7 %collective-permute-done.7.refs_2_ = f32[16,896]{1,0:T(8,128)S(1)} collective-permute-done((f32[16,896]{1,0:T(8,128)S(1)}, f32[16,896]{1,0:T(8,128)S(1)}, u32[]{:S(2)}, u32[]{:S(2)}) %collective-permute-start.7) | collective-permute-done | bytes 57376 | tf_op jit(solution)/shard_map/ppermute | solution.py:509
  93.7 10.6 %all-to-all-done.2.refs_0_ = f32[32,96,128]{2,1,0:T(8,128)S(1)} async-done(((f32[32,96,128]{2,1,0:T(8,128)}), f32[32,96,128]{2,1,0:T(8,128)S(1)}, u32[]{:S(2)}, u32[]{:S(2)}) %all-to-all-start.2) | async-done | bytes 1572896 | tf_op jit(solution)/shard_map/all_to_all | solution.py:621
  104.3 3.7 %shard_map.105 = (f32[3,256,128]{2,1,0:T(8,128)}, f32[3,864,128]{2,1,0:T(8,128)}) custom-call(f32[32,96,128]{2,1,0:T(8,128)S(1)} %all-to-all-done.2.refs_0_, f32[56,896]{1,0:T(8,128)S(1)} %get-tuple-element.32.refs_1_, f32[16,896]{1,0:T(8,128)S(1)} %collective-permute-done.7.refs_2_, f32[16,896]{1,0:T(8,128)S(1)} %collective-permute-done.8.refs_3_, ...), custom_call_target="tpu_custom_call" | custom-call | bytes 3940352 | tf_op jit(solution)/shard_map/pallas_call | solution.py:103
  (18 shorter events, 11.8 us)
Async XLA Ops:
  1.9 32.2 %collective-permute-start = (f32[1296,128]{1,0:T(8,128)S(1)}, f32[1296,128]{1,0:T(8,128)S(1)}, u32[]{:S(2)}, u32[]{:S(2)}) collective-permute-start(f32[1296,128]{1,0:T(8,128)S(1)} %shard_map.95.refs_1_), channel_id=1, source_target_pairs={{0,2},{1,3},{2,0},{3,1},{4,6},{5,7},{6,4},{7,5},{8,10},{9,11},{10,... | collective-permute-start | bytes 1990664 | tf_op jit(solution)/shard_map/ppermute | solution.py:554
  7.3 18.8 %copy-start = (f32[16,136,128]{2,1,0:T(8,128)S(1)}, f32[16,136,128]{2,1,0:T(8,128)}, u32[]{:S(2)}) copy-start(f32[16,136,128]{2,1,0:T(8,128)} %shard_map.96.refs_4_) | copy-start | bytes 3342340
  7.3 33.4 %all-to-all-start.1 = ((f32[16,136,128]{2,1,0:T(8,128)}), f32[16,136,128]{2,1,0:T(8,128)}, u32[]{:S(2)}, u32[]{:S(2)}) async-start(f32[16,136,128]{2,1,0:T(8,128)} %shard_map.96.refs_4_), calls=%async_computation.1 | async-start | bytes 2228224 | tf_op jit(solution)/shard_map/all_to_all | solution.py:543
  13.9 9.4 %collective-permute-start.1 = (f32[6,8,128]{2,1,0:T(8,128)S(1)}, f32[6,8,128]{2,1,0:T(8,128)S(1)}, u32[]{:S(2)}, u32[]{:S(2)}) collective-permute-start(f32[6,8,128]{2,1,0:T(8,128)S(1)} %pad_maximum_fusion), channel_id=1, source_target_pairs={{0,4},{4,8},{8,12},{12,16},{16,20},{20,24},{24,28},{1,5},{5,9},{9,... | collective-permute-start | bytes 73736 | tf_op jit(solution)/shard_map/ppermute | solution.py:509
  17.5 8.7 %collective-permute-start.2 = (f32[6,8,128]{2,1,0:T(8,128)S(1)}, f32[6,8,128]{2,1,0:T(8,128)S(1)}, u32[]{:S(2)}, u32[]{:S(2)}) collective-permute-start(f32[6,8,128]{2,1,0:T(8,128)S(1)} %pad_maximum_fusion.1), channel_id=1, source_target_pairs={{4,0},{8,4},{12,8},{16,12},{20,16},{24,20},{28,24},{5,1},{9,5},{13... | collective-permute-start | bytes 73736 | tf_op jit(solution)/shard_map/ppermute | solution.py:509
  29.3 16.4 %collective-permute-start.3 = (f32[16,896]{1,0:T(8,128)S(1)}, f32[16,896]{1,0:T(8,128)S(1)}, u32[]{:S(2)}, u32[]{:S(2)}) collective-permute-start(f32[16,896]{1,0:T(8,128)S(1)} %get-tuple-element.22), channel_id=1, source_target_pairs={{0,1},{1,2},{2,3},{4,5},{5,6},{6,7},{8,9},{9,10},{10,11},{12,13},{... | collective-permute-start | bytes 172040 | tf_op jit(solution)/shard_map/ppermute | solution.py:509
  30.6 15.1 %collective-permute-start.4 = (f32[16,896]{1,0:T(8,128)S(1)}, f32[16,896]{1,0:T(8,128)S(1)}, u32[]{:S(2)}, u32[]{:S(2)}) collective-permute-start(f32[16,896]{1,0:T(8,128)S(1)} %get-tuple-element.23), channel_id=1, source_target_pairs={{1,0},{2,1},{3,2},{5,4},{6,5},{7,6},{9,8},{10,9},{11,10},{13,12},{... | collective-permute-start | bytes 172040 | tf_op jit(solution)/shard_map/ppermute | solution.py:509
  40.7 20.1 %all-to-all-start = ((f32[16,136,128]{2,1,0:T(8,128)}), f32[16,136,128]{2,1,0:T(8,128)S(1)}, u32[]{:S(2)}, u32[]{:S(2)}) async-start(f32[16,136,128]{2,1,0:T(8,128)} %shard_map.98.refs_7_), calls=%async_computation | async-start | bytes 2228224 | tf_op jit(solution)/shard_map/all_to_all | solution.py:543
  45.7 1.3 %copy-start.1 = (f32[16,136,128]{2,1,0:T(8,128)S(1)}, f32[16,136,128]{2,1,0:T(8,128)}, u32[]{:S(2)}) copy-start(f32[16,136,128]{2,1,0:T(8,128)} %shard_map.98.refs_7_) | copy-start | bytes 3342340
  63.5 40.8 %all-to-all-start.2 = ((f32[32,96,128]{2,1,0:T(8,128)}), f32[32,96,128]{2,1,0:T(8,128)S(1)}, u32[]{:S(2)}, u32[]{:S(2)}) async-start(f32[32,96,128]{2,1,0:T(8,128)} %get-tuple-element.26.refs_3_), calls=%async_computation.2 | async-start | bytes 3145728 | tf_op jit(solution)/shard_map/all_to_all | solution.py:621
  71.5 5.5 %collective-permute-start.5 = (f32[3,8,128]{2,1,0:T(8,128)S(1)}, f32[3,8,128]{2,1,0:T(8,128)S(1)}, u32[]{:S(2)}, u32[]{:S(2)}) collective-permute-start(f32[3,8,128]{2,1,0:T(8,128)S(1)} %get-tuple-element.29), channel_id=1, source_target_pairs={{0,4},{4,8},{8,12},{12,16},{16,20},{20,24},{24,28},{1,5},{5,9},{9,... | collective-permute-start | bytes 36872 | tf_op jit(solution)/shard_map/ppermute | solution.py:509
  75.1 5.6 %collective-permute-start.6 = (f32[3,8,128]{2,1,0:T(8,128)S(1)}, f32[3,8,128]{2,1,0:T(8,128)S(1)}, u32[]{:S(2)}, u32[]{:S(2)}) collective-permute-start(f32[3,8,128]{2,1,0:T(8,128)S(1)} %get-tuple-element.31), channel_id=1, source_target_pairs={{4,0},{8,4},{12,8},{16,12},{20,16},{24,20},{28,24},{5,1},{9,5},{13... | collective-permute-start | bytes 36872 | tf_op jit(solution)/shard_map/ppermute | solution.py:509
  81.5 12.2 %collective-permute-start.7 = (f32[16,896]{1,0:T(8,128)S(1)}, f32[16,896]{1,0:T(8,128)S(1)}, u32[]{:S(2)}, u32[]{:S(2)}) collective-permute-start(f32[16,896]{1,0:T(8,128)S(1)} %get-tuple-element.33), channel_id=1, source_target_pairs={{0,1},{1,2},{2,3},{4,5},{5,6},{6,7},{8,9},{9,10},{10,11},{12,13},{... | collective-permute-start | bytes 172040 | tf_op jit(solution)/shard_map/ppermute | solution.py:509
  84.4 9.3 %collective-permute-start.8 = (f32[16,896]{1,0:T(8,128)S(1)}, f32[16,896]{1,0:T(8,128)S(1)}, u32[]{:S(2)}, u32[]{:S(2)}) collective-permute-start(f32[16,896]{1,0:T(8,128)S(1)} %get-tuple-element.34), channel_id=1, source_target_pairs={{1,0},{2,1},{3,2},{5,4},{6,5},{7,6},{9,8},{10,9},{11,10},{13,12},{... | collective-permute-start | bytes 172040 | tf_op jit(solution)/shard_map/ppermute | solution.py:509

commit v4 on v3

--- a/solution.py
+++ b/solution.py
@@ -242,14 +242,14 @@
     for chan in range(chans):
         beside = slice(first + chan * take, first + (chan + 1) * take)
         inner = slice(chan * STRIP + ITERS, (chan + 1) * STRIP - ITERS)
-        pieces += gap + [left[beside, :], own[inner, :], right[beside, :]] + gap
+        pieces += gap + [left[beside, 0, :], own[inner, :], right[beside, 0, :]] + gap
     pieces.append(jnp.zeros((own.shape[0] - chans * STRIP, own.shape[1]), F32))
     return jnp.concatenate(pieces, axis=0)
 
 
 def edge_columns(pieces, outputs):
     width = pieces[0][0].shape[1]
-    length = outputs[0][0].shape[1]
+    length = outputs[0][0].shape[-1]
     tail = length - sum(piece.shape[0] for piece in pieces[0])
     whole = jnp.concatenate(
         [jnp.concatenate([*piece, jnp.zeros((tail, width), F32)], axis=0) for piece in pieces],
@@ -257,7 +257,7 @@
     )
     rows = []
     for ref, lane in outputs:
-        shape = (ref.shape[0], whole.shape[1])
+        shape = (-(-ref.shape[0] // EDGE) * EDGE, whole.shape[1])
         rows.append(iota(shape, 1) == lane(iota(shape, 0)))
     select = one_hot(jnp.concatenate([row.astype(jnp.int32) for row in rows], axis=0) > 0)
     top, middle, bottom = split3(whole)
@@ -265,8 +265,8 @@
     edges = edges + dot(select, top, (1, 1))
     first = 0
     for ref, _ in outputs:
-        ref[...] = edges[first : first + ref.shape[0]]
-        first += ref.shape[0]
+        ref[...] = edges[first : first + ref.shape[0]].reshape(ref.shape)
+        first += -(-ref.shape[0] // EDGE) * EDGE
 
 
 def first_columns_kernel(before, after, atm, diff, low, high, own):
@@ -339,7 +339,7 @@
 
 
 def nearest_columns(left, right, width, chans):
-    edges = jnp.concatenate([left[:EDGE, :], right[:EDGE, :]], axis=0)
+    edges = jnp.concatenate([left[:EDGE, 0, :], right[:EDGE, 0, :]], axis=0)
     shape = (6 * EDGE, chans * width)
     which, lane = iota(shape, 0), iota(shape, 1)
     line = which % (2 * EDGE)
@@ -356,7 +356,7 @@
     rows = table.shape[0]
     across = ocn_count // 2
     base = (1 - half[0] if mirrored else half[0]) * across
-    groups = 2
+    groups = 4
     each = owners // groups
     stores = []
     label_rows[...] = incoming[:, (chans + 1) * cap, :]
@@ -572,12 +572,14 @@
     own_incoming = exchange(own_packed)
     long = -(-(rows + 2 * EDGE) // 128) * 128
 
+    edge = shape(chans * ITERS, 1, long)
+
     def lines(columns):
         return shape(-(-columns // EDGE) * EDGE, long)
 
     low, high, diff_own = call(
         first_columns_kernel,
-        (lines(chans * ITERS), lines(chans * ITERS), lines(chans * STRIP)),
+        (edge, edge, lines(chans * STRIP)),
         (before, after, atm, diff),
         late=(2, 3),
         after=(own_packed,),
@@ -638,7 +640,7 @@
     forced_before, forced_after = shift("atm", top, bottom)
     forced_low, forced_high, forced_own = call(
         columns_kernel,
-        (lines(chans * ITERS), lines(chans * ITERS), lines(chans * STRIP)),
+        (edge, edge, lines(chans * STRIP)),
         (forced_before, forced, forced_after),
     )
     forced_left, forced_right = shift("ocn", forced_low, forced_high)

time: 109 us -> 109 us (level)
  no operation moved by 1% of the time
where the time goes in v4:
time: 109 us; the launch traced here: 108 us
  waiting for transfers between devices  38.2 us (35%)
  starting transfers between devices  35 us (32%)
  Pallas kernels  31.7 us (29%)
  local copies, waits for them, and re-layouts  2.02 us (2%)
    pallas_call x11, Pallas kernels, call(): pl.pallas_call(body, out_shape=out_shape, in_specs=[pl.BlockSpec(memory_s...  31.7 us
    ppermute x4, starting transfers between devices, shift(): lax.ppermute(high_edge, axis, forward)  11.3 us
    all_to_all x2, waiting for transfers between devices, exchange(): lax.all_to_all(x, BOTH, split_axis=0, concat_axis=0, tiled=True, axis_ind...  11.3 us
    all_to_all x1, waiting for transfers between devices, per_device(): lax.all_to_all(weighted, BOTH, split_axis=0, concat_axis=0, tiled=True)  11.2 us
    all_to_all x2, starting transfers between devices, exchange(): lax.all_to_all(x, BOTH, split_axis=0, concat_axis=0, tiled=True, axis_ind...  10.7 us
    ppermute x4, waiting for transfers between devices, shift(): lax.ppermute(high_edge, axis, forward)  7.08 us
    ppermute x4, starting transfers between devices, shift(): lax.ppermute(low_edge, axis, backward)  6.43 us
    ppermute x4, waiting for transfers between devices, shift(): lax.ppermute(low_edge, axis, backward)  6.41 us
  transfers between devices with their start and end apart: 12, of which 8 were waited for; matrix products, arithmetic and copies ran while one was open for 1% of the time, Pallas kernels for 22%

profile of v4, /device:TPU:1, one launch (start us, length us, event | category | flops | bytes accessed | tf_op | source)
XLA Modules:
  0.0 107.9 jit_solution(17612880914281657742)
XLA Ops:
  1.9 3.2 %collective-permute-start = (f32[1296,128]{1,0:T(8,128)S(1)}, f32[1296,128]{1,0:T(8,128)S(1)}, u32[]{:S(2)}, u32[]{:S(2)}) collective-permute-start(f32[1296,128]{1,0:T(8,128)S(1)} %shard_map.95.refs_1_), channel_id=1, source_target_pairs={{0,2},{1,3},{2,0},{3,1},{4,6},{5,7},{6,4},{7,5},{8,10},{9,11},{10,... | collective-permute-start | bytes 1990664 | tf_op jit(solution)/shard_map/ppermute | solution.py:554
  5.1 2.1 %shard_map.96.refs_4_ = f32[16,136,128]{2,1,0:T(8,128)} custom-call(s32[1]{0:T(128)} %bitcast.refs_0_, f32[1296,128]{1,0:T(8,128)S(1)} %shard_map.95.refs_1_), custom_call_target="tpu_custom_call" | custom-call | flops 1024000 | bytes 1024 | tf_op jit(solution)/shard_map/pallas_call | solution.py:103
  7.3 5.8 %all-to-all-start.1 = ((f32[16,136,128]{2,1,0:T(8,128)}), f32[16,136,128]{2,1,0:T(8,128)}, u32[]{:S(2)}, u32[]{:S(2)}) async-start(f32[16,136,128]{2,1,0:T(8,128)} %shard_map.96.refs_4_), calls=%async_computation.1 | async-start | bytes 2228224 | tf_op jit(solution)/shard_map/all_to_all | solution.py:543
  13.9 3.5 %collective-permute-start.1 = (f32[6,8,128]{2,1,0:T(8,128)S(1)}, f32[6,8,128]{2,1,0:T(8,128)S(1)}, u32[]{:S(2)}, u32[]{:S(2)}) collective-permute-start(f32[6,8,128]{2,1,0:T(8,128)S(1)} %pad_maximum_fusion), channel_id=1, source_target_pairs={{0,4},{4,8},{8,12},{12,16},{16,20},{20,24},{24,28},{1,5},{5,9},{9,... | collective-permute-start | bytes 73736 | tf_op jit(solution)/shard_map/ppermute | solution.py:509
  19.4 4.0 %collective-permute-done.1.refs_0_.refs_6_ = f32[6,8,128]{2,1,0:T(8,128)S(1)} collective-permute-done((f32[6,8,128]{2,1,0:T(8,128)S(1)}, f32[6,8,128]{2,1,0:T(8,128)S(1)}, u32[]{:S(2)}, u32[]{:S(2)}) %collective-permute-start.1) | collective-permute-done | bytes 24608 | tf_op jit(solution)/shard_map/ppermute | solution.py:509
  23.3 2.8 %collective-permute-done.2.refs_1_.refs_7_ = f32[6,8,128]{2,1,0:T(8,128)S(1)} collective-permute-done((f32[6,8,128]{2,1,0:T(8,128)S(1)}, f32[6,8,128]{2,1,0:T(8,128)S(1)}, u32[]{:S(2)}, u32[]{:S(2)}) %collective-permute-start.2) | collective-permute-done | bytes 24608 | tf_op jit(solution)/shard_map/ppermute | solution.py:509
  26.1 3.1 %shard_map.97 = (f32[9,1,896]{2,1,0:T(1,128)S(1)}, f32[9,1,896]{2,1,0:T(1,128)S(1)}, f32[56,896]{1,0:T(8,128)S(1)}) custom-call(f32[6,8,128]{2,1,0:T(8,128)S(1)} %collective-permute-done.1.refs_0_.refs_6_, f32[6,8,128]{2,1,0:T(8,128)S(1)} %collective-permute-done.2.refs_1_.refs_7_, f32[3,864,128]{2,1,0:T(8,128)} %bitcast.10, f32[3,864,128]{2,1,0:T(8,128)} %bitcast.14, ...), custom_call_target="tpu_custom_call" | custom-call | flops 1024000 | bytes 1024 | tf_op jit(solution)/shard_map/pallas_call | solution.py:103
  31.9 2.3 %collective-permute-done.refs_1_ = f32[1296,128]{1,0:T(8,128)S(1)} collective-permute-done((f32[1296,128]{1,0:T(8,128)S(1)}, f32[1296,128]{1,0:T(8,128)S(1)}, u32[]{:S(2)}, u32[]{:S(2)}) %collective-permute-start) | collective-permute-done | bytes 663584 | tf_op jit(solution)/shard_map/ppermute | solution.py:554
  34.1 2.2 %shard_map.98.refs_7_ = f32[16,136,128]{2,1,0:T(8,128)} custom-call(s32[1]{0:T(128)} %bitcast.refs_0_, f32[1296,128]{1,0:T(8,128)S(1)} %collective-permute-done.refs_1_, f32[56,896]{1,0:T(8,128)S(1)} %get-tuple-element.21.refs_2_.refs_3_), custom_call_target="tpu_custom_call" | custom-call | flops 16777216000 | bytes 16777216 | tf_op jit(solution)/shard_map/pallas_call | solution.py:103
  36.3 4.4 %all-to-all-done.1.refs_1_ = f32[16,136,128]{2,1,0:T(8,128)} async-done(((f32[16,136,128]{2,1,0:T(8,128)}), f32[16,136,128]{2,1,0:T(8,128)}, u32[]{:S(2)}, u32[]{:S(2)}) %all-to-all-start.1) | async-done | bytes 1114144 | tf_op jit(solution)/shard_map/all_to_all | solution.py:543
  40.7 4.8 %all-to-all-start = ((f32[16,136,128]{2,1,0:T(8,128)}), f32[16,136,128]{2,1,0:T(8,128)S(1)}, u32[]{:S(2)}, u32[]{:S(2)}) async-start(f32[16,136,128]{2,1,0:T(8,128)} %shard_map.98.refs_7_), calls=%async_computation | async-start | bytes 2228224 | tf_op jit(solution)/shard_map/all_to_all | solution.py:543
  46.8 3.2 %shard_map.99 = (bf16[864,1152]{1,0:T(8,128)(2,1)S(1)}, bf16[256,1024]{1,0:T(8,128)(2,1)}) custom-call(f32[6,8,128]{2,1,0:T(8,128)S(1)} %collective-permute-done.1.refs_0_.refs_6_, f32[6,8,128]{2,1,0:T(8,128)S(1)} %collective-permute-done.2.refs_1_.refs_7_, f32[9,1,896]{2,1,0:T(1,128)S(1)} %collective-permute-done.3.refs_2_.refs_4_, ...), custom_call_target="tpu_custom_call" | custom-call | flops 104857600000 | bytes 104857600 | tf_op jit(solution)/shard_map/pallas_call | solution.py:103
  50.0 3.8 %shard_map.100 = (f32[32,96,128]{2,1,0:T(8,128)}, f32[16,128]{1,0:T(8,128)S(1)}) custom-call(s32[1]{0:T(128)} %bitcast.refs_0_, f32[16,136,128]{2,1,0:T(8,128)} %all-to-all-done.1.refs_1_, bf16[864,1152]{1,0:T(8,128)(2,1)S(1)} %get-tuple-element.24.refs_2_), custom_call_target="tpu_custom_call" | custom-call | bytes 3104772 | tf_op jit(solution)/shard_map/pallas_call | solution.py:103
  53.8 6.9 %all-to-all-done.refs_1_ = f32[16,136,128]{2,1,0:T(8,128)S(1)} async-done(((f32[16,136,128]{2,1,0:T(8,128)}), f32[16,136,128]{2,1,0:T(8,128)S(1)}, u32[]{:S(2)}, u32[]{:S(2)}) %all-to-all-start) | async-done | bytes 1114144 | tf_op jit(solution)/shard_map/all_to_all | solution.py:543
  60.7 2.5 %shard_map.101 = (f32[32,96,128]{2,1,0:T(8,128)}, f32[16,128]{1,0:T(8,128)S(1)}) custom-call(s32[1]{0:T(128)} %bitcast.refs_0_, f32[16,136,128]{2,1,0:T(8,128)S(1)} %all-to-all-done.refs_1_, bf16[864,1152]{1,0:T(8,128)(2,1)S(1)} %get-tuple-element.24.refs_2_, f32[32,96,128]{2,1,0:T(8,128)} %get-tuple-element.25.refs_3_), custom_call_target="tpu_custom_call", output_to_operand_aliasing={{0}: (3, {})} | custom-call | bytes 4677636 | tf_op jit(solution)/shard_map/pallas_call | solution.py:103
  63.2 3.5 %all-to-all-start.2 = ((f32[32,96,128]{2,1,0:T(8,128)}), f32[32,96,128]{2,1,0:T(8,128)S(1)}, u32[]{:S(2)}, u32[]{:S(2)}) async-start(f32[32,96,128]{2,1,0:T(8,128)} %get-tuple-element.26.refs_3_), calls=%async_computation.2 | async-start | bytes 3145728 | tf_op jit(solution)/shard_map/all_to_all | solution.py:623
  66.7 4.6 %shard_map.102 = (f32[3,864,128]{2,1,0:T(8,128)S(1)}, f32[3,8,128]{2,1,0:T(8,128)S(1)}, f32[3,8,128]{2,1,0:T(8,128)S(1)}) custom-call(s32[1]{0:T(128)} %bitcast.refs_0_, f32[16,128]{1,0:T(8,128)S(1)} %get-tuple-element.27.refs_1_, f32[16,128]{1,0:T(8,128)S(1)} %get-tuple-element.28.refs_2_, f32[32,96,128]{2,1,0:T(8,128)} %get-tuple-element.26.refs_3_, ...), custom_call_target="tpu_custom_call" | custom-call | bytes 2916356 | tf_op jit(solution)/shard_map/pallas_call | solution.py:103
  71.3 3.5 %collective-permute-start.5 = (f32[3,8,128]{2,1,0:T(8,128)S(1)}, f32[3,8,128]{2,1,0:T(8,128)S(1)}, u32[]{:S(2)}, u32[]{:S(2)}) collective-permute-start(f32[3,8,128]{2,1,0:T(8,128)S(1)} %get-tuple-element.29), channel_id=1, source_target_pairs={{0,4},{4,8},{8,12},{12,16},{16,20},{20,24},{24,28},{1,5},{5,9},{9,... | collective-permute-start | bytes 36872 | tf_op jit(solution)/shard_map/ppermute | solution.py:509
  76.8 3.6 %collective-permute-done.6.refs_2_ = f32[3,8,128]{2,1,0:T(8,128)S(1)} collective-permute-done((f32[3,8,128]{2,1,0:T(8,128)S(1)}, f32[3,8,128]{2,1,0:T(8,128)S(1)}, u32[]{:S(2)}, u32[]{:S(2)}) %collective-permute-start.6) | collective-permute-done | bytes 12320 | tf_op jit(solution)/shard_map/ppermute | solution.py:509
  81.2 2.9 %collective-permute-start.7 = (f32[9,1,896]{2,1,0:T(1,128)S(1)}, f32[9,1,896]{2,1,0:T(1,128)S(1)}, u32[]{:S(2)}, u32[]{:S(2)}) collective-permute-start(f32[9,1,896]{2,1,0:T(1,128)S(1)} %get-tuple-element.33), channel_id=1, source_target_pairs={{0,1},{1,2},{2,3},{4,5},{5,6},{6,7},{8,9},{9,10},{10,11},{12,13},{... | collective-permute-start | bytes 96776 | tf_op jit(solution)/shard_map/ppermute | solution.py:509
  85.5 4.3 %shard_map.104 = (f32[3,864,128]{2,1,0:T(8,128)}, f32[56,896]{1,0:T(8,128)S(1)}) custom-call(f32[3,864,128]{2,1,0:T(8,128)S(1)} %get-tuple-element.30.refs_1_.refs_0_, f32[3,8,128]{2,1,0:T(8,128)S(1)} %collective-permute-done.5.refs_0_.refs_1_, f32[3,8,128]{2,1,0:T(8,128)S(1)} %collective-permute-done.6.refs_2_, ...), custom_call_target="tpu_custom_call" | custom-call | bytes 2993152 | tf_op jit(solution)/shard_map/pallas_call | solution.py:103
  89.8 3.1 %collective-permute-done.7.refs_2_ = f32[9,1,896]{2,1,0:T(1,128)S(1)} collective-permute-done((f32[9,1,896]{2,1,0:T(1,128)S(1)}, f32[9,1,896]{2,1,0:T(1,128)S(1)}, u32[]{:S(2)}, u32[]{:S(2)}) %collective-permute-start.7) | collective-permute-done | bytes 32288 | tf_op jit(solution)/shard_map/ppermute | solution.py:509
  92.9 11.2 %all-to-all-done.2.refs_0_ = f32[32,96,128]{2,1,0:T(8,128)S(1)} async-done(((f32[32,96,128]{2,1,0:T(8,128)}), f32[32,96,128]{2,1,0:T(8,128)S(1)}, u32[]{:S(2)}, u32[]{:S(2)}) %all-to-all-start.2) | async-done | bytes 1572896 | tf_op jit(solution)/shard_map/all_to_all | solution.py:623
  104.1 3.7 %shard_map.105 = (f32[3,256,128]{2,1,0:T(8,128)}, f32[3,864,128]{2,1,0:T(8,128)}) custom-call(f32[32,96,128]{2,1,0:T(8,128)S(1)} %all-to-all-done.2.refs_0_, f32[56,896]{1,0:T(8,128)S(1)} %get-tuple-element.32.refs_1_, f32[9,1,896]{2,1,0:T(1,128)S(1)} %collective-permute-done.7.refs_2_, f32[9,1,896]{2,1,0:T(1,128)S(1)} %collective-permute-done.8.refs_3_, ...), custom_call_target="tpu_custom_call" | custom-call | bytes 3890176 | tf_op jit(solution)/shard_map/pallas_call | solution.py:103
  (18 shorter events, 11.9 us)
Async XLA Ops:
  1.9 32.2 %collective-permute-start = (f32[1296,128]{1,0:T(8,128)S(1)}, f32[1296,128]{1,0:T(8,128)S(1)}, u32[]{:S(2)}, u32[]{:S(2)}) collective-permute-start(f32[1296,128]{1,0:T(8,128)S(1)} %shard_map.95.refs_1_), channel_id=1, source_target_pairs={{0,2},{1,3},{2,0},{3,1},{4,6},{5,7},{6,4},{7,5},{8,10},{9,11},{10,... | collective-permute-start | bytes 1990664 | tf_op jit(solution)/shard_map/ppermute | solution.py:554
  7.3 18.8 %copy-start = (f32[16,136,128]{2,1,0:T(8,128)S(1)}, f32[16,136,128]{2,1,0:T(8,128)}, u32[]{:S(2)}) copy-start(f32[16,136,128]{2,1,0:T(8,128)} %shard_map.96.refs_4_) | copy-start | bytes 3342340
  7.3 33.4 %all-to-all-start.1 = ((f32[16,136,128]{2,1,0:T(8,128)}), f32[16,136,128]{2,1,0:T(8,128)}, u32[]{:S(2)}, u32[]{:S(2)}) async-start(f32[16,136,128]{2,1,0:T(8,128)} %shard_map.96.refs_4_), calls=%async_computation.1 | async-start | bytes 2228224 | tf_op jit(solution)/shard_map/all_to_all | solution.py:543
  13.9 9.4 %collective-permute-start.1 = (f32[6,8,128]{2,1,0:T(8,128)S(1)}, f32[6,8,128]{2,1,0:T(8,128)S(1)}, u32[]{:S(2)}, u32[]{:S(2)}) collective-permute-start(f32[6,8,128]{2,1,0:T(8,128)S(1)} %pad_maximum_fusion), channel_id=1, source_target_pairs={{0,4},{4,8},{8,12},{12,16},{16,20},{20,24},{24,28},{1,5},{5,9},{9,... | collective-permute-start | bytes 73736 | tf_op jit(solution)/shard_map/ppermute | solution.py:509
  17.5 8.7 %collective-permute-start.2 = (f32[6,8,128]{2,1,0:T(8,128)S(1)}, f32[6,8,128]{2,1,0:T(8,128)S(1)}, u32[]{:S(2)}, u32[]{:S(2)}) collective-permute-start(f32[6,8,128]{2,1,0:T(8,128)S(1)} %pad_maximum_fusion.1), channel_id=1, source_target_pairs={{4,0},{8,4},{12,8},{16,12},{20,16},{24,20},{28,24},{5,1},{9,5},{13... | collective-permute-start | bytes 73736 | tf_op jit(solution)/shard_map/ppermute | solution.py:509
  29.3 16.3 %collective-permute-start.3 = (f32[9,1,896]{2,1,0:T(1,128)S(1)}, f32[9,1,896]{2,1,0:T(1,128)S(1)}, u32[]{:S(2)}, u32[]{:S(2)}) collective-permute-start(f32[9,1,896]{2,1,0:T(1,128)S(1)} %get-tuple-element.22), channel_id=1, source_target_pairs={{0,1},{1,2},{2,3},{4,5},{5,6},{6,7},{8,9},{9,10},{10,11},{12,13},{... | collective-permute-start | bytes 96776 | tf_op jit(solution)/shard_map/ppermute | solution.py:509
  30.6 15.0 %collective-permute-start.4 = (f32[9,1,896]{2,1,0:T(1,128)S(1)}, f32[9,1,896]{2,1,0:T(1,128)S(1)}, u32[]{:S(2)}, u32[]{:S(2)}) collective-permute-start(f32[9,1,896]{2,1,0:T(1,128)S(1)} %get-tuple-element.23), channel_id=1, source_target_pairs={{1,0},{2,1},{3,2},{5,4},{6,5},{7,6},{9,8},{10,9},{11,10},{13,12},{... | collective-permute-start | bytes 96776 | tf_op jit(solution)/shard_map/ppermute | solution.py:509
  40.7 20.0 %all-to-all-start = ((f32[16,136,128]{2,1,0:T(8,128)}), f32[16,136,128]{2,1,0:T(8,128)S(1)}, u32[]{:S(2)}, u32[]{:S(2)}) async-start(f32[16,136,128]{2,1,0:T(8,128)} %shard_map.98.refs_7_), calls=%async_computation | async-start | bytes 2228224 | tf_op jit(solution)/shard_map/all_to_all | solution.py:543
  45.5 1.3 %copy-start.1 = (f32[16,136,128]{2,1,0:T(8,128)S(1)}, f32[16,136,128]{2,1,0:T(8,128)}, u32[]{:S(2)}) copy-start(f32[16,136,128]{2,1,0:T(8,128)} %shard_map.98.refs_7_) | copy-start | bytes 3342340
  63.2 40.8 %all-to-all-start.2 = ((f32[32,96,128]{2,1,0:T(8,128)}), f32[32,96,128]{2,1,0:T(8,128)S(1)}, u32[]{:S(2)}, u32[]{:S(2)}) async-start(f32[32,96,128]{2,1,0:T(8,128)} %get-tuple-element.26.refs_3_), calls=%async_computation.2 | async-start | bytes 3145728 | tf_op jit(solution)/shard_map/all_to_all | solution.py:623
  71.3 5.5 %collective-permute-start.5 = (f32[3,8,128]{2,1,0:T(8,128)S(1)}, f32[3,8,128]{2,1,0:T(8,128)S(1)}, u32[]{:S(2)}, u32[]{:S(2)}) collective-permute-start(f32[3,8,128]{2,1,0:T(8,128)S(1)} %get-tuple-element.29), channel_id=1, source_target_pairs={{0,4},{4,8},{8,12},{12,16},{16,20},{20,24},{24,28},{1,5},{5,9},{9,... | collective-permute-start | bytes 36872 | tf_op jit(solution)/shard_map/ppermute | solution.py:509
  74.9 5.6 %collective-permute-start.6 = (f32[3,8,128]{2,1,0:T(8,128)S(1)}, f32[3,8,128]{2,1,0:T(8,128)S(1)}, u32[]{:S(2)}, u32[]{:S(2)}) collective-permute-start(f32[3,8,128]{2,1,0:T(8,128)S(1)} %get-tuple-element.31), channel_id=1, source_target_pairs={{4,0},{8,4},{12,8},{16,12},{20,16},{24,20},{28,24},{5,1},{9,5},{13... | collective-permute-start | bytes 36872 | tf_op jit(solution)/shard_map/ppermute | solution.py:509
  81.2 11.7 %collective-permute-start.7 = (f32[9,1,896]{2,1,0:T(1,128)S(1)}, f32[9,1,896]{2,1,0:T(1,128)S(1)}, u32[]{:S(2)}, u32[]{:S(2)}) collective-permute-start(f32[9,1,896]{2,1,0:T(1,128)S(1)} %get-tuple-element.33), channel_id=1, source_target_pairs={{0,1},{1,2},{2,3},{4,5},{5,6},{6,7},{8,9},{9,10},{10,11},{12,13},{... | collective-permute-start | bytes 96776 | tf_op jit(solution)/shard_map/ppermute | solution.py:509
  84.2 8.7 %collective-permute-start.8 = (f32[9,1,896]{2,1,0:T(1,128)S(1)}, f32[9,1,896]{2,1,0:T(1,128)S(1)}, u32[]{:S(2)}, u32[]{:S(2)}) collective-permute-start(f32[9,1,896]{2,1,0:T(1,128)S(1)} %get-tuple-element.34), channel_id=1, source_target_pairs={{1,0},{2,1},{3,2},{5,4},{6,5},{7,6},{9,8},{10,9},{11,10},{13,12},{... | collective-permute-start | bytes 96776 | tf_op jit(solution)/shard_map/ppermute | solution.py:509

commit v5 on v4

--- a/solution.py
+++ b/solution.py
@@ -146,10 +146,10 @@
     place = one_hot(iota((slots, count), 0) == slot)
     member = one_hot(iota((segs, count), 0) == seg)
     of_seg = dot(place, member, (1, 1)).astype(BF16)
+    (reach,) = exact_dots(place, [weight])
+    send(chans, cap, reach)
     for chan, sent in enumerate(exact_dots(of_seg, ocean)):
         send(chan, cap, sent)
-    (reach,) = exact_dots(place, [weight])
-    send(chans, cap, reach)
     line = iota((owners * EDGE, count), 0)
     tall = line == group * EDGE + (position & (EDGE - 1))
     flat = line == group * EDGE
@@ -474,8 +474,9 @@
         returned[:, chan * cap : (chan + 1) * cap, :].reshape(devices * cap, width)
         for chan in range(chans)
     ]
-    for chan, total in enumerate(exact_dots(seg_select.get()[...], values)):
-        flux_staged[chan] = total
+    select = seg_select.get()[...]
+    for chan in range(chans):
+        (flux_staged[chan],) = exact_dots(select, [values[chan]])
     send(flux_staged, ocean_flux)
     state = fill_strip(own, left, right, 0, chans, ITERS)
     spread = diff_strip[...]

time: 109 us -> 109 us (level)
  no operation moved by 1% of the time
where the time goes in v5:
time: 109 us; the launch traced here: 108 us
  waiting for transfers between devices  38.4 us (35%)
  starting transfers between devices  35.1 us (32%)
  Pallas kernels  31.2 us (29%)
  local copies, waits for them, and re-layouts  2.02 us (2%)
    pallas_call x11, Pallas kernels, call(): pl.pallas_call(body, out_shape=out_shape, in_specs=[pl.BlockSpec(memory_s...  31.2 us
    ppermute x4, starting transfers between devices, shift(): lax.ppermute(high_edge, axis, forward)  11.3 us
    all_to_all x2, waiting for transfers between devices, exchange(): lax.all_to_all(x, BOTH, split_axis=0, concat_axis=0, tiled=True, axis_ind...  11.2 us
    all_to_all x1, waiting for transfers between devices, per_device(): lax.all_to_all(weighted, BOTH, split_axis=0, concat_axis=0, tiled=True)  11.2 us
    all_to_all x2, starting transfers between devices, exchange(): lax.all_to_all(x, BOTH, split_axis=0, concat_axis=0, tiled=True, axis_ind...  10.7 us
    ppermute x4, waiting for transfers between devices, shift(): lax.ppermute(high_edge, axis, forward)  7.23 us
    ppermute x4, starting transfers between devices, shift(): lax.ppermute(low_edge, axis, backward)  6.43 us
    ppermute x4, waiting for transfers between devices, shift(): lax.ppermute(low_edge, axis, backward)  6.41 us
  transfers between devices with their start and end apart: 12, of which 8 were waited for; matrix products, arithmetic and copies ran while one was open for 1% of the time, Pallas kernels for 22%

profile of v5, /device:TPU:1, one launch (start us, length us, event | category | flops | bytes accessed | tf_op | source)
XLA Modules:
  0.0 107.8 jit_solution(11721842818599574747)
XLA Ops:
  1.9 3.2 %collective-permute-start = (f32[1296,128]{1,0:T(8,128)S(1)}, f32[1296,128]{1,0:T(8,128)S(1)}, u32[]{:S(2)}, u32[]{:S(2)}) collective-permute-start(f32[1296,128]{1,0:T(8,128)S(1)} %shard_map.95.refs_1_), channel_id=1, source_target_pairs={{0,2},{1,3},{2,0},{3,1},{4,6},{5,7},{6,4},{7,5},{8,10},{9,11},{10,... | collective-permute-start | bytes 1990664 | tf_op jit(solution)/shard_map/ppermute | solution.py:555
  5.1 1.9 %shard_map.96.refs_4_ = f32[16,136,128]{2,1,0:T(8,128)} custom-call(s32[1]{0:T(128)} %bitcast.refs_0_, f32[1296,128]{1,0:T(8,128)S(1)} %shard_map.95.refs_1_), custom_call_target="tpu_custom_call" | custom-call | flops 1024000 | bytes 1024 | tf_op jit(solution)/shard_map/pallas_call | solution.py:103
  7.1 5.8 %all-to-all-start.1 = ((f32[16,136,128]{2,1,0:T(8,128)}), f32[16,136,128]{2,1,0:T(8,128)}, u32[]{:S(2)}, u32[]{:S(2)}) async-start(f32[16,136,128]{2,1,0:T(8,128)} %shard_map.96.refs_4_), calls=%async_computation.1 | async-start | bytes 2228224 | tf_op jit(solution)/shard_map/all_to_all | solution.py:544
  13.7 3.5 %collective-permute-start.1 = (f32[6,8,128]{2,1,0:T(8,128)S(1)}, f32[6,8,128]{2,1,0:T(8,128)S(1)}, u32[]{:S(2)}, u32[]{:S(2)}) collective-permute-start(f32[6,8,128]{2,1,0:T(8,128)S(1)} %pad_maximum_fusion), channel_id=1, source_target_pairs={{0,4},{4,8},{8,12},{12,16},{16,20},{20,24},{24,28},{1,5},{5,9},{9,... | collective-permute-start | bytes 73736 | tf_op jit(solution)/shard_map/ppermute | solution.py:510
  19.2 4.1 %collective-permute-done.1.refs_0_.refs_6_ = f32[6,8,128]{2,1,0:T(8,128)S(1)} collective-permute-done((f32[6,8,128]{2,1,0:T(8,128)S(1)}, f32[6,8,128]{2,1,0:T(8,128)S(1)}, u32[]{:S(2)}, u32[]{:S(2)}) %collective-permute-start.1) | collective-permute-done | bytes 24608 | tf_op jit(solution)/shard_map/ppermute | solution.py:510
  23.3 2.8 %collective-permute-done.2.refs_1_.refs_7_ = f32[6,8,128]{2,1,0:T(8,128)S(1)} collective-permute-done((f32[6,8,128]{2,1,0:T(8,128)S(1)}, f32[6,8,128]{2,1,0:T(8,128)S(1)}, u32[]{:S(2)}, u32[]{:S(2)}) %collective-permute-start.2) | collective-permute-done | bytes 24608 | tf_op jit(solution)/shard_map/ppermute | solution.py:510
  26.1 3.1 %shard_map.97 = (f32[9,1,896]{2,1,0:T(1,128)S(1)}, f32[9,1,896]{2,1,0:T(1,128)S(1)}, f32[56,896]{1,0:T(8,128)S(1)}) custom-call(f32[6,8,128]{2,1,0:T(8,128)S(1)} %collective-permute-done.1.refs_0_.refs_6_, f32[6,8,128]{2,1,0:T(8,128)S(1)} %collective-permute-done.2.refs_1_.refs_7_, f32[3,864,128]{2,1,0:T(8,128)} %bitcast.10, f32[3,864,128]{2,1,0:T(8,128)} %bitcast.14, ...), custom_call_target="tpu_custom_call" | custom-call | flops 1024000 | bytes 1024 | tf_op jit(solution)/shard_map/pallas_call | solution.py:103
  31.8 2.3 %collective-permute-done.refs_1_ = f32[1296,128]{1,0:T(8,128)S(1)} collective-permute-done((f32[1296,128]{1,0:T(8,128)S(1)}, f32[1296,128]{1,0:T(8,128)S(1)}, u32[]{:S(2)}, u32[]{:S(2)}) %collective-permute-start) | collective-permute-done | bytes 663584 | tf_op jit(solution)/shard_map/ppermute | solution.py:555
  34.2 2.0 %shard_map.98.refs_7_ = f32[16,136,128]{2,1,0:T(8,128)} custom-call(s32[1]{0:T(128)} %bitcast.refs_0_, f32[1296,128]{1,0:T(8,128)S(1)} %collective-permute-done.refs_1_, f32[56,896]{1,0:T(8,128)S(1)} %get-tuple-element.21.refs_2_.refs_3_), custom_call_target="tpu_custom_call" | custom-call | flops 16777216000 | bytes 16777216 | tf_op jit(solution)/shard_map/pallas_call | solution.py:103
  36.2 4.4 %all-to-all-done.1.refs_1_ = f32[16,136,128]{2,1,0:T(8,128)} async-done(((f32[16,136,128]{2,1,0:T(8,128)}), f32[16,136,128]{2,1,0:T(8,128)}, u32[]{:S(2)}, u32[]{:S(2)}) %all-to-all-start.1) | async-done | bytes 1114144 | tf_op jit(solution)/shard_map/all_to_all | solution.py:544
  40.5 4.8 %all-to-all-start = ((f32[16,136,128]{2,1,0:T(8,128)}), f32[16,136,128]{2,1,0:T(8,128)S(1)}, u32[]{:S(2)}, u32[]{:S(2)}) async-start(f32[16,136,128]{2,1,0:T(8,128)} %shard_map.98.refs_7_), calls=%async_computation | async-start | bytes 2228224 | tf_op jit(solution)/shard_map/all_to_all | solution.py:544
  46.6 3.2 %shard_map.99 = (bf16[864,1152]{1,0:T(8,128)(2,1)S(1)}, bf16[256,1024]{1,0:T(8,128)(2,1)}) custom-call(f32[6,8,128]{2,1,0:T(8,128)S(1)} %collective-permute-done.1.refs_0_.refs_6_, f32[6,8,128]{2,1,0:T(8,128)S(1)} %collective-permute-done.2.refs_1_.refs_7_, f32[9,1,896]{2,1,0:T(1,128)S(1)} %collective-permute-done.3.refs_2_.refs_4_, ...), custom_call_target="tpu_custom_call" | custom-call | flops 104857600000 | bytes 104857600 | tf_op jit(solution)/shard_map/pallas_call | solution.py:103
  49.8 3.8 %shard_map.100 = (f32[32,96,128]{2,1,0:T(8,128)}, f32[16,128]{1,0:T(8,128)S(1)}) custom-call(s32[1]{0:T(128)} %bitcast.refs_0_, f32[16,136,128]{2,1,0:T(8,128)} %all-to-all-done.1.refs_1_, bf16[864,1152]{1,0:T(8,128)(2,1)S(1)} %get-tuple-element.24.refs_2_), custom_call_target="tpu_custom_call" | custom-call | bytes 3104772 | tf_op jit(solution)/shard_map/pallas_call | solution.py:103
  53.6 6.9 %all-to-all-done.refs_1_ = f32[16,136,128]{2,1,0:T(8,128)S(1)} async-done(((f32[16,136,128]{2,1,0:T(8,128)}), f32[16,136,128]{2,1,0:T(8,128)S(1)}, u32[]{:S(2)}, u32[]{:S(2)}) %all-to-all-start) | async-done | bytes 1114144 | tf_op jit(solution)/shard_map/all_to_all | solution.py:544
  60.5 2.5 %shard_map.101 = (f32[32,96,128]{2,1,0:T(8,128)}, f32[16,128]{1,0:T(8,128)S(1)}) custom-call(s32[1]{0:T(128)} %bitcast.refs_0_, f32[16,136,128]{2,1,0:T(8,128)S(1)} %all-to-all-done.refs_1_, bf16[864,1152]{1,0:T(8,128)(2,1)S(1)} %get-tuple-element.24.refs_2_, f32[32,96,128]{2,1,0:T(8,128)} %get-tuple-element.25.refs_3_), custom_call_target="tpu_custom_call", output_to_operand_aliasing={{0}: (3, {})} | custom-call | bytes 4677636 | tf_op jit(solution)/shard_map/pallas_call | solution.py:103
  63.0 3.5 %all-to-all-start.2 = ((f32[32,96,128]{2,1,0:T(8,128)}), f32[32,96,128]{2,1,0:T(8,128)S(1)}, u32[]{:S(2)}, u32[]{:S(2)}) async-start(f32[32,96,128]{2,1,0:T(8,128)} %get-tuple-element.26.refs_3_), calls=%async_computation.2 | async-start | bytes 3145728 | tf_op jit(solution)/shard_map/all_to_all | solution.py:624
  66.6 4.6 %shard_map.102 = (f32[3,864,128]{2,1,0:T(8,128)S(1)}, f32[3,8,128]{2,1,0:T(8,128)S(1)}, f32[3,8,128]{2,1,0:T(8,128)S(1)}) custom-call(s32[1]{0:T(128)} %bitcast.refs_0_, f32[16,128]{1,0:T(8,128)S(1)} %get-tuple-element.27.refs_1_, f32[16,128]{1,0:T(8,128)S(1)} %get-tuple-element.28.refs_2_, f32[32,96,128]{2,1,0:T(8,128)} %get-tuple-element.26.refs_3_, ...), custom_call_target="tpu_custom_call" | custom-call | bytes 2916356 | tf_op jit(solution)/shard_map/pallas_call | solution.py:103
  71.2 3.5 %collective-permute-start.5 = (f32[3,8,128]{2,1,0:T(8,128)S(1)}, f32[3,8,128]{2,1,0:T(8,128)S(1)}, u32[]{:S(2)}, u32[]{:S(2)}) collective-permute-start(f32[3,8,128]{2,1,0:T(8,128)S(1)} %get-tuple-element.29), channel_id=1, source_target_pairs={{0,4},{4,8},{8,12},{12,16},{16,20},{20,24},{24,28},{1,5},{5,9},{9,... | collective-permute-start | bytes 36872 | tf_op jit(solution)/shard_map/ppermute | solution.py:510
  76.7 3.6 %collective-permute-done.6.refs_2_ = f32[3,8,128]{2,1,0:T(8,128)S(1)} collective-permute-done((f32[3,8,128]{2,1,0:T(8,128)S(1)}, f32[3,8,128]{2,1,0:T(8,128)S(1)}, u32[]{:S(2)}, u32[]{:S(2)}) %collective-permute-start.6) | collective-permute-done | bytes 12320 | tf_op jit(solution)/shard_map/ppermute | solution.py:510
  81.1 2.9 %collective-permute-start.7 = (f32[9,1,896]{2,1,0:T(1,128)S(1)}, f32[9,1,896]{2,1,0:T(1,128)S(1)}, u32[]{:S(2)}, u32[]{:S(2)}) collective-permute-start(f32[9,1,896]{2,1,0:T(1,128)S(1)} %get-tuple-element.33), channel_id=1, source_target_pairs={{0,1},{1,2},{2,3},{4,5},{5,6},{6,7},{8,9},{9,10},{10,11},{12,13},{... | collective-permute-start | bytes 96776 | tf_op jit(solution)/shard_map/ppermute | solution.py:510
  85.3 4.3 %shard_map.104 = (f32[3,864,128]{2,1,0:T(8,128)}, f32[56,896]{1,0:T(8,128)S(1)}) custom-call(f32[3,864,128]{2,1,0:T(8,128)S(1)} %get-tuple-element.30.refs_1_.refs_0_, f32[3,8,128]{2,1,0:T(8,128)S(1)} %collective-permute-done.5.refs_0_.refs_1_, f32[3,8,128]{2,1,0:T(8,128)S(1)} %collective-permute-done.6.refs_2_, ...), custom_call_target="tpu_custom_call" | custom-call | bytes 2993152 | tf_op jit(solution)/shard_map/pallas_call | solution.py:103
  89.7 3.1 %collective-permute-done.7.refs_2_ = f32[9,1,896]{2,1,0:T(1,128)S(1)} collective-permute-done((f32[9,1,896]{2,1,0:T(1,128)S(1)}, f32[9,1,896]{2,1,0:T(1,128)S(1)}, u32[]{:S(2)}, u32[]{:S(2)}) %collective-permute-start.7) | collective-permute-done | bytes 32288 | tf_op jit(solution)/shard_map/ppermute | solution.py:510
  92.8 11.2 %all-to-all-done.2.refs_0_ = f32[32,96,128]{2,1,0:T(8,128)S(1)} async-done(((f32[32,96,128]{2,1,0:T(8,128)}), f32[32,96,128]{2,1,0:T(8,128)S(1)}, u32[]{:S(2)}, u32[]{:S(2)}) %all-to-all-start.2) | async-done | bytes 1572896 | tf_op jit(solution)/shard_map/all_to_all | solution.py:624
  103.9 3.6 %shard_map.105 = (f32[3,256,128]{2,1,0:T(8,128)}, f32[3,864,128]{2,1,0:T(8,128)}) custom-call(f32[32,96,128]{2,1,0:T(8,128)S(1)} %all-to-all-done.2.refs_0_, f32[56,896]{1,0:T(8,128)S(1)} %get-tuple-element.32.refs_1_, f32[9,1,896]{2,1,0:T(1,128)S(1)} %collective-permute-done.7.refs_2_, f32[9,1,896]{2,1,0:T(1,128)S(1)} %collective-permute-done.8.refs_3_, ...), custom_call_target="tpu_custom_call" | custom-call | bytes 3890176 | tf_op jit(solution)/shard_map/pallas_call | solution.py:103
  (18 shorter events, 11.9 us)
Async XLA Ops:
  1.9 32.2 %collective-permute-start = (f32[1296,128]{1,0:T(8,128)S(1)}, f32[1296,128]{1,0:T(8,128)S(1)}, u32[]{:S(2)}, u32[]{:S(2)}) collective-permute-start(f32[1296,128]{1,0:T(8,128)S(1)} %shard_map.95.refs_1_), channel_id=1, source_target_pairs={{0,2},{1,3},{2,0},{3,1},{4,6},{5,7},{6,4},{7,5},{8,10},{9,11},{10,... | collective-permute-start | bytes 1990664 | tf_op jit(solution)/shard_map/ppermute | solution.py:555
  7.1 19.0 %copy-start = (f32[16,136,128]{2,1,0:T(8,128)S(1)}, f32[16,136,128]{2,1,0:T(8,128)}, u32[]{:S(2)}) copy-start(f32[16,136,128]{2,1,0:T(8,128)} %shard_map.96.refs_4_) | copy-start | bytes 3342340
  7.1 33.4 %all-to-all-start.1 = ((f32[16,136,128]{2,1,0:T(8,128)}), f32[16,136,128]{2,1,0:T(8,128)}, u32[]{:S(2)}, u32[]{:S(2)}) async-start(f32[16,136,128]{2,1,0:T(8,128)} %shard_map.96.refs_4_), calls=%async_computation.1 | async-start | bytes 2228224 | tf_op jit(solution)/shard_map/all_to_all | solution.py:544
  13.7 9.6 %collective-permute-start.1 = (f32[6,8,128]{2,1,0:T(8,128)S(1)}, f32[6,8,128]{2,1,0:T(8,128)S(1)}, u32[]{:S(2)}, u32[]{:S(2)}) collective-permute-start(f32[6,8,128]{2,1,0:T(8,128)S(1)} %pad_maximum_fusion), channel_id=1, source_target_pairs={{0,4},{4,8},{8,12},{12,16},{16,20},{20,24},{24,28},{1,5},{5,9},{9,... | collective-permute-start | bytes 73736 | tf_op jit(solution)/shard_map/ppermute | solution.py:510
  17.3 8.8 %collective-permute-start.2 = (f32[6,8,128]{2,1,0:T(8,128)S(1)}, f32[6,8,128]{2,1,0:T(8,128)S(1)}, u32[]{:S(2)}, u32[]{:S(2)}) collective-permute-start(f32[6,8,128]{2,1,0:T(8,128)S(1)} %pad_maximum_fusion.1), channel_id=1, source_target_pairs={{4,0},{8,4},{12,8},{16,12},{20,16},{24,20},{28,24},{5,1},{9,5},{13... | collective-permute-start | bytes 73736 | tf_op jit(solution)/shard_map/ppermute | solution.py:510
  29.2 16.1 %collective-permute-start.3 = (f32[9,1,896]{2,1,0:T(1,128)S(1)}, f32[9,1,896]{2,1,0:T(1,128)S(1)}, u32[]{:S(2)}, u32[]{:S(2)}) collective-permute-start(f32[9,1,896]{2,1,0:T(1,128)S(1)} %get-tuple-element.22), channel_id=1, source_target_pairs={{0,1},{1,2},{2,3},{4,5},{5,6},{6,7},{8,9},{9,10},{10,11},{12,13},{... | collective-permute-start | bytes 96776 | tf_op jit(solution)/shard_map/ppermute | solution.py:510
  30.5 14.8 %collective-permute-start.4 = (f32[9,1,896]{2,1,0:T(1,128)S(1)}, f32[9,1,896]{2,1,0:T(1,128)S(1)}, u32[]{:S(2)}, u32[]{:S(2)}) collective-permute-start(f32[9,1,896]{2,1,0:T(1,128)S(1)} %get-tuple-element.23), channel_id=1, source_target_pairs={{1,0},{2,1},{3,2},{5,4},{6,5},{7,6},{9,8},{10,9},{11,10},{13,12},{... | collective-permute-start | bytes 96776 | tf_op jit(solution)/shard_map/ppermute | solution.py:510
  40.5 20.0 %all-to-all-start = ((f32[16,136,128]{2,1,0:T(8,128)}), f32[16,136,128]{2,1,0:T(8,128)S(1)}, u32[]{:S(2)}, u32[]{:S(2)}) async-start(f32[16,136,128]{2,1,0:T(8,128)} %shard_map.98.refs_7_), calls=%async_computation | async-start | bytes 2228224 | tf_op jit(solution)/shard_map/all_to_all | solution.py:544
  45.4 1.3 %copy-start.1 = (f32[16,136,128]{2,1,0:T(8,128)S(1)}, f32[16,136,128]{2,1,0:T(8,128)}, u32[]{:S(2)}) copy-start(f32[16,136,128]{2,1,0:T(8,128)} %shard_map.98.refs_7_) | copy-start | bytes 3342340
  63.0 40.9 %all-to-all-start.2 = ((f32[32,96,128]{2,1,0:T(8,128)}), f32[32,96,128]{2,1,0:T(8,128)S(1)}, u32[]{:S(2)}, u32[]{:S(2)}) async-start(f32[32,96,128]{2,1,0:T(8,128)} %get-tuple-element.26.refs_3_), calls=%async_computation.2 | async-start | bytes 3145728 | tf_op jit(solution)/shard_map/all_to_all | solution.py:624
  71.2 5.5 %collective-permute-start.5 = (f32[3,8,128]{2,1,0:T(8,128)S(1)}, f32[3,8,128]{2,1,0:T(8,128)S(1)}, u32[]{:S(2)}, u32[]{:S(2)}) collective-permute-start(f32[3,8,128]{2,1,0:T(8,128)S(1)} %get-tuple-element.29), channel_id=1, source_target_pairs={{0,4},{4,8},{8,12},{12,16},{16,20},{20,24},{24,28},{1,5},{5,9},{9,... | collective-permute-start | bytes 36872 | tf_op jit(solution)/shard_map/ppermute | solution.py:510
  74.8 5.6 %collective-permute-start.6 = (f32[3,8,128]{2,1,0:T(8,128)S(1)}, f32[3,8,128]{2,1,0:T(8,128)S(1)}, u32[]{:S(2)}, u32[]{:S(2)}) collective-permute-start(f32[3,8,128]{2,1,0:T(8,128)S(1)} %get-tuple-element.31), channel_id=1, source_target_pairs={{4,0},{8,4},{12,8},{16,12},{20,16},{24,20},{28,24},{5,1},{9,5},{13... | collective-permute-start | bytes 36872 | tf_op jit(solution)/shard_map/ppermute | solution.py:510
  81.1 11.7 %collective-permute-start.7 = (f32[9,1,896]{2,1,0:T(1,128)S(1)}, f32[9,1,896]{2,1,0:T(1,128)S(1)}, u32[]{:S(2)}, u32[]{:S(2)}) collective-permute-start(f32[9,1,896]{2,1,0:T(1,128)S(1)} %get-tuple-element.33), channel_id=1, source_target_pairs={{0,1},{1,2},{2,3},{4,5},{5,6},{6,7},{8,9},{9,10},{10,11},{12,13},{... | collective-permute-start | bytes 96776 | tf_op jit(solution)/shard_map/ppermute | solution.py:510
  84.0 8.7 %collective-permute-start.8 = (f32[9,1,896]{2,1,0:T(1,128)S(1)}, f32[9,1,896]{2,1,0:T(1,128)S(1)}, u32[]{:S(2)}, u32[]{:S(2)}) collective-permute-start(f32[9,1,896]{2,1,0:T(1,128)S(1)} %get-tuple-element.34), channel_id=1, source_target_pairs={{1,0},{2,1},{3,2},{5,4},{6,5},{7,6},{9,8},{10,9},{11,10},{13,12},{... | collective-permute-start | bytes 96776 | tf_op jit(solution)/shard_map/ppermute | solution.py:510

commit v6 on v5

--- a/solution.py
+++ b/solution.py
@@ -431,7 +431,8 @@
     values = [
         held[:, chan * cap : (chan + 1) * cap, :].reshape(slots, width) for chan in range(chans)
     ]
-    for chan, air_sum in enumerate(exact_dots(select, values)):
+    for chan in range(chans):
+        (air_sum,) = exact_dots(select, [values[chan]])
         result = state[chan] + air_sum if chan == 0 else state[chan] - air_sum
         forced[chan] = result
         top[chan] = result[:EDGE]

time: 109 us -> 109 us (level)
  no operation moved by 1% of the time
where the time goes in v6:
time: 109 us; the launch traced here: 108 us
  waiting for transfers between devices  38.1 us (35%)
  starting transfers between devices  34.9 us (32%)
  Pallas kernels  31.7 us (29%)
  local copies, waits for them, and re-layouts  2.02 us (2%)
    pallas_call x11, Pallas kernels, call(): pl.pallas_call(body, out_shape=out_shape, in_specs=[pl.BlockSpec(memory_s...  31.7 us
    all_to_all x2, waiting for transfers between devices, exchange(): lax.all_to_all(x, BOTH, split_axis=0, concat_axis=0, tiled=True, axis_ind...  11.2 us
    all_to_all x1, waiting for transfers between devices, per_device(): lax.all_to_all(weighted, BOTH, split_axis=0, concat_axis=0, tiled=True)  11.2 us
    ppermute x4, starting transfers between devices, shift(): lax.ppermute(high_edge, axis, forward)  11.1 us
    all_to_all x2, starting transfers between devices, exchange(): lax.all_to_all(x, BOTH, split_axis=0, concat_axis=0, tiled=True, axis_ind...  10.7 us
    ppermute x4, waiting for transfers between devices, shift(): lax.ppermute(high_edge, axis, forward)  6.84 us
    ppermute x4, waiting for transfers between devices, shift(): lax.ppermute(low_edge, axis, backward)  6.54 us
    ppermute x4, starting transfers between devices, shift(): lax.ppermute(low_edge, axis, backward)  6.43 us
  transfers between devices with their start and end apart: 12, of which 8 were waited for; matrix products, arithmetic and copies ran while one was open for 1% of the time, Pallas kernels for 22%

profile of v6, /device:TPU:1, one launch (start us, length us, event | category | flops | bytes accessed | tf_op | source)
XLA Modules:
  0.0 107.8 jit_solution(5613910437045919763)
XLA Ops:
  1.9 3.2 %collective-permute-start = (f32[1296,128]{1,0:T(8,128)S(1)}, f32[1296,128]{1,0:T(8,128)S(1)}, u32[]{:S(2)}, u32[]{:S(2)}) collective-permute-start(f32[1296,128]{1,0:T(8,128)S(1)} %shard_map.95.refs_1_), channel_id=1, source_target_pairs={{0,2},{1,3},{2,0},{3,1},{4,6},{5,7},{6,4},{7,5},{8,10},{9,11},{10,... | collective-permute-start | bytes 1990664 | tf_op jit(solution)/shard_map/ppermute | solution.py:556
  5.1 1.9 %shard_map.96.refs_4_ = f32[16,136,128]{2,1,0:T(8,128)} custom-call(s32[1]{0:T(128)} %bitcast.refs_0_, f32[1296,128]{1,0:T(8,128)S(1)} %shard_map.95.refs_1_), custom_call_target="tpu_custom_call" | custom-call | flops 1024000 | bytes 1024 | tf_op jit(solution)/shard_map/pallas_call | solution.py:103
  7.1 5.8 %all-to-all-start.1 = ((f32[16,136,128]{2,1,0:T(8,128)}), f32[16,136,128]{2,1,0:T(8,128)}, u32[]{:S(2)}, u32[]{:S(2)}) async-start(f32[16,136,128]{2,1,0:T(8,128)} %shard_map.96.refs_4_), calls=%async_computation.1 | async-start | bytes 2228224 | tf_op jit(solution)/shard_map/all_to_all | solution.py:545
  13.7 3.5 %collective-permute-start.1 = (f32[6,8,128]{2,1,0:T(8,128)S(1)}, f32[6,8,128]{2,1,0:T(8,128)S(1)}, u32[]{:S(2)}, u32[]{:S(2)}) collective-permute-start(f32[6,8,128]{2,1,0:T(8,128)S(1)} %pad_maximum_fusion), channel_id=1, source_target_pairs={{0,4},{4,8},{8,12},{12,16},{16,20},{20,24},{24,28},{1,5},{5,9},{9,... | collective-permute-start | bytes 73736 | tf_op jit(solution)/shard_map/ppermute | solution.py:511
  19.2 4.1 %collective-permute-done.1.refs_0_.refs_6_ = f32[6,8,128]{2,1,0:T(8,128)S(1)} collective-permute-done((f32[6,8,128]{2,1,0:T(8,128)S(1)}, f32[6,8,128]{2,1,0:T(8,128)S(1)}, u32[]{:S(2)}, u32[]{:S(2)}) %collective-permute-start.1) | collective-permute-done | bytes 24608 | tf_op jit(solution)/shard_map/ppermute | solution.py:511
  23.3 2.8 %collective-permute-done.2.refs_1_.refs_7_ = f32[6,8,128]{2,1,0:T(8,128)S(1)} collective-permute-done((f32[6,8,128]{2,1,0:T(8,128)S(1)}, f32[6,8,128]{2,1,0:T(8,128)S(1)}, u32[]{:S(2)}, u32[]{:S(2)}) %collective-permute-start.2) | collective-permute-done | bytes 24608 | tf_op jit(solution)/shard_map/ppermute | solution.py:511
  26.1 3.1 %shard_map.97 = (f32[9,1,896]{2,1,0:T(1,128)S(1)}, f32[9,1,896]{2,1,0:T(1,128)S(1)}, f32[56,896]{1,0:T(8,128)S(1)}) custom-call(f32[6,8,128]{2,1,0:T(8,128)S(1)} %collective-permute-done.1.refs_0_.refs_6_, f32[6,8,128]{2,1,0:T(8,128)S(1)} %collective-permute-done.2.refs_1_.refs_7_, f32[3,864,128]{2,1,0:T(8,128)} %bitcast.10, f32[3,864,128]{2,1,0:T(8,128)} %bitcast.14, ...), custom_call_target="tpu_custom_call" | custom-call | flops 1024000 | bytes 1024 | tf_op jit(solution)/shard_map/pallas_call | solution.py:103
  31.8 2.3 %collective-permute-done.refs_1_ = f32[1296,128]{1,0:T(8,128)S(1)} collective-permute-done((f32[1296,128]{1,0:T(8,128)S(1)}, f32[1296,128]{1,0:T(8,128)S(1)}, u32[]{:S(2)}, u32[]{:S(2)}) %collective-permute-start) | collective-permute-done | bytes 663584 | tf_op jit(solution)/shard_map/ppermute | solution.py:556
  34.2 2.0 %shard_map.98.refs_7_ = f32[16,136,128]{2,1,0:T(8,128)} custom-call(s32[1]{0:T(128)} %bitcast.refs_0_, f32[1296,128]{1,0:T(8,128)S(1)} %collective-permute-done.refs_1_, f32[56,896]{1,0:T(8,128)S(1)} %get-tuple-element.21.refs_2_.refs_3_), custom_call_target="tpu_custom_call" | custom-call | flops 16777216000 | bytes 16777216 | tf_op jit(solution)/shard_map/pallas_call | solution.py:103
  36.2 4.4 %all-to-all-done.1.refs_1_ = f32[16,136,128]{2,1,0:T(8,128)} async-done(((f32[16,136,128]{2,1,0:T(8,128)}), f32[16,136,128]{2,1,0:T(8,128)}, u32[]{:S(2)}, u32[]{:S(2)}) %all-to-all-start.1) | async-done | bytes 1114144 | tf_op jit(solution)/shard_map/all_to_all | solution.py:545
  40.5 4.8 %all-to-all-start = ((f32[16,136,128]{2,1,0:T(8,128)}), f32[16,136,128]{2,1,0:T(8,128)S(1)}, u32[]{:S(2)}, u32[]{:S(2)}) async-start(f32[16,136,128]{2,1,0:T(8,128)} %shard_map.98.refs_7_), calls=%async_computation | async-start | bytes 2228224 | tf_op jit(solution)/shard_map/all_to_all | solution.py:545
  46.6 3.2 %shard_map.99 = (bf16[864,1152]{1,0:T(8,128)(2,1)S(1)}, bf16[256,1024]{1,0:T(8,128)(2,1)}) custom-call(f32[6,8,128]{2,1,0:T(8,128)S(1)} %collective-permute-done.1.refs_0_.refs_6_, f32[6,8,128]{2,1,0:T(8,128)S(1)} %collective-permute-done.2.refs_1_.refs_7_, f32[9,1,896]{2,1,0:T(1,128)S(1)} %collective-permute-done.3.refs_2_.refs_4_, ...), custom_call_target="tpu_custom_call" | custom-call | flops 104857600000 | bytes 104857600 | tf_op jit(solution)/shard_map/pallas_call | solution.py:103
  49.8 3.8 %shard_map.100 = (f32[32,96,128]{2,1,0:T(8,128)}, f32[16,128]{1,0:T(8,128)S(1)}) custom-call(s32[1]{0:T(128)} %bitcast.refs_0_, f32[16,136,128]{2,1,0:T(8,128)} %all-to-all-done.1.refs_1_, bf16[864,1152]{1,0:T(8,128)(2,1)S(1)} %get-tuple-element.24.refs_2_), custom_call_target="tpu_custom_call" | custom-call | bytes 3104772 | tf_op jit(solution)/shard_map/pallas_call | solution.py:103
  53.6 6.9 %all-to-all-done.refs_1_ = f32[16,136,128]{2,1,0:T(8,128)S(1)} async-done(((f32[16,136,128]{2,1,0:T(8,128)}), f32[16,136,128]{2,1,0:T(8,128)S(1)}, u32[]{:S(2)}, u32[]{:S(2)}) %all-to-all-start) | async-done | bytes 1114144 | tf_op jit(solution)/shard_map/all_to_all | solution.py:545
  60.5 2.5 %shard_map.101 = (f32[32,96,128]{2,1,0:T(8,128)}, f32[16,128]{1,0:T(8,128)S(1)}) custom-call(s32[1]{0:T(128)} %bitcast.refs_0_, f32[16,136,128]{2,1,0:T(8,128)S(1)} %all-to-all-done.refs_1_, bf16[864,1152]{1,0:T(8,128)(2,1)S(1)} %get-tuple-element.24.refs_2_, f32[32,96,128]{2,1,0:T(8,128)} %get-tuple-element.25.refs_3_), custom_call_target="tpu_custom_call", output_to_operand_aliasing={{0}: (3, {})} | custom-call | bytes 4677636 | tf_op jit(solution)/shard_map/pallas_call | solution.py:103
  63.0 3.5 %all-to-all-start.2 = ((f32[32,96,128]{2,1,0:T(8,128)}), f32[32,96,128]{2,1,0:T(8,128)S(1)}, u32[]{:S(2)}, u32[]{:S(2)}) async-start(f32[32,96,128]{2,1,0:T(8,128)} %get-tuple-element.26.refs_3_), calls=%async_computation.2 | async-start | bytes 3145728 | tf_op jit(solution)/shard_map/all_to_all | solution.py:625
  66.6 5.0 %shard_map.102 = (f32[3,864,128]{2,1,0:T(8,128)S(1)}, f32[3,8,128]{2,1,0:T(8,128)S(1)}, f32[3,8,128]{2,1,0:T(8,128)S(1)}) custom-call(s32[1]{0:T(128)} %bitcast.refs_0_, f32[16,128]{1,0:T(8,128)S(1)} %get-tuple-element.27.refs_1_, f32[16,128]{1,0:T(8,128)S(1)} %get-tuple-element.28.refs_2_, f32[32,96,128]{2,1,0:T(8,128)} %get-tuple-element.26.refs_3_, ...), custom_call_target="tpu_custom_call" | custom-call | bytes 2916356 | tf_op jit(solution)/shard_map/pallas_call | solution.py:103
  71.6 3.5 %collective-permute-start.5 = (f32[3,8,128]{2,1,0:T(8,128)S(1)}, f32[3,8,128]{2,1,0:T(8,128)S(1)}, u32[]{:S(2)}, u32[]{:S(2)}) collective-permute-start(f32[3,8,128]{2,1,0:T(8,128)S(1)} %get-tuple-element.29), channel_id=1, source_target_pairs={{0,4},{4,8},{8,12},{12,16},{16,20},{20,24},{24,28},{1,5},{5,9},{9,... | collective-permute-start | bytes 36872 | tf_op jit(solution)/shard_map/ppermute | solution.py:511
  77.1 3.8 %collective-permute-done.6.refs_2_ = f32[3,8,128]{2,1,0:T(8,128)S(1)} collective-permute-done((f32[3,8,128]{2,1,0:T(8,128)S(1)}, f32[3,8,128]{2,1,0:T(8,128)S(1)}, u32[]{:S(2)}, u32[]{:S(2)}) %collective-permute-start.6) | collective-permute-done | bytes 12320 | tf_op jit(solution)/shard_map/ppermute | solution.py:511
  81.7 2.8 %collective-permute-start.7 = (f32[9,1,896]{2,1,0:T(1,128)S(1)}, f32[9,1,896]{2,1,0:T(1,128)S(1)}, u32[]{:S(2)}, u32[]{:S(2)}) collective-permute-start(f32[9,1,896]{2,1,0:T(1,128)S(1)} %get-tuple-element.33), channel_id=1, source_target_pairs={{0,1},{1,2},{2,3},{4,5},{5,6},{6,7},{8,9},{9,10},{10,11},{12,13},{... | collective-permute-start | bytes 96776 | tf_op jit(solution)/shard_map/ppermute | solution.py:511
  85.7 4.3 %shard_map.104 = (f32[3,864,128]{2,1,0:T(8,128)}, f32[56,896]{1,0:T(8,128)S(1)}) custom-call(f32[3,864,128]{2,1,0:T(8,128)S(1)} %get-tuple-element.30.refs_1_.refs_0_, f32[3,8,128]{2,1,0:T(8,128)S(1)} %collective-permute-done.5.refs_0_.refs_1_, f32[3,8,128]{2,1,0:T(8,128)S(1)} %collective-permute-done.6.refs_2_, ...), custom_call_target="tpu_custom_call" | custom-call | bytes 2993152 | tf_op jit(solution)/shard_map/pallas_call | solution.py:103
  90.1 2.7 %collective-permute-done.7.refs_2_ = f32[9,1,896]{2,1,0:T(1,128)S(1)} collective-permute-done((f32[9,1,896]{2,1,0:T(1,128)S(1)}, f32[9,1,896]{2,1,0:T(1,128)S(1)}, u32[]{:S(2)}, u32[]{:S(2)}) %collective-permute-start.7) | collective-permute-done | bytes 32288 | tf_op jit(solution)/shard_map/ppermute | solution.py:511
  92.8 11.2 %all-to-all-done.2.refs_0_ = f32[32,96,128]{2,1,0:T(8,128)S(1)} async-done(((f32[32,96,128]{2,1,0:T(8,128)}), f32[32,96,128]{2,1,0:T(8,128)S(1)}, u32[]{:S(2)}, u32[]{:S(2)}) %all-to-all-start.2) | async-done | bytes 1572896 | tf_op jit(solution)/shard_map/all_to_all | solution.py:625
  103.9 3.6 %shard_map.105 = (f32[3,256,128]{2,1,0:T(8,128)}, f32[3,864,128]{2,1,0:T(8,128)}) custom-call(f32[32,96,128]{2,1,0:T(8,128)S(1)} %all-to-all-done.2.refs_0_, f32[56,896]{1,0:T(8,128)S(1)} %get-tuple-element.32.refs_1_, f32[9,1,896]{2,1,0:T(1,128)S(1)} %collective-permute-done.7.refs_2_, f32[9,1,896]{2,1,0:T(1,128)S(1)} %collective-permute-done.8.refs_3_, ...), custom_call_target="tpu_custom_call" | custom-call | bytes 3890176 | tf_op jit(solution)/shard_map/pallas_call | solution.py:103
  (18 shorter events, 11.9 us)
Async XLA Ops:
  1.9 32.2 %collective-permute-start = (f32[1296,128]{1,0:T(8,128)S(1)}, f32[1296,128]{1,0:T(8,128)S(1)}, u32[]{:S(2)}, u32[]{:S(2)}) collective-permute-start(f32[1296,128]{1,0:T(8,128)S(1)} %shard_map.95.refs_1_), channel_id=1, source_target_pairs={{0,2},{1,3},{2,0},{3,1},{4,6},{5,7},{6,4},{7,5},{8,10},{9,11},{10,... | collective-permute-start | bytes 1990664 | tf_op jit(solution)/shard_map/ppermute | solution.py:556
  7.1 19.0 %copy-start = (f32[16,136,128]{2,1,0:T(8,128)S(1)}, f32[16,136,128]{2,1,0:T(8,128)}, u32[]{:S(2)}) copy-start(f32[16,136,128]{2,1,0:T(8,128)} %shard_map.96.refs_4_) | copy-start | bytes 3342340
  7.1 33.4 %all-to-all-start.1 = ((f32[16,136,128]{2,1,0:T(8,128)}), f32[16,136,128]{2,1,0:T(8,128)}, u32[]{:S(2)}, u32[]{:S(2)}) async-start(f32[16,136,128]{2,1,0:T(8,128)} %shard_map.96.refs_4_), calls=%async_computation.1 | async-start | bytes 2228224 | tf_op jit(solution)/shard_map/all_to_all | solution.py:545
  13.7 9.6 %collective-permute-start.1 = (f32[6,8,128]{2,1,0:T(8,128)S(1)}, f32[6,8,128]{2,1,0:T(8,128)S(1)}, u32[]{:S(2)}, u32[]{:S(2)}) collective-permute-start(f32[6,8,128]{2,1,0:T(8,128)S(1)} %pad_maximum_fusion), channel_id=1, source_target_pairs={{0,4},{4,8},{8,12},{12,16},{16,20},{20,24},{24,28},{1,5},{5,9},{9,... | collective-permute-start | bytes 73736 | tf_op jit(solution)/shard_map/ppermute | solution.py:511
  17.3 8.8 %collective-permute-start.2 = (f32[6,8,128]{2,1,0:T(8,128)S(1)}, f32[6,8,128]{2,1,0:T(8,128)S(1)}, u32[]{:S(2)}, u32[]{:S(2)}) collective-permute-start(f32[6,8,128]{2,1,0:T(8,128)S(1)} %pad_maximum_fusion.1), channel_id=1, source_target_pairs={{4,0},{8,4},{12,8},{16,12},{20,16},{24,20},{28,24},{5,1},{9,5},{13... | collective-permute-start | bytes 73736 | tf_op jit(solution)/shard_map/ppermute | solution.py:511
  29.2 16.1 %collective-permute-start.3 = (f32[9,1,896]{2,1,0:T(1,128)S(1)}, f32[9,1,896]{2,1,0:T(1,128)S(1)}, u32[]{:S(2)}, u32[]{:S(2)}) collective-permute-start(f32[9,1,896]{2,1,0:T(1,128)S(1)} %get-tuple-element.22), channel_id=1, source_target_pairs={{0,1},{1,2},{2,3},{4,5},{5,6},{6,7},{8,9},{9,10},{10,11},{12,13},{... | collective-permute-start | bytes 96776 | tf_op jit(solution)/shard_map/ppermute | solution.py:511
  30.5 14.8 %collective-permute-start.4 = (f32[9,1,896]{2,1,0:T(1,128)S(1)}, f32[9,1,896]{2,1,0:T(1,128)S(1)}, u32[]{:S(2)}, u32[]{:S(2)}) collective-permute-start(f32[9,1,896]{2,1,0:T(1,128)S(1)} %get-tuple-element.23), channel_id=1, source_target_pairs={{1,0},{2,1},{3,2},{5,4},{6,5},{7,6},{9,8},{10,9},{11,10},{13,12},{... | collective-permute-start | bytes 96776 | tf_op jit(solution)/shard_map/ppermute | solution.py:511
  40.5 20.0 %all-to-all-start = ((f32[16,136,128]{2,1,0:T(8,128)}), f32[16,136,128]{2,1,0:T(8,128)S(1)}, u32[]{:S(2)}, u32[]{:S(2)}) async-start(f32[16,136,128]{2,1,0:T(8,128)} %shard_map.98.refs_7_), calls=%async_computation | async-start | bytes 2228224 | tf_op jit(solution)/shard_map/all_to_all | solution.py:545
  45.4 1.3 %copy-start.1 = (f32[16,136,128]{2,1,0:T(8,128)S(1)}, f32[16,136,128]{2,1,0:T(8,128)}, u32[]{:S(2)}) copy-start(f32[16,136,128]{2,1,0:T(8,128)} %shard_map.98.refs_7_) | copy-start | bytes 3342340
  63.0 40.9 %all-to-all-start.2 = ((f32[32,96,128]{2,1,0:T(8,128)}), f32[32,96,128]{2,1,0:T(8,128)S(1)}, u32[]{:S(2)}, u32[]{:S(2)}) async-start(f32[32,96,128]{2,1,0:T(8,128)} %get-tuple-element.26.refs_3_), calls=%async_computation.2 | async-start | bytes 3145728 | tf_op jit(solution)/shard_map/all_to_all | solution.py:625
  71.6 5.5 %collective-permute-start.5 = (f32[3,8,128]{2,1,0:T(8,128)S(1)}, f32[3,8,128]{2,1,0:T(8,128)S(1)}, u32[]{:S(2)}, u32[]{:S(2)}) collective-permute-start(f32[3,8,128]{2,1,0:T(8,128)S(1)} %get-tuple-element.29), channel_id=1, source_target_pairs={{0,4},{4,8},{8,12},{12,16},{16,20},{20,24},{24,28},{1,5},{5,9},{9,... | collective-permute-start | bytes 36872 | tf_op jit(solution)/shard_map/ppermute | solution.py:511
  75.2 5.7 %collective-permute-start.6 = (f32[3,8,128]{2,1,0:T(8,128)S(1)}, f32[3,8,128]{2,1,0:T(8,128)S(1)}, u32[]{:S(2)}, u32[]{:S(2)}) collective-permute-start(f32[3,8,128]{2,1,0:T(8,128)S(1)} %get-tuple-element.31), channel_id=1, source_target_pairs={{4,0},{8,4},{12,8},{16,12},{20,16},{24,20},{28,24},{5,1},{9,5},{13... | collective-permute-start | bytes 36872 | tf_op jit(solution)/shard_map/ppermute | solution.py:511
  81.7 11.1 %collective-permute-start.7 = (f32[9,1,896]{2,1,0:T(1,128)S(1)}, f32[9,1,896]{2,1,0:T(1,128)S(1)}, u32[]{:S(2)}, u32[]{:S(2)}) collective-permute-start(f32[9,1,896]{2,1,0:T(1,128)S(1)} %get-tuple-element.33), channel_id=1, source_target_pairs={{0,1},{1,2},{2,3},{4,5},{5,6},{6,7},{8,9},{9,10},{10,11},{12,13},{... | collective-permute-start | bytes 96776 | tf_op jit(solution)/shard_map/ppermute | solution.py:511
  84.4 8.4 %collective-permute-start.8 = (f32[9,1,896]{2,1,0:T(1,128)S(1)}, f32[9,1,896]{2,1,0:T(1,128)S(1)}, u32[]{:S(2)}, u32[]{:S(2)}) collective-permute-start(f32[9,1,896]{2,1,0:T(1,128)S(1)} %get-tuple-element.34), channel_id=1, source_target_pairs={{1,0},{2,1},{3,2},{5,4},{6,5},{7,6},{9,8},{10,9},{11,10},{13,12},{... | collective-permute-start | bytes 96776 | tf_op jit(solution)/shard_map/ppermute | solution.py:511

commit v7 on v6

--- a/solution.py
+++ b/solution.py
@@ -148,8 +148,6 @@
     of_seg = dot(place, member, (1, 1)).astype(BF16)
     (reach,) = exact_dots(place, [weight])
     send(chans, cap, reach)
-    for chan, sent in enumerate(exact_dots(of_seg, ocean)):
-        send(chan, cap, sent)
     line = iota((owners * EDGE, count), 0)
     tall = line == group * EDGE + (position & (EDGE - 1))
     flat = line == group * EDGE
@@ -166,6 +164,8 @@
     ).astype(BF16)
     labels = dot(jnp.concatenate([one_hot(tall), one_hot(flat)], axis=1), lanes, (1, 1))
     send(chans + 1, EDGE, labels[:, :width] * 32.0 + labels[:, width:])
+    for chan, sent in enumerate(exact_dots(of_seg, ocean)):
+        send(chan, cap, sent)
     return stores
 
 

time: 109 us -> 109 us (level)
  transfers between devices with their start and end apart: 12 -> 12, of which waited for: 8 -> 8; matrix products, arithmetic and copies ran while one was open for 1% -> 1% of each run, Pallas kernels for 22% -> 23%
where the time goes in v7:
time: 109 us; the launch traced here: 108 us
  waiting for transfers between devices  37.9 us (35%)
  starting transfers between devices  34.9 us (32%)
  Pallas kernels  32.1 us (29%)
  local copies, waits for them, and re-layouts  2.02 us (2%)
    pallas_call x11, Pallas kernels, call(): pl.pallas_call(body, out_shape=out_shape, in_specs=[pl.BlockSpec(memory_s...  32.1 us
    all_to_all x2, waiting for transfers between devices, exchange(): lax.all_to_all(x, BOTH, split_axis=0, concat_axis=0, tiled=True, axis_ind...  11.2 us
    all_to_all x1, waiting for transfers between devices, per_device(): lax.all_to_all(weighted, BOTH, split_axis=0, concat_axis=0, tiled=True)  11.2 us
    ppermute x4, starting transfers between devices, shift(): lax.ppermute(high_edge, axis, forward)  11.1 us
    all_to_all x2, starting transfers between devices, exchange(): lax.all_to_all(x, BOTH, split_axis=0, concat_axis=0, tiled=True, axis_ind...  10.7 us
    ppermute x4, waiting for transfers between devices, shift(): lax.ppermute(high_edge, axis, forward)  6.69 us
    ppermute x4, waiting for transfers between devices, shift(): lax.ppermute(low_edge, axis, backward)  6.55 us
    ppermute x4, starting transfers between devices, shift(): lax.ppermute(low_edge, axis, backward)  6.43 us
  transfers between devices with their start and end apart: 12, of which 8 were waited for; matrix products, arithmetic and copies ran while one was open for 1% of the time, Pallas kernels for 23%

profile of v7, /device:TPU:1, one launch (start us, length us, event | category | flops | bytes accessed | tf_op | source)
XLA Modules:
  0.0 107.9 jit_solution(1506939011298622509)
XLA Ops:
  1.9 3.2 %collective-permute-start = (f32[1296,128]{1,0:T(8,128)S(1)}, f32[1296,128]{1,0:T(8,128)S(1)}, u32[]{:S(2)}, u32[]{:S(2)}) collective-permute-start(f32[1296,128]{1,0:T(8,128)S(1)} %shard_map.95.refs_1_), channel_id=1, source_target_pairs={{0,2},{1,3},{2,0},{3,1},{4,6},{5,7},{6,4},{7,5},{8,10},{9,11},{10,... | collective-permute-start | bytes 1990664 | tf_op jit(solution)/shard_map/ppermute | solution.py:556
  5.1 2.1 %shard_map.96.refs_4_ = f32[16,136,128]{2,1,0:T(8,128)} custom-call(s32[1]{0:T(128)} %bitcast.refs_0_, f32[1296,128]{1,0:T(8,128)S(1)} %shard_map.95.refs_1_), custom_call_target="tpu_custom_call" | custom-call | flops 1024000 | bytes 1024 | tf_op jit(solution)/shard_map/pallas_call | solution.py:103
  7.3 5.8 %all-to-all-start.1 = ((f32[16,136,128]{2,1,0:T(8,128)}), f32[16,136,128]{2,1,0:T(8,128)}, u32[]{:S(2)}, u32[]{:S(2)}) async-start(f32[16,136,128]{2,1,0:T(8,128)} %shard_map.96.refs_4_), calls=%async_computation.1 | async-start | bytes 2228224 | tf_op jit(solution)/shard_map/all_to_all | solution.py:545
  13.9 3.5 %collective-permute-start.1 = (f32[6,8,128]{2,1,0:T(8,128)S(1)}, f32[6,8,128]{2,1,0:T(8,128)S(1)}, u32[]{:S(2)}, u32[]{:S(2)}) collective-permute-start(f32[6,8,128]{2,1,0:T(8,128)S(1)} %pad_maximum_fusion), channel_id=1, source_target_pairs={{0,4},{4,8},{8,12},{12,16},{16,20},{20,24},{24,28},{1,5},{5,9},{9,... | collective-permute-start | bytes 73736 | tf_op jit(solution)/shard_map/ppermute | solution.py:511
  19.4 4.0 %collective-permute-done.1.refs_0_.refs_6_ = f32[6,8,128]{2,1,0:T(8,128)S(1)} collective-permute-done((f32[6,8,128]{2,1,0:T(8,128)S(1)}, f32[6,8,128]{2,1,0:T(8,128)S(1)}, u32[]{:S(2)}, u32[]{:S(2)}) %collective-permute-start.1) | collective-permute-done | bytes 24608 | tf_op jit(solution)/shard_map/ppermute | solution.py:511
  23.3 2.8 %collective-permute-done.2.refs_1_.refs_7_ = f32[6,8,128]{2,1,0:T(8,128)S(1)} collective-permute-done((f32[6,8,128]{2,1,0:T(8,128)S(1)}, f32[6,8,128]{2,1,0:T(8,128)S(1)}, u32[]{:S(2)}, u32[]{:S(2)}) %collective-permute-start.2) | collective-permute-done | bytes 24608 | tf_op jit(solution)/shard_map/ppermute | solution.py:511
  26.1 3.1 %shard_map.97 = (f32[9,1,896]{2,1,0:T(1,128)S(1)}, f32[9,1,896]{2,1,0:T(1,128)S(1)}, f32[56,896]{1,0:T(8,128)S(1)}) custom-call(f32[6,8,128]{2,1,0:T(8,128)S(1)} %collective-permute-done.1.refs_0_.refs_6_, f32[6,8,128]{2,1,0:T(8,128)S(1)} %collective-permute-done.2.refs_1_.refs_7_, f32[3,864,128]{2,1,0:T(8,128)} %bitcast.10, f32[3,864,128]{2,1,0:T(8,128)} %bitcast.14, ...), custom_call_target="tpu_custom_call" | custom-call | flops 1024000 | bytes 1024 | tf_op jit(solution)/shard_map/pallas_call | solution.py:103
  31.9 2.3 %collective-permute-done.refs_1_ = f32[1296,128]{1,0:T(8,128)S(1)} collective-permute-done((f32[1296,128]{1,0:T(8,128)S(1)}, f32[1296,128]{1,0:T(8,128)S(1)}, u32[]{:S(2)}, u32[]{:S(2)}) %collective-permute-start) | collective-permute-done | bytes 663584 | tf_op jit(solution)/shard_map/ppermute | solution.py:556
  34.1 2.2 %shard_map.98.refs_7_ = f32[16,136,128]{2,1,0:T(8,128)} custom-call(s32[1]{0:T(128)} %bitcast.refs_0_, f32[1296,128]{1,0:T(8,128)S(1)} %collective-permute-done.refs_1_, f32[56,896]{1,0:T(8,128)S(1)} %get-tuple-element.21.refs_2_.refs_3_), custom_call_target="tpu_custom_call" | custom-call | flops 16777216000 | bytes 16777216 | tf_op jit(solution)/shard_map/pallas_call | solution.py:103
  36.4 4.4 %all-to-all-done.1.refs_1_ = f32[16,136,128]{2,1,0:T(8,128)} async-done(((f32[16,136,128]{2,1,0:T(8,128)}), f32[16,136,128]{2,1,0:T(8,128)}, u32[]{:S(2)}, u32[]{:S(2)}) %all-to-all-start.1) | async-done | bytes 1114144 | tf_op jit(solution)/shard_map/all_to_all | solution.py:545
  40.7 4.8 %all-to-all-start = ((f32[16,136,128]{2,1,0:T(8,128)}), f32[16,136,128]{2,1,0:T(8,128)S(1)}, u32[]{:S(2)}, u32[]{:S(2)}) async-start(f32[16,136,128]{2,1,0:T(8,128)} %shard_map.98.refs_7_), calls=%async_computation | async-start | bytes 2228224 | tf_op jit(solution)/shard_map/all_to_all | solution.py:545
  46.8 3.2 %shard_map.99 = (bf16[864,1152]{1,0:T(8,128)(2,1)S(1)}, bf16[256,1024]{1,0:T(8,128)(2,1)}) custom-call(f32[6,8,128]{2,1,0:T(8,128)S(1)} %collective-permute-done.1.refs_0_.refs_6_, f32[6,8,128]{2,1,0:T(8,128)S(1)} %collective-permute-done.2.refs_1_.refs_7_, f32[9,1,896]{2,1,0:T(1,128)S(1)} %collective-permute-done.3.refs_2_.refs_4_, ...), custom_call_target="tpu_custom_call" | custom-call | flops 104857600000 | bytes 104857600 | tf_op jit(solution)/shard_map/pallas_call | solution.py:103
  50.0 3.8 %shard_map.100 = (f32[32,96,128]{2,1,0:T(8,128)}, f32[16,128]{1,0:T(8,128)S(1)}) custom-call(s32[1]{0:T(128)} %bitcast.refs_0_, f32[16,136,128]{2,1,0:T(8,128)} %all-to-all-done.1.refs_1_, bf16[864,1152]{1,0:T(8,128)(2,1)S(1)} %get-tuple-element.24.refs_2_), custom_call_target="tpu_custom_call" | custom-call | bytes 3104772 | tf_op jit(solution)/shard_map/pallas_call | solution.py:103
  53.8 6.9 %all-to-all-done.refs_1_ = f32[16,136,128]{2,1,0:T(8,128)S(1)} async-done(((f32[16,136,128]{2,1,0:T(8,128)}), f32[16,136,128]{2,1,0:T(8,128)S(1)}, u32[]{:S(2)}, u32[]{:S(2)}) %all-to-all-start) | async-done | bytes 1114144 | tf_op jit(solution)/shard_map/all_to_all | solution.py:545
  60.7 2.5 %shard_map.101 = (f32[32,96,128]{2,1,0:T(8,128)}, f32[16,128]{1,0:T(8,128)S(1)}) custom-call(s32[1]{0:T(128)} %bitcast.refs_0_, f32[16,136,128]{2,1,0:T(8,128)S(1)} %all-to-all-done.refs_1_, bf16[864,1152]{1,0:T(8,128)(2,1)S(1)} %get-tuple-element.24.refs_2_, f32[32,96,128]{2,1,0:T(8,128)} %get-tuple-element.25.refs_3_), custom_call_target="tpu_custom_call", output_to_operand_aliasing={{0}: (3, {})} | custom-call | bytes 4677636 | tf_op jit(solution)/shard_map/pallas_call | solution.py:103
  63.2 3.5 %all-to-all-start.2 = ((f32[32,96,128]{2,1,0:T(8,128)}), f32[32,96,128]{2,1,0:T(8,128)S(1)}, u32[]{:S(2)}, u32[]{:S(2)}) async-start(f32[32,96,128]{2,1,0:T(8,128)} %get-tuple-element.26.refs_3_), calls=%async_computation.2 | async-start | bytes 3145728 | tf_op jit(solution)/shard_map/all_to_all | solution.py:625
  66.7 5.0 %shard_map.102 = (f32[3,864,128]{2,1,0:T(8,128)S(1)}, f32[3,8,128]{2,1,0:T(8,128)S(1)}, f32[3,8,128]{2,1,0:T(8,128)S(1)}) custom-call(s32[1]{0:T(128)} %bitcast.refs_0_, f32[16,128]{1,0:T(8,128)S(1)} %get-tuple-element.27.refs_1_, f32[16,128]{1,0:T(8,128)S(1)} %get-tuple-element.28.refs_2_, f32[32,96,128]{2,1,0:T(8,128)} %get-tuple-element.26.refs_3_, ...), custom_call_target="tpu_custom_call" | custom-call | bytes 2916356 | tf_op jit(solution)/shard_map/pallas_call | solution.py:103
  71.7 3.5 %collective-permute-start.5 = (f32[3,8,128]{2,1,0:T(8,128)S(1)}, f32[3,8,128]{2,1,0:T(8,128)S(1)}, u32[]{:S(2)}, u32[]{:S(2)}) collective-permute-start(f32[3,8,128]{2,1,0:T(8,128)S(1)} %get-tuple-element.29), channel_id=1, source_target_pairs={{0,4},{4,8},{8,12},{12,16},{16,20},{20,24},{24,28},{1,5},{5,9},{9,... | collective-permute-start | bytes 36872 | tf_op jit(solution)/shard_map/ppermute | solution.py:511
  77.2 3.8 %collective-permute-done.6.refs_2_ = f32[3,8,128]{2,1,0:T(8,128)S(1)} collective-permute-done((f32[3,8,128]{2,1,0:T(8,128)S(1)}, f32[3,8,128]{2,1,0:T(8,128)S(1)}, u32[]{:S(2)}, u32[]{:S(2)}) %collective-permute-start.6) | collective-permute-done | bytes 12320 | tf_op jit(solution)/shard_map/ppermute | solution.py:511
  81.8 2.8 %collective-permute-start.7 = (f32[9,1,896]{2,1,0:T(1,128)S(1)}, f32[9,1,896]{2,1,0:T(1,128)S(1)}, u32[]{:S(2)}, u32[]{:S(2)}) collective-permute-start(f32[9,1,896]{2,1,0:T(1,128)S(1)} %get-tuple-element.33), channel_id=1, source_target_pairs={{0,1},{1,2},{2,3},{4,5},{5,6},{6,7},{8,9},{9,10},{10,11},{12,13},{... | collective-permute-start | bytes 96776 | tf_op jit(solution)/shard_map/ppermute | solution.py:511
  85.8 4.3 %shard_map.104 = (f32[3,864,128]{2,1,0:T(8,128)}, f32[56,896]{1,0:T(8,128)S(1)}) custom-call(f32[3,864,128]{2,1,0:T(8,128)S(1)} %get-tuple-element.30.refs_1_.refs_0_, f32[3,8,128]{2,1,0:T(8,128)S(1)} %collective-permute-done.5.refs_0_.refs_1_, f32[3,8,128]{2,1,0:T(8,128)S(1)} %collective-permute-done.6.refs_2_, ...), custom_call_target="tpu_custom_call" | custom-call | bytes 2993152 | tf_op jit(solution)/shard_map/pallas_call | solution.py:103
  90.2 2.7 %collective-permute-done.7.refs_2_ = f32[9,1,896]{2,1,0:T(1,128)S(1)} collective-permute-done((f32[9,1,896]{2,1,0:T(1,128)S(1)}, f32[9,1,896]{2,1,0:T(1,128)S(1)}, u32[]{:S(2)}, u32[]{:S(2)}) %collective-permute-start.7) | collective-permute-done | bytes 32288 | tf_op jit(solution)/shard_map/ppermute | solution.py:511
  92.9 11.2 %all-to-all-done.2.refs_0_ = f32[32,96,128]{2,1,0:T(8,128)S(1)} async-done(((f32[32,96,128]{2,1,0:T(8,128)}), f32[32,96,128]{2,1,0:T(8,128)S(1)}, u32[]{:S(2)}, u32[]{:S(2)}) %all-to-all-start.2) | async-done | bytes 1572896 | tf_op jit(solution)/shard_map/all_to_all | solution.py:625
  104.1 3.6 %shard_map.105 = (f32[3,256,128]{2,1,0:T(8,128)}, f32[3,864,128]{2,1,0:T(8,128)}) custom-call(f32[32,96,128]{2,1,0:T(8,128)S(1)} %all-to-all-done.2.refs_0_, f32[56,896]{1,0:T(8,128)S(1)} %get-tuple-element.32.refs_1_, f32[9,1,896]{2,1,0:T(1,128)S(1)} %collective-permute-done.7.refs_2_, f32[9,1,896]{2,1,0:T(1,128)S(1)} %collective-permute-done.8.refs_3_, ...), custom_call_target="tpu_custom_call" | custom-call | bytes 3890176 | tf_op jit(solution)/shard_map/pallas_call | solution.py:103
  (18 shorter events, 11.9 us)
Async XLA Ops:
  1.9 32.2 %collective-permute-start = (f32[1296,128]{1,0:T(8,128)S(1)}, f32[1296,128]{1,0:T(8,128)S(1)}, u32[]{:S(2)}, u32[]{:S(2)}) collective-permute-start(f32[1296,128]{1,0:T(8,128)S(1)} %shard_map.95.refs_1_), channel_id=1, source_target_pairs={{0,2},{1,3},{2,0},{3,1},{4,6},{5,7},{6,4},{7,5},{8,10},{9,11},{10,... | collective-permute-start | bytes 1990664 | tf_op jit(solution)/shard_map/ppermute | solution.py:556
  7.3 18.8 %copy-start = (f32[16,136,128]{2,1,0:T(8,128)S(1)}, f32[16,136,128]{2,1,0:T(8,128)}, u32[]{:S(2)}) copy-start(f32[16,136,128]{2,1,0:T(8,128)} %shard_map.96.refs_4_) | copy-start | bytes 3342340
  7.3 33.4 %all-to-all-start.1 = ((f32[16,136,128]{2,1,0:T(8,128)}), f32[16,136,128]{2,1,0:T(8,128)}, u32[]{:S(2)}, u32[]{:S(2)}) async-start(f32[16,136,128]{2,1,0:T(8,128)} %shard_map.96.refs_4_), calls=%async_computation.1 | async-start | bytes 2228224 | tf_op jit(solution)/shard_map/all_to_all | solution.py:545
  13.9 9.4 %collective-permute-start.1 = (f32[6,8,128]{2,1,0:T(8,128)S(1)}, f32[6,8,128]{2,1,0:T(8,128)S(1)}, u32[]{:S(2)}, u32[]{:S(2)}) collective-permute-start(f32[6,8,128]{2,1,0:T(8,128)S(1)} %pad_maximum_fusion), channel_id=1, source_target_pairs={{0,4},{4,8},{8,12},{12,16},{16,20},{20,24},{24,28},{1,5},{5,9},{9,... | collective-permute-start | bytes 73736 | tf_op jit(solution)/shard_map/ppermute | solution.py:511
  17.5 8.7 %collective-permute-start.2 = (f32[6,8,128]{2,1,0:T(8,128)S(1)}, f32[6,8,128]{2,1,0:T(8,128)S(1)}, u32[]{:S(2)}, u32[]{:S(2)}) collective-permute-start(f32[6,8,128]{2,1,0:T(8,128)S(1)} %pad_maximum_fusion.1), channel_id=1, source_target_pairs={{4,0},{8,4},{12,8},{16,12},{20,16},{24,20},{28,24},{5,1},{9,5},{13... | collective-permute-start | bytes 73736 | tf_op jit(solution)/shard_map/ppermute | solution.py:511
  29.3 16.3 %collective-permute-start.3 = (f32[9,1,896]{2,1,0:T(1,128)S(1)}, f32[9,1,896]{2,1,0:T(1,128)S(1)}, u32[]{:S(2)}, u32[]{:S(2)}) collective-permute-start(f32[9,1,896]{2,1,0:T(1,128)S(1)} %get-tuple-element.22), channel_id=1, source_target_pairs={{0,1},{1,2},{2,3},{4,5},{5,6},{6,7},{8,9},{9,10},{10,11},{12,13},{... | collective-permute-start | bytes 96776 | tf_op jit(solution)/shard_map/ppermute | solution.py:511
  30.6 15.0 %collective-permute-start.4 = (f32[9,1,896]{2,1,0:T(1,128)S(1)}, f32[9,1,896]{2,1,0:T(1,128)S(1)}, u32[]{:S(2)}, u32[]{:S(2)}) collective-permute-start(f32[9,1,896]{2,1,0:T(1,128)S(1)} %get-tuple-element.23), channel_id=1, source_target_pairs={{1,0},{2,1},{3,2},{5,4},{6,5},{7,6},{9,8},{10,9},{11,10},{13,12},{... | collective-permute-start | bytes 96776 | tf_op jit(solution)/shard_map/ppermute | solution.py:511
  40.7 20.0 %all-to-all-start = ((f32[16,136,128]{2,1,0:T(8,128)}), f32[16,136,128]{2,1,0:T(8,128)S(1)}, u32[]{:S(2)}, u32[]{:S(2)}) async-start(f32[16,136,128]{2,1,0:T(8,128)} %shard_map.98.refs_7_), calls=%async_computation | async-start | bytes 2228224 | tf_op jit(solution)/shard_map/all_to_all | solution.py:545
  45.5 1.3 %copy-start.1 = (f32[16,136,128]{2,1,0:T(8,128)S(1)}, f32[16,136,128]{2,1,0:T(8,128)}, u32[]{:S(2)}) copy-start(f32[16,136,128]{2,1,0:T(8,128)} %shard_map.98.refs_7_) | copy-start | bytes 3342340
  63.2 40.8 %all-to-all-start.2 = ((f32[32,96,128]{2,1,0:T(8,128)}), f32[32,96,128]{2,1,0:T(8,128)S(1)}, u32[]{:S(2)}, u32[]{:S(2)}) async-start(f32[32,96,128]{2,1,0:T(8,128)} %get-tuple-element.26.refs_3_), calls=%async_computation.2 | async-start | bytes 3145728 | tf_op jit(solution)/shard_map/all_to_all | solution.py:625
  71.7 5.5 %collective-permute-start.5 = (f32[3,8,128]{2,1,0:T(8,128)S(1)}, f32[3,8,128]{2,1,0:T(8,128)S(1)}, u32[]{:S(2)}, u32[]{:S(2)}) collective-permute-start(f32[3,8,128]{2,1,0:T(8,128)S(1)} %get-tuple-element.29), channel_id=1, source_target_pairs={{0,4},{4,8},{8,12},{12,16},{16,20},{20,24},{24,28},{1,5},{5,9},{9,... | collective-permute-start | bytes 36872 | tf_op jit(solution)/shard_map/ppermute | solution.py:511
  75.3 5.7 %collective-permute-start.6 = (f32[3,8,128]{2,1,0:T(8,128)S(1)}, f32[3,8,128]{2,1,0:T(8,128)S(1)}, u32[]{:S(2)}, u32[]{:S(2)}) collective-permute-start(f32[3,8,128]{2,1,0:T(8,128)S(1)} %get-tuple-element.31), channel_id=1, source_target_pairs={{4,0},{8,4},{12,8},{16,12},{20,16},{24,20},{28,24},{5,1},{9,5},{13... | collective-permute-start | bytes 36872 | tf_op jit(solution)/shard_map/ppermute | solution.py:511
  81.8 11.1 %collective-permute-start.7 = (f32[9,1,896]{2,1,0:T(1,128)S(1)}, f32[9,1,896]{2,1,0:T(1,128)S(1)}, u32[]{:S(2)}, u32[]{:S(2)}) collective-permute-start(f32[9,1,896]{2,1,0:T(1,128)S(1)} %get-tuple-element.33), channel_id=1, source_target_pairs={{0,1},{1,2},{2,3},{4,5},{5,6},{6,7},{8,9},{9,10},{10,11},{12,13},{... | collective-permute-start | bytes 96776 | tf_op jit(solution)/shard_map/ppermute | solution.py:511
  84.5 8.4 %collective-permute-start.8 = (f32[9,1,896]{2,1,0:T(1,128)S(1)}, f32[9,1,896]{2,1,0:T(1,128)S(1)}, u32[]{:S(2)}, u32[]{:S(2)}) collective-permute-start(f32[9,1,896]{2,1,0:T(1,128)S(1)} %get-tuple-element.34), channel_id=1, source_target_pairs={{1,0},{2,1},{3,2},{5,4},{6,5},{7,6},{9,8},{10,9},{11,10},{13,12},{... | collective-permute-start | bytes 96776 | tf_op jit(solution)/shard_map/ppermute | solution.py:511
